TPU v7x, 32 devices: a whole 2x2x4 slice. The times are simulated.
32 devices in a mesh: tp: 2 (over x), dp: 16 (over z, y, core).
Axes of the slice: x: 2, y: 2, z: 4, core: 2. Of those that a mesh axis runs over, the one named last changes fastest.
Arguments:
- tokens: bfloat16 [8192, 768], P('dp'), may hold values from -6 to 6
- latents: bfloat16 [256, 768], P('dp'), may hold values from -6 to 6
- latent_query: bfloat16 [768, 768], P(None, 'tp'), may hold values from -0.21875 to 0.21875
- latent_key: bfloat16 [768, 768], P(None, 'tp'), may hold values from -0.21875 to 0.21875
- latent_value: bfloat16 [768, 768], P(None, 'tp'), may hold values from -0.21875 to 0.21875
- latent_output: bfloat16 [768, 768], P('tp'), may hold values from -1.75 to 1.75
- query_weight: bfloat16 [768, 768], P(None, 'tp'), may hold values from -0.21875 to 0.21875
- key_weight: bfloat16 [768, 768], P(None, 'tp'), may hold values from -0.21875 to 0.21875
- value_weight: bfloat16 [768, 768], P(None, 'tp'), may hold values from -0.21875 to 0.21875
- output_weight: bfloat16 [768, 768], P('tp'), may hold values from -1.75 to 1.75
- up_weight: bfloat16 [768, 3072], P(None, 'tp'), may hold values from -0.21875 to 0.21875
- up_bias: float32 [3072], P('tp'), may hold values from -3 to 3
- down_weight: bfloat16 [3072, 768], P('tp'), may hold values from -0.109375 to 0.109375
- down_bias: float32 [768], replicated, may hold values from -3 to 3
- latent_gain: float32 [768], replicated, may hold values from 0.1 to 1.9
- attention_gain: float32 [768], replicated, may hold values from 0.1 to 1.9
- feed_gain: float32 [768], replicated, may hold values from 0.1 to 1.9
- group_image: int32 [32], replicated, may hold values from 0 to 10, as said below
- token_cotangent: bfloat16 [8192, 768], P('dp'), may hold values from -6 to 6
- latent_cotangent: bfloat16 [256, 768], P('dp'), may hold values from -6 to 6
Outputs:
- mixed_tokens: bfloat16 [8192, 768], P('dp')
- mixed_latents: bfloat16 [256, 768], P('dp')
- token_grad: float32 [8192, 768], P('dp')
- latent_grad: float32 [256, 768], P('dp')
- latent_query_grad: float32 [768, 768], P('dp', 'tp')
- latent_key_grad: float32 [768, 768], P('dp', 'tp')
- latent_value_grad: float32 [768, 768], P('dp', 'tp')
- latent_output_grad: float32 [768, 768], P('tp', 'dp')
- query_weight_grad: float32 [768, 768], P('dp', 'tp')
- key_weight_grad: float32 [768, 768], P('dp', 'tp')
- value_weight_grad: float32 [768, 768], P('dp', 'tp')
- output_weight_grad: float32 [768, 768], P('tp', 'dp')
- up_weight_grad: float32 [768, 3072], P('dp', 'tp')
- up_bias_grad: float32 [3072], P(('tp', 'dp'))
- down_weight_grad: float32 [3072, 768], P('tp', 'dp')
- down_bias_grad: float32 [768], P('dp')
- latent_gain_grad: float32 [768], P('dp')
- attention_gain_grad: float32 [768], P('dp')
- feed_gain_grad: float32 [768], P('dp')
Inputs may be any that keep to these rules, and one draw needn't show every extreme that they name: group_image[g] names the image of group g; each image has at least 1 group.
All inputs are finite; a program needn't handle non-finite values.
Results may differ from a plain program's by a relative error of at most 0.02.
Values may be sent and summed in bfloat16 or wider, within the bound.
No kernel may reach another device: no remote copies, remote signals or barrier semaphores. Data moves between devices by JAX's collectives and lax.ppermute only.
A program may use at most 128 MiB of HBM per device.

v0:
```python
from functools import partial

import jax
import jax.numpy as jnp
from jax import lax
from jax.experimental import pallas as pl
from jax.experimental.pallas import tpu as pltpu
from jax.sharding import PartitionSpec as P

E = 64
S = 256
L = 8
EPSILON = 1e-05
NEGATIVE = -1000000000.0
FACTOR = E ** (-0.5)
LOG2E = 1.4426950408889634
F32 = jnp.float32
B16 = jnp.bfloat16


def nn(left, right):
    return lax.dot_general(left, right, (((1,), (0,)), ((), ())), preferred_element_type=F32)


def nt(left, right):
    return lax.dot_general(left, right, (((1,), (1,)), ((), ())), preferred_element_type=F32)


def tn(left, right):
    return lax.dot_general(left, right, (((0,), (0,)), ((), ())), preferred_element_type=F32)


def norm_parts(values):
    average = jnp.mean(values, axis=-1, keepdims=True)
    centred = values - average
    spread = jnp.mean(centred * centred, axis=-1, keepdims=True)
    rate = lax.rsqrt(spread + EPSILON)
    return centred * rate, rate


def norm_back(grad, unit, rate, gain):
    scaled = grad * gain
    first = jnp.mean(scaled, axis=-1, keepdims=True)
    second = jnp.mean(scaled * unit, axis=-1, keepdims=True)
    return rate * (scaled - first - unit * second)


def gelu_both(values):
    square = values * values
    wave = jnp.tanh(0.7978845608028654 * values * (1.0 + 0.044715 * square))
    slope = 0.7978845608028654 * (1.0 + 0.134145 * square)
    half = 0.5 * (1.0 + wave)
    return values * half, half + 0.5 * values * (1.0 - wave * wave) * slope


def head_mask(heads, rows, width):
    row = lax.broadcasted_iota(jnp.int32, (heads * rows, width), 0)
    column = lax.broadcasted_iota(jnp.int32, (heads * rows, width), 1)
    return (row // rows) == (column // E)


def spread_heads(values, heads):
    rows, width = values.shape
    stacked = jnp.concatenate([values] * heads, axis=0)
    return jnp.where(head_mask(heads, rows, width), stacked, jnp.zeros_like(stacked))


def fold_heads(values, heads):
    rows, width = values.shape[0] // heads, values.shape[1]
    kept = jnp.where(head_mask(heads, rows, width), values, jnp.zeros_like(values))
    total = kept[:rows]
    for h in range(1, heads):
        total = total + kept[h * rows : (h + 1) * rows]
    return total


def half_mask(width):
    return lax.broadcasted_iota(jnp.int32, (1, width), 1) < E


def head_only(values, second):
    mask = half_mask(values.shape[1])
    zero = jnp.zeros_like(values)
    return jnp.where(mask, zero, values) if second else jnp.where(mask, values, zero)


def enter_kernel(tokens, gain, wq, wk, wv, q_out, k_out, v_out, saved_out):
    unit, _ = norm_parts(tokens[...].astype(F32))
    low = (unit * gain[...]).astype(B16)
    q = nn(low, wq[...]).astype(B16)
    k = nn(low, wk[...]).astype(B16)
    v = nn(low, wv[...]).astype(B16)
    q_out[...] = q
    k_out[...] = k
    v_out[...] = v
    width = q.shape[1]
    saved_out[:, :width] = q
    saved_out[:, width : 2 * width] = k
    saved_out[:, 2 * width : 3 * width] = v
    saved_out[:, 3 * width :] = low


def latent_kernel(
    heads, own, one, two, gain, own_images, images, wq, wk, wv, wo, latents_out, q_out, k_out, v_out, part_out
):
    latents = jnp.concatenate([one[...], two[...]], axis=0)
    latents_out[...] = latents
    unit, _ = norm_parts(latents.astype(F32))
    low = (unit * gain[...]).astype(B16)
    q = nn(low, wq[...]).astype(B16)
    k = nn(low, wk[...]).astype(B16)
    v = nn(low, wv[...]).astype(B16)
    q_out[...] = q
    k_out[...] = k
    v_out[...] = v
    scores = nt(spread_heads(q[:own], heads), k) * FACTOR
    member = jnp.concatenate([own_images[...]] * heads, axis=0) == images[...]
    scores = jnp.where(member, scores, NEGATIVE)
    weights = jnp.exp(scores - jnp.max(scores, axis=-1, keepdims=True))
    probs = weights / jnp.sum(weights, axis=-1, keepdims=True)
    mixed = fold_heads(nn(probs.astype(B16), v), heads).astype(B16)
    part_out[...] = nn(mixed, wo[...]).astype(B16)


def attend_kernel(
    g, heads, q, k, v, latents, part_one, part_two, gain, wk, wv, wo,
    part_out, o_out, probs_out, side_out, mid_out, mid_low_out,
):
    mid = latents[...].astype(F32) + (part_one[...].astype(F32) + part_two[...].astype(F32))
    mid_out[...] = mid
    mid_low_out[...] = mid.astype(B16)
    unit, _ = norm_parts(mid[g * L : (g + 1) * L])
    side_low = (unit * gain[...]).astype(B16)
    side_k = nn(side_low, wk[...]).astype(B16).astype(F32)
    side_v = nn(side_low, wv[...]).astype(B16).astype(F32)
    width = side_k.shape[1]
    side_out[:, :width] = side_k
    side_out[:, width : 2 * width] = side_v
    side_out[:, 2 * width :] = side_low.astype(F32)
    side_v = spread_heads(side_v, heads).astype(B16)
    side_scores = nt(spread_heads(side_k, heads).astype(B16), q[...])
    scale = FACTOR * LOG2E
    outs, side_probs, lses = [], [], []
    for pair in range(heads // 2):
        cut = slice(pair * 2 * E, (pair + 1) * 2 * E)
        q_pair, k_pair, v_pair = q[:, cut], k[:, cut], v[:, cut]
        for second in (0, 1):
            h = 2 * pair + second
            scores = nt(head_only(k_pair, second), q_pair)
            side = side_scores[h * L : (h + 1) * L]
            top = jnp.maximum(
                jnp.max(scores, axis=0, keepdims=True), jnp.max(side, axis=0, keepdims=True)
            )
            weights = jnp.exp2((scores - top) * scale)
            side = jnp.exp2((side - top) * scale)
            total = jnp.sum(weights, axis=0, keepdims=True) + jnp.sum(side, axis=0, keepdims=True)
            inverse = 1.0 / total
            side_probs.append(side * inverse)
            lses.append(top * scale + jnp.log2(total))
            outs.append(tn((weights * inverse).astype(B16), v_pair))
    side_probs = jnp.concatenate(side_probs, axis=0)
    probs_out[: heads * L, :] = side_probs
    probs_out[heads * L :, :] = jnp.concatenate(
        lses + [jnp.zeros_like(lses[0])] * (8 - heads), axis=0
    )
    side_o = tn(side_probs.astype(B16), side_v)
    first = half_mask(2 * E)
    token_o = jnp.concatenate(
        [jnp.where(first, outs[2 * i], outs[2 * i + 1]) for i in range(heads // 2)], axis=1
    )
    o = (token_o + side_o).astype(B16)
    o_out[...] = o
    part_out[...] = nn(o, wo[...]).astype(B16)


def feed_kernel(
    tokens, part_one, part_two, cotangent, gain, up, up_bias, down,
    part_out, active_out, hidden_grad_out, low_out, middle_out, down_part_out, up_bias_out, down_bias_out,
    part_sum, down_sum,
):
    step = pl.program_id(0)

    @pl.when(step == 0)
    def _():
        middle = tokens[...].astype(F32) + (part_one[...].astype(F32) + part_two[...].astype(F32))
        middle_out[...] = middle
        unit, _ = norm_parts(middle)
        low_out[...] = (unit * gain[...]).astype(B16)
        down_bias_out[...] = jnp.sum(cotangent[...].astype(F32), axis=0, keepdims=True)
        part_sum[...] = jnp.zeros_like(part_sum)
        down_sum[...] = jnp.zeros_like(down_sum)

    hidden = nn(low_out[...], up[...]) + up_bias[...]
    active, slope = gelu_both(hidden)
    active = active.astype(B16)
    active_out[...] = active
    grad = (slope * nt(cotangent[...], down[...])).astype(B16)
    hidden_grad_out[...] = grad
    up_bias_out[...] = jnp.sum(grad.astype(F32), axis=0, keepdims=True)
    part_sum[...] += nt(grad, up[...])
    down_sum[...] += nn(active, down[...])

    @pl.when(step == pl.num_programs(0) - 1)
    def _():
        part_out[...] = part_sum[...].astype(B16)
        down_part_out[...] = down_sum[...].astype(B16)


def turn_kernel(
    g, heads, cotangent, middle, part_one, part_two, gain, wo, wk, wv, o, q, probs, side, mid, *rest
):
    earlier, outs = rest[:g], rest[g:]
    o_grad_out, delta_out, side_score_grad_out, part_out, grads_out, gain_out = outs[:6]
    middle_grad_out, middle_low_out = outs[6:]
    unit, rate = norm_parts(middle[...])
    grad = part_one[...].astype(F32) + part_two[...].astype(F32)
    gain_out[0:1, :] = jnp.sum(grad * unit, axis=0, keepdims=True)
    middle_grad = cotangent[...].astype(F32) + norm_back(grad, unit, rate, gain[...])
    middle_grad_out[...] = middle_grad
    middle_low = middle_grad.astype(B16)
    middle_low_out[...] = middle_low
    o_grad = nt(middle_low, wo[...]).astype(B16)
    o_grad_out[...] = o_grad
    width = o_grad.shape[1]
    rows8 = lax.broadcasted_iota(jnp.int32, (8, width), 0)
    columns8 = lax.broadcasted_iota(jnp.int32, (8, width), 1) // E
    pick = (rows8 == columns8).astype(B16)
    weighted = o_grad.astype(F32) * o[...].astype(F32)
    high = weighted.astype(B16)
    low = (weighted - high.astype(F32)).astype(B16)
    delta = nt(pick, high) + nt(pick, low)
    delta_out[...] = delta
    side_v = spread_heads(side[:, width : 2 * width], heads).astype(B16)
    side_prob_grad = nt(side_v, o_grad)
    side_probs = probs[: heads * L, :]
    wide = jnp.concatenate(
        [jnp.broadcast_to(delta[h : h + 1], (L, delta.shape[1])) for h in range(heads)], axis=0
    )
    score_grad = (side_probs * (side_prob_grad - wide)).astype(B16)
    side_score_grad_out[...] = score_grad
    k_grad = (fold_heads(nn(score_grad, q[...]), heads) * FACTOR).astype(B16)
    v_grad = fold_heads(nn(side_probs.astype(B16), o_grad), heads).astype(B16)
    grads_out[:, :width] = k_grad.astype(F32)
    grads_out[:, width:] = v_grad.astype(F32)
    part = nt(k_grad, wk[...]) + nt(v_grad, wv[...])
    side_unit, _ = norm_parts(mid[g * L : (g + 1) * L, :])
    gain_out[1:2, :] = jnp.sum(part * side_unit, axis=0, keepdims=True)
    gain_out[2:, :] = jnp.zeros_like(gain_out[2:, :])
    part = jnp.concatenate([r[...] for r in earlier] + [part], axis=0)
    part_out[...] = part.astype(part_out.dtype)


def side_kernel(part_one, part_two, mid, cotangent, gain, low_out, grad_out):
    unit, rate = norm_parts(mid[...])
    part = part_one[...].astype(F32) + part_two[...].astype(F32)
    grad = cotangent[...].astype(F32) + norm_back(part, unit, rate, gain[...])
    grad_out[...] = grad
    low_out[...] = grad.astype(B16)


def attend_back_kernel(
    heads, tokens, q, k, v, o_grad, probs, delta, side_score_grad, side, wq, wk, wv, earlier_gain, *rest
):
    side_gains, (part_out, grads_out, gain_out) = rest[:-3], rest[-3:]
    scale = FACTOR * LOG2E
    first = half_mask(2 * E)
    width = q.shape[1]
    side_k = spread_heads(side[:, :width], heads).astype(B16)
    side_q_grad = tn(side_score_grad[...], side_k)
    at = heads * L
    for pair in range(heads // 2):
        start = pair * 2 * E
        cut = slice(start, start + 2 * E)
        q_pair, k_pair, v_pair, grad_pair = q[:, cut], k[:, cut], v[:, cut], o_grad[:, cut]
        q_grads, k_grads, v_grads = [], [], []
        for second in (0, 1):
            h = 2 * pair + second
            scores = nt(head_only(k_pair, second), q_pair)
            weights = jnp.exp2(scores * scale - probs[at + h : at + h + 1, :])
            prob_grad = nt(head_only(v_pair, second), grad_pair)
            score_grad = (weights * (prob_grad - delta[h : h + 1, :])).astype(B16)
            v_grads.append(nn(weights.astype(B16), grad_pair))
            k_grads.append(nn(score_grad, q_pair))
            q_grads.append(tn(score_grad, k_pair))
        q_pair_grad = jnp.where(first, q_grads[0], q_grads[1]) + side_q_grad[:, cut]
        k_pair_grad = jnp.where(first, k_grads[0], k_grads[1])
        v_pair_grad = jnp.where(first, v_grads[0], v_grads[1])
        grads_out[:, start : start + 2 * E] = (q_pair_grad * FACTOR).astype(B16)
        grads_out[:, width + start : width + start + 2 * E] = (k_pair_grad * FACTOR).astype(B16)
        grads_out[:, 2 * width + start : 2 * width + start + 2 * E] = v_pair_grad.astype(B16)
    part = nt(grads_out[:, :width], wq[...]) + nt(grads_out[:, width : 2 * width], wk[...])
    part = part + nt(grads_out[:, 2 * width :], wv[...])
    part_out[...] = part.astype(B16)
    unit, _ = norm_parts(tokens[...].astype(F32))
    total = earlier_gain[...] + jnp.sum(part * unit, axis=0, keepdims=True)
    for r in side_gains:
        total = total + r[1:2, :]
    gain_out[...] = total


def leave_kernel(groups, tokens, gain, *refs):
    grad_out = refs[-1]
    for g in range(groups):
        part_one, part_two, middle_grad = refs[3 * g : 3 * g + 3]
        rows = slice(g * S, (g + 1) * S)
        unit, rate = norm_parts(tokens[rows, :].astype(F32))
        grad = part_one[...].astype(F32) + part_two[...].astype(F32)
        grad_out[rows, :] = middle_grad[...] + norm_back(grad, unit, rate, gain[...])


def result_kernel(groups, bias, *refs):
    out = refs[-1]
    for g in range(groups):
        middle, part_one, part_two = refs[3 * g : 3 * g + 3]
        rows = slice(g * S, (g + 1) * S)
        total = part_one[...].astype(F32) + part_two[...].astype(F32)
        out[rows, :] = (middle[...] + total + bias[...]).astype(B16)


def latent_leave_kernel(latents, part_one, part_two, gain, mid_grad, grad_out, gain_out):
    own = latents.shape[0]
    unit, rate = norm_parts(latents[...].astype(F32))
    total = part_one[...].astype(F32) + part_two[...].astype(F32)
    grad_out[...] = mid_grad[...] + norm_back(total[:own], unit, rate, gain[...])
    gain_out[...] = total[own : own + 8]


def split_pairs(values, bit, share, send_out, keep_out, cut):
    blocks = values.reshape(values.shape[0] // (2 * share), 2, share, values.shape[1])
    even, odd = blocks[:, 0], blocks[:, 1]
    send_out[:, :, cut] = jnp.where(bit == 0, odd, even).astype(B16)
    keep_out[:, :, cut] = jnp.where(bit == 0, even, odd).astype(B16)


def weight_grad_kernel(groups, share, chunk, me, *refs):
    lefts, rights = refs[:groups], refs[groups : 2 * groups]
    send_out, keep_out = refs[2 * groups :]
    flat = [left[...].T for left in lefts]
    for start in range(0, rights[0].shape[1], chunk):
        cut = slice(start, start + chunk)
        total = nn(flat[0], rights[0][:, cut])
        for g in range(1, groups):
            total = total + nn(flat[g], rights[g][:, cut])
        split_pairs(total, me[0] % 2, share, send_out, keep_out, cut)


def attention_grad_kernel(groups, share, me, gain_one, gain_two, *refs):
    saved, grads, middle_low, o, side, side_grads, up_bias, down_bias, gains = (
        refs[i * groups : (i + 1) * groups] for i in range(9)
    )
    send_out, keep_out = refs[9 * groups :]
    bit = me[0] % 2
    width = o[0].shape[1]
    model = middle_low[0].shape[1]
    stack = [jnp.concatenate([r[...] for r in rs], axis=0) for rs in (side, side_grads)]
    side_low = stack[0][:, 2 * width :].astype(B16)
    side_k, side_v = stack[1][:, :width].astype(B16), stack[1][:, width:].astype(B16)
    flat = [r[:, 3 * width :].T for r in saved]
    low_flat = [r[...].T for r in middle_low]

    def total_of(lefts, rights, cut):
        total = nn(lefts[0], rights[0][:, cut])
        for g in range(1, groups):
            total = total + nn(lefts[g], rights[g][:, cut])
        return total

    def cut_of(i):
        return slice(i * width, (i + 1) * width)

    split_pairs(total_of(flat, grads, cut_of(0)), bit, share, send_out, keep_out, cut_of(0))
    total = total_of(flat, grads, cut_of(1)) + tn(side_low, side_k)
    split_pairs(total, bit, share, send_out, keep_out, cut_of(1))
    total = total_of(flat, grads, cut_of(2)) + tn(side_low, side_v)
    split_pairs(total, bit, share, send_out, keep_out, cut_of(2))
    total = total_of(low_flat, o, cut_of(0))
    split_pairs(total, bit, share, send_out, keep_out, cut_of(3))

    def column(rows):
        return jnp.broadcast_to(rows, (8, rows.shape[1])).T

    def sum_of(parts):
        total = parts[0]
        for part in parts[1:]:
            total = total + part
        return total

    columns = [
        column(sum_of([r[...] for r in down_bias])),
        column(sum_of([r[0:1, :] for r in gains])),
        column(gain_one[...] + gain_two[...]),
    ]
    bias = column(sum_of([r[...] for r in up_bias]))
    times = bias.shape[0] // model
    bias = bias.reshape(model // share, times, share, 8)
    columns += [bias[:, i].reshape(model, 8) for i in range(times)]
    lane = lax.broadcasted_iota(jnp.int32, (model, 128), 1)
    block = jnp.zeros((model, 128), F32)
    for i, one in enumerate(columns):
        block = jnp.where(lane == i, one[:, 0:1], block)
    split_pairs(block, bit, share, send_out, keep_out, slice(4 * width, 4 * width + 128))


def halve_kernel(shift, me, keep, got, send_out, keep_out):
    bit = (me[0] // shift) % 2
    for i in range(keep.shape[0]):
        there = keep[i, pl.ds(1 - bit, 1)].astype(F32) + got[i, pl.ds(1 - bit, 1)].astype(F32)
        here = keep[i, pl.ds(bit, 1)].astype(F32) + got[i, pl.ds(bit, 1)].astype(F32)
        send_out[pl.ds(i, 1)] = there.astype(B16)
        keep_out[pl.ds(i, 1)] = here.astype(B16)


def spread_kernel(shift, me, keep, got, own_out, *outs):
    place = me[0] // shift
    for k in range(keep.shape[0]):
        at = pl.ds(place ^ k, 1)
        total = (keep[at].astype(F32) + got[at].astype(F32))[0]
        if k == 0:
            own_out[...] = total
        else:
            outs[k - 1][...] = total.astype(B16)


def finish_kernel(cuts, own, *refs):
    gots, outs = refs[: len(refs) - len(cuts)], refs[len(refs) - len(cuts) :]
    total = own[...]
    for got in gots:
        total = total + got[...].astype(F32)
    for out, (start, end, flat) in zip(outs, cuts):
        part = total[:, start:end]
        out[...] = part.T if flat else part


def latent_back_kernel(
    heads, own, block, me, latents, q, k, v, mid_one, mid_two, images_column, images_row, gain, wq, wk, wv, wo,
    part_out, wq_out, wk_out, wv_out, wo_out, mixed, q_grad, k_grad, v_grad,
):
    mid_low = jnp.concatenate([mid_one[...], mid_two[...]], axis=0)
    o_grad = nt(mid_low, wo[...]).astype(B16)
    unit, _ = norm_parts(latents[...].astype(F32))
    low = (unit * gain[...]).astype(B16)
    everyone = low.shape[0]

    def rows_of(start, ref_q, ref_grad, ref_images):
        wide_q = spread_heads(ref_q, heads)
        wide_grad = spread_heads(ref_grad, heads)
        scores = nt(wide_q, k[...]) * FACTOR
        member = jnp.concatenate([ref_images] * heads, axis=0) == images_row[...]
        scores = jnp.where(member, scores, NEGATIVE)
        weights = jnp.exp(scores - jnp.max(scores, axis=-1, keepdims=True))
        probs = weights / jnp.sum(weights, axis=-1, keepdims=True)
        probs_low = probs.astype(B16)
        prob_grad = nt(wide_grad, v[...])
        delta = jnp.sum(prob_grad * probs, axis=-1, keepdims=True)
        score_grad = (probs * (prob_grad - delta)).astype(B16)
        mixed[pl.ds(start, block), :] = fold_heads(nn(probs_low, v[...]), heads).astype(B16)
        q_grad[pl.ds(start, block), :] = (
            fold_heads(nn(score_grad, k[...]), heads) * FACTOR
        ).astype(B16)
        return tn(score_grad, wide_q), tn(probs_low, wide_grad)

    if block == everyone:
        k_sum, v_sum = rows_of(0, q[...], o_grad, images_column[...])
        k_sum, v_sum = k_sum * FACTOR, v_sum
    else:
        v_grad[...] = o_grad

        def step(i, held):
            start = pl.multiple_of(i * block, block)
            here = pl.ds(start, block)
            one, two = rows_of(start, q[here, :], v_grad[here, :], images_column[here, :])
            return held[0] + one, held[1] + two

        zero = jnp.zeros(k.shape, F32)
        k_sum, v_sum = lax.fori_loop(0, everyone // block, step, (zero, zero))
        k_sum = k_sum * FACTOR
    k_grad[...] = k_sum.astype(B16)
    v_grad[...] = v_sum.astype(B16)
    part = nt(q_grad[...], wq[...]) + nt(k_grad[...], wk[...]) + nt(v_grad[...], wv[...])
    gain_part = jnp.sum(part * unit, axis=0, keepdims=True)
    part_out[...] = jnp.concatenate(
        [part[:own], jnp.broadcast_to(gain_part, (16, part.shape[1]))], axis=0
    ).astype(B16)
    share = wq_out.shape[0]
    model = low.shape[1]
    row = lax.broadcasted_iota(jnp.int32, (share, model), 0)
    column = lax.broadcasted_iota(jnp.int32, (share, model), 1)
    pick = (column == row + me[0] * share).astype(B16)
    columns = nt(pick, low).astype(B16)
    wq_out[...] = nn(columns, q_grad[...])
    wk_out[...] = nn(columns, k_grad[...])
    wv_out[...] = nn(columns, v_grad[...])
    wo_out[...] = nn(nt(pick, mid_low).astype(B16), mixed[...])


MIB = 1024 * 1024
KEPT = "kept"


class Order:
    def __init__(self):
        self.last = None

    def call(self, kernel, name, outs, ins, grid=(1,), scratch=(), limit=24):
        def spec(shape, block):
            if block is None:
                return pl.BlockSpec(tuple(shape), lambda *_: (0,) * len(shape))
            if block == "smem":
                return pl.BlockSpec(memory_space=pltpu.SMEM)
            extent, where = block
            if isinstance(extent, int):
                return pl.BlockSpec((extent, shape[1]), lambda *_: (where, 0))
            return pl.BlockSpec(extent, where)

        arrays = [entry[0] for entry in ins]
        if self.last is not None:
            least = min(range(len(arrays)), key=lambda i: arrays[i].size)
            arrays[least] = after(arrays[least], self.last)
        arrays = [
            pltpu.with_memory_space_constraint(a, pltpu.HBM) if KEPT in entry[2:] else a
            for a, entry in zip(arrays, ins)
        ]
        results = pl.pallas_call(
            kernel,
            out_shape=[
                pltpu.HBM(entry[0], entry[1])
                if KEPT in entry[3:]
                else jax.ShapeDtypeStruct(entry[0], entry[1])
                for entry in outs
            ],
            grid=grid,
            in_specs=[spec(entry[0].shape, entry[1]) for entry in ins],
            out_specs=[spec(entry[0], entry[2]) for entry in outs],
            scratch_shapes=list(scratch),
            compiler_params=pltpu.CompilerParams(vmem_limit_bytes=limit * MIB),
            cost_estimate=pl.CostEstimate(flops=0, bytes_accessed=0, transcendentals=0),
            name=name,
        )(*arrays)
        self.last = min(results, key=lambda a: a.size)
        return results


def after(value, *earlier):
    return lax.optimization_barrier((value, earlier))[0]


def swap_tp(values):
    return lax.ppermute(values, "tp", [(0, 1), (1, 0)])


def flip(values, bits):
    size = lax.axis_size("dp")
    return lax.ppermute(values, "dp", [(i, i ^ bits) for i in range(size)])


def gather_steps(size):
    width, steps = 2, []
    while width * 4 < size:
        steps.append([width])
        width *= 2
    if width < size:
        steps.append([width * k for k in range(1, size // width)])
    steps.reverse()
    return steps + [[1]]


def gather_order(size):
    order = [0]
    for step in gather_steps(size):
        order = order + [i ^ bits for bits in [0] + step for i in order][len(order) :]
    return order


def gather_relative(own):
    held = own
    for step in gather_steps(lax.axis_size("dp"))[:-1]:
        held = jnp.concatenate([held] + [flip(held, bits) for bits in step], axis=0)
    return held, flip(held, 1)


def scatter_sum(grads):
    size = lax.axis_size("dp")
    me = lax.axis_index("dp")
    width = 1
    while width * 4 < size:
        bit = (me // width) % 2
        pairs = grads.reshape((grads.shape[0] // 2, 2) + grads.shape[1:])
        send = lax.dynamic_index_in_dim(pairs, 1 - bit, 1, keepdims=False)
        keep = lax.dynamic_index_in_dim(pairs, bit, 1, keepdims=False)
        got = flip(send.astype(B16), width)
        grads = keep.astype(F32) + got.astype(F32)
        width *= 2
    place = me // width
    total = lax.dynamic_index_in_dim(grads, place, 0, keepdims=False)
    for k in range(1, size // width):
        send = lax.dynamic_index_in_dim(grads, place ^ k, 0, keepdims=False)
        total = total + flip(send.astype(B16), width * k).astype(F32)
    return total


class Scatter:
    def __init__(self, order, share, me):
        self.order, self.share, self.me = order, share, me

    def begin(self, send, keep):
        self.keep, self.got, self.width = keep, flip(send, 1), 2

    def halve(self):
        n, share, columns = self.keep.shape
        four = (n // 2, 2, share, columns)
        half = (n // 2, share, columns)
        send, keep = self.order.call(
            partial(halve_kernel, self.width),
            "halve",
            [(half, B16, None), (half, B16, None, KEPT)],
            [
                (self.me, "smem"),
                (self.keep.reshape(four), None, KEPT),
                (self.got.reshape(four), None),
            ],
        )
        self.keep, self.got = keep, flip(send, self.width)
        self.width *= 2

    def spread(self):
        n, share, columns = self.keep.shape
        flat = (share, columns)
        own, *sends = self.order.call(
            partial(spread_kernel, self.width),
            "spread",
            [(flat, F32, None, KEPT)] + [(flat, B16, None)] * (n - 1),
            [(self.me, "smem"), (self.keep, None, KEPT), (self.got, None)],
        )
        self.own = own
        self.gots = [flip(s, self.width * (k + 1)) for k, s in enumerate(sends)]

    def finish(self, cuts):
        share = self.own.shape[0]
        shapes = [(e - s, share) if flat else (share, e - s) for s, e, flat in cuts]
        return self.order.call(
            partial(finish_kernel, cuts),
            "finish",
            [(shape, F32, None) for shape in shapes],
            [(self.own, None, KEPT)] + [(got, None) for got in self.gots],
        )


def local(
    tokens,
    latents,
    latent_query,
    latent_key,
    latent_value,
    latent_output,
    query_weight,
    key_weight,
    value_weight,
    output_weight,
    up_weight,
    up_bias,
    down_weight,
    down_bias,
    latent_gain,
    attention_gain,
    feed_gain,
    group_image,
    token_cotangent,
    latent_cotangent,
):
    size = lax.axis_size("dp")
    me = lax.axis_index("dp")
    me_row = me.reshape(1)
    width = latent_query.shape[1]
    heads = width // E
    rows, model = tokens.shape
    hidden_units = up_weight.shape[1]
    groups = rows // S
    own = latents.shape[0]
    everyone = own * size
    share = model // size
    aligned = share % 16 == 0 and size >= 8
    each = range(groups)
    latent_gain_row = latent_gain.reshape(1, model)
    attention_gain_row = attention_gain.reshape(1, model)
    feed_gain_row = feed_gain.reshape(1, model)
    up_bias_row = up_bias.reshape(1, hidden_units)
    down_bias_row = down_bias.reshape(1, model)
    chain = Order()
    call = chain.call

    latents_one, latents_two = gather_relative(latents)
    turns = jnp.bitwise_xor(jnp.array(gather_order(size), jnp.int32), me)
    images = jnp.repeat(group_image.reshape(size, groups)[turns].reshape(-1), L)
    q, k, v, saved = zip(
        *(
            call(
                enter_kernel,
                "enter",
                [((S, width), B16, None)] * 3 + [((S, 3 * width + model), B16, None, KEPT)],
                [
                    (tokens, (S, g), KEPT),
                    (attention_gain_row, None),
                    (query_weight, None, KEPT),
                    (key_weight, None, KEPT),
                    (value_weight, None, KEPT),
                ],
            )
            for g in each
        )
    )
    latents_all, lat_q, lat_k, lat_v, latent_part = call(
        partial(latent_kernel, heads, own),
        "latent",
        [((everyone, model), B16, None, KEPT)]
        + [((everyone, width), B16, None, KEPT)] * 3
        + [((own, model), B16, None)],
        [
            (latents_one, None),
            (latents_two, None),
            (latent_gain_row, None),
            (images[:own].reshape(own, 1), None),
            (images.reshape(1, everyone), None),
            (latent_query, None),
            (latent_key, None),
            (latent_value, None),
            (latent_output, None),
        ],
        limit=24 if everyone <= 512 else 56,
    )
    latent_part_two = swap_tp(latent_part)
    part, o, probs, side, mids, mid_lows = zip(
        *(
            call(
                partial(attend_kernel, g, heads),
                "attend",
                [
                    ((S, model), B16, None),
                    ((S, width), B16, None, KEPT),
                    ((heads * L + 8, S), F32, None, KEPT),
                    ((L, 2 * width + model), F32, None, KEPT),
                    ((own, model), F32, None, KEPT),
                    ((own, model), B16, None, KEPT),
                ],
                [
                    (q[g], None),
                    (k[g], None),
                    (v[g], None),
                    (latents, None),
                    (latent_part, None),
                    (latent_part_two, None),
                    (attention_gain_row, None),
                    (key_weight, None),
                    (value_weight, None),
                    (output_weight, None),
                ],
            )
            for g in each
        )
    )
    mid, mixed_latents = mids[0], mid_lows[0]
    part_two = [swap_tp(p) for p in part]
    chunk = hidden_units // 3
    step = (S, chunk), lambda i: (0, i)
    (
        feed_part,
        active,
        hidden_grad,
        feed_low,
        middle,
        down_part,
        up_bias_sum,
        down_bias_sum,
    ) = zip(
        *(
            call(
                feed_kernel,
                "feed",
                [
                    ((S, model), B16, None),
                    ((S, hidden_units), B16, step),
                    ((S, hidden_units), B16, step),
                    ((S, model), B16, None),
                    ((S, model), F32, None, KEPT),
                    ((S, model), B16, None, KEPT),
                    ((1, hidden_units), F32, ((1, chunk), lambda i: (0, i)), KEPT),
                    ((1, model), F32, None, KEPT),
                ],
                [
                    (tokens, (S, g)),
                    (part[g], None),
                    (part_two[g], None),
                    (token_cotangent, (S, g)),
                    (feed_gain_row, None),
                    (up_weight, ((model, chunk), lambda i: (0, i))),
                    (up_bias_row, ((1, chunk), lambda i: (0, i))),
                    (down_weight, ((chunk, model), lambda i: (i, 0))),
                ],
                grid=(hidden_units // chunk,),
                scratch=[pltpu.VMEM((S, model), F32)] * 2,
            )
            for g in each
        )
    )
    feed_part_two = [swap_tp(p) for p in feed_part]

    def weight_grad(lefts, rights, blocks):
        columns = rights[0].shape[1]
        half = (size // 2, share, columns)
        return call(
            partial(weight_grad_kernel, groups, share, columns // 3),
            "weight_grad",
            [(half, B16, None), (half, B16, None, KEPT)],
            [(me_row, "smem")] + list(zip(lefts, blocks)) + [(a, None) for a in rights],
        )

    def turn(g, earlier):
        last = g == groups - 1
        return call(
            partial(turn_kernel, g, heads),
            "turn",
            [
                ((S, width), B16, None),
                ((8, S), F32, None),
                ((heads * L, S), B16, None),
                ((own if last else L, model), B16 if last else F32, None),
                ((L, 2 * width), F32, None, KEPT),
                ((8, model), F32, None, KEPT),
                ((S, model), F32, None, KEPT),
                ((S, model), B16, None, KEPT),
            ],
            [
                (token_cotangent, (S, g)),
                (middle[g], None, KEPT),
                (feed_part[g], None),
                (feed_part_two[g], None),
                (feed_gain_row, None),
                (output_weight, None),
                (key_weight, None),
                (value_weight, None),
                (o[g], None, KEPT),
                (saved[g], ((S, width), lambda *_: (0, 0)), KEPT),
                (probs[g], None, KEPT),
                (side[g], None, KEPT),
                (mid, None, KEPT),
            ]
            + [(a, None) for a in earlier],
        )

    down_sum, up_sum, rest_sum = (Scatter(chain, share, me_row) for _ in range(3))
    if aligned:
        blocks = [(S, g) for g in each]
        down_sum.begin(*weight_grad([token_cotangent] * groups, active, blocks))
    turned = []
    for g in each:
        turned.append(turn(g, [t[3] for t in turned]))
        if aligned and g == 0:
            down_sum.halve()
            up_sum.begin(*weight_grad(feed_low, hidden_grad, [None] * groups))
    (
        o_grad,
        delta,
        side_score_grad,
        side_parts,
        side_grads,
        gains,
        middle_grad,
        middle_low,
    ) = zip(*turned)
    side_part = side_parts[-1]
    side_part_two = swap_tp(side_part)
    if aligned:
        up_sum.halve()
    back = []
    gain_sum = jnp.zeros((1, model), F32)
    for g in each:
        last = g == groups - 1
        back.append(
            call(
                partial(attend_back_kernel, heads),
                "attend_back",
                [
                    ((S, model), B16, None),
                    ((S, 3 * width), B16, None),
                    ((1, model), F32, None),
                ],
                [(tokens, (S, g), KEPT)]
                + [
                    (saved[g], ((S, width), lambda *_, i=i: (0, i)), KEPT) for i in range(3)
                ]
                + [
                    (o_grad[g], None),
                    (probs[g], None, KEPT),
                    (delta[g], None),
                    (side_score_grad[g], None),
                    (side[g], None, KEPT),
                    (query_weight, None),
                    (key_weight, None),
                    (value_weight, None),
                    (gain_sum, None),
                ]
                + [(a, None, KEPT) for a in gains if last],
            )
        )
        gain_sum = back[-1][2]
        if g == 0:
            mid_low, middle_latent_grad = call(
                side_kernel,
                "side",
                [((own, model), B16, None), ((own, model), F32, None, KEPT)],
                [
                    (side_part, None),
                    (side_part_two, None),
                    (mid, None, KEPT),
                    (latent_cotangent, None),
                    (attention_gain_row, None),
                ],
            )
    mid_low_one, mid_low_two = gather_relative(mid_low)
    token_part, grads, _ = zip(*back)
    gain_two = swap_tp(gain_sum)
    token_part_two = [swap_tp(p) for p in token_part]
    if aligned:
        columns = 4 * width + 128
        half = (size // 2, share, columns)
        arrays = (saved, grads, middle_low, o, side, side_grads, up_bias_sum, down_bias_sum, gains)
        kept = [a for of_groups in arrays for a in of_groups]
        down_sum.spread()
        rest_sum.begin(
            *call(
                partial(attention_grad_kernel, groups, share),
                "attention_grad",
                [(half, B16, None), (half, B16, None, KEPT)],
                [(me_row, "smem"), (gain_sum, None), (gain_two, None)]
                + [(a, None) if any(a is b for b in grads) else (a, None, KEPT) for a in kept],
            )
        )
        up_sum.spread()
        rest_sum.halve()
    else:

        def flat(arrays, start, end):
            return jnp.concatenate([a[:, start:end] for a in arrays], axis=0).astype(B16)

        token_low = flat(saved, 3 * width, 3 * width + model)
        side_low = flat(side, 2 * width, 2 * width + model)
        products = (
            tn(token_cotangent, flat(active, 0, hidden_units)),
            tn(flat(feed_low, 0, model), flat(hidden_grad, 0, hidden_units)),
            tn(token_low, flat(grads, 0, width)),
            tn(token_low, flat(grads, width, 2 * width)) + tn(side_low, flat(side_grads, 0, width)),
            tn(token_low, flat(grads, 2 * width, 3 * width))
            + tn(side_low, flat(side_grads, width, 2 * width)),
            tn(flat(middle_low, 0, model), flat(o, 0, width)),
        )
        vectors = [sum(down_bias_sum), sum(gains)[:1], gain_sum + gain_two]
        vectors.append(sum(up_bias_sum).reshape(size, -1, share).swapaxes(0, 1).reshape(-1, model))
        vectors = jnp.concatenate(vectors, axis=0)
        total = jnp.concatenate([a.astype(B16) for a in products + (vectors.T,)], axis=1)
        total = scatter_sum(total.reshape(size, share, -1))
    block = min(everyone, max(16, 65536 // everyone))
    latent_sum, latent_query_done, latent_key_done, latent_value_done, latent_output_done = call(
        partial(latent_back_kernel, heads, own, block),
        "latent_back",
        [((own + 16, model), B16, None)] + [((share, width), F32, None)] * 4,
        [
            (me_row, "smem"),
            (latents_all, None, KEPT),
            (lat_q, None, KEPT),
            (lat_k, None, KEPT),
            (lat_v, None, KEPT),
            (mid_low_one, None),
            (mid_low_two, None),
            (images.reshape(everyone, 1), None),
            (images.reshape(1, everyone), None),
            (latent_gain_row, None),
            (latent_query, None),
            (latent_key, None),
            (latent_value, None),
            (latent_output, None),
        ],
        scratch=[pltpu.VMEM((everyone, width), B16)] * 4,
        limit=24 if everyone <= 512 else 56,
    )
    latent_sum_two = swap_tp(latent_sum)
    (token_grad,) = call(
        partial(leave_kernel, groups),
        "leave",
        [((rows, model), F32, None)],
        [(tokens, None, KEPT), (attention_gain_row, None)]
        + [
            entry
            for g in each
            for entry in (
                (token_part[g], None),
                (token_part_two[g], None),
                (middle_grad[g], None, KEPT),
            )
        ],
    )
    down_part_two = [swap_tp(after(p, *token_part_two)) for p in down_part]
    latent_grad, latent_gain_sum = call(
        latent_leave_kernel,
        "latent_leave",
        [((own, model), F32, None), ((8, model), F32, None)],
        [
            (latents, None),
            (latent_sum, None),
            (latent_sum_two, None),
            (latent_gain_row, None),
            (middle_latent_grad, None, KEPT),
        ],
    )
    latent_gain_done = lax.dynamic_slice_in_dim(latent_gain_sum[0], me * share, share)
    cuts = [(i * width, (i + 1) * width, i == 3) for i in range(4)]
    if aligned:
        rest_sum.spread()
        (down_done,) = down_sum.finish([(0, hidden_units, True)])
        (up_done,) = up_sum.finish([(0, hidden_units, False)])
    (mixed_tokens,) = call(
        partial(result_kernel, groups),
        "result",
        [((rows, model), B16, None)],
        [(down_bias_row, None)]
        + [
            entry
            for g in each
            for entry in (
                (middle[g], None, KEPT),
                (down_part[g], None),
                (down_part_two[g], None),
            )
        ],
    )
    if aligned:
        cuts.append((4 * width, 4 * width + 128, True))
        query_done, key_done, value_done, output_done, vectors = rest_sum.finish(cuts)
    else:
        ends = [hidden_units, 2 * hidden_units] + [2 * hidden_units + i * width for i in range(1, 5)]
        down_done, up_done, query_done, key_done, value_done, output_done, vectors = jnp.split(
            total, ends, axis=1
        )
        down_done, output_done, vectors = down_done.T, output_done.T, vectors.T
    return (
        mixed_tokens,
        mixed_latents,
        token_grad,
        latent_grad,
        latent_query_done,
        latent_key_done,
        latent_value_done,
        latent_output_done.T,
        query_done,
        key_done,
        value_done,
        output_done,
        up_done,
        vectors[3 : 3 + hidden_units // model].reshape(-1),
        down_done,
        vectors[0],
        latent_gain_done,
        vectors[2],
        vectors[1],
    )


def solution(mesh):
    placed = (
        P("dp", None),
        P("dp", None),
        P(None, "tp"),
        P(None, "tp"),
        P(None, "tp"),
        P("tp", None),
        P(None, "tp"),
        P(None, "tp"),
        P(None, "tp"),
        P("tp", None),
        P(None, "tp"),
        P("tp"),
        P("tp", None),
        P(),
        P(),
        P(),
        P(),
        P(),
        P("dp", None),
        P("dp", None),
    )
    return jax.shard_map(
        local,
        mesh=mesh,
        in_specs=placed,
        out_specs=(
            P("dp", None),
            P("dp", None),
            P("dp", None),
            P("dp", None),
            P("dp", "tp"),
            P("dp", "tp"),
            P("dp", "tp"),
            P("tp", "dp"),
            P("dp", "tp"),
            P("dp", "tp"),
            P("dp", "tp"),
            P("tp", "dp"),
            P("dp", "tp"),
            P(("tp", "dp")),
            P("tp", "dp"),
            P("dp"),
            P("dp"),
            P("dp"),
            P("dp"),
        ),
        check_vma=False,
    )
```

profile of v0, /device:TPU:0, one launch (start us, length us, event | category | flops | bytes accessed | tf_op | source)
XLA Modules:
  0.0 202.9 jit_solution(12447875648479830083)
XLA Ops:
  0.7 3.1 %collective-permute-start = (bf16[16,768]{1,0:T(8,128)(2,1)}, bf16[16,768]{1,0:T(8,128)(2,1)S(1)}, u32[]{:S(2)}, u32[]{:S(2)}) collective-permute-start(bf16[16,768]{1,0:T(8,128)(2,1)} %latents.5), channel_id=1, source_target_pairs={{0,4},{1,5},{2,6},{3,7},{4,0},{5,1},{6,2},{7,3},{8,12},{9,13},{10,... | collective-permute-start | bytes 73736 | tf_op jit(solution)/shard_map/ppermute | solution.py:552
  3.7 2.6 %collective-permute-start.1 = (bf16[16,768]{1,0:T(8,128)(2,1)}, bf16[16,768]{1,0:T(8,128)(2,1)S(1)}, u32[]{:S(2)}, u32[]{:S(2)}) collective-permute-start(bf16[16,768]{1,0:T(8,128)(2,1)} %latents.5), channel_id=1, source_target_pairs={{0,8},{1,9},{2,10},{3,11},{4,12},{5,13},{6,14},{7,15},{8,0},{9,1},... | collective-permute-start | bytes 73736 | tf_op jit(solution)/shard_map/ppermute | solution.py:552
  8.5 3.5 %enter.2 = (bf16[256,384]{1,0:T(8,128)(2,1)S(1)}, bf16[256,384]{1,0:T(8,128)(2,1)S(1)}, bf16[256,384]{1,0:T(8,128)(2,1)S(1)}, bf16[256,1920]{1,0:T(8,128)(2,1)}) custom-call(bf16[512,768]{1,0:T(8,128)(2,1)} %tokens.13, f32[1,768]{1,0:T(1,128)S(1)} %reshape.93.gain, bf16[768,384]{1,0:T(8,128)(2,1)} %wq.10, bf16[768,384]{1,0:T(8,128)(2,1)} %wk.18, ...), custom_call_target="tpu_custom_call" | custom-call | tf_op jit(solution)/shard_map/enter/pallas_call | solution.py:522
  12.8 3.7 %enter.3 = (bf16[256,384]{1,0:T(8,128)(2,1)S(1)}, bf16[256,384]{1,0:T(8,128)(2,1)S(1)}, bf16[256,384]{1,0:T(8,128)(2,1)S(1)}, bf16[256,1920]{1,0:T(8,128)(2,1)}) custom-call(bf16[512,768]{1,0:T(8,128)(2,1)} %tokens.13, f32[1,768]{1,0:T(1,128)S(1)} %reshape.93.gain, bf16[768,384]{1,0:T(8,128)(2,1)} %wq.10, bf16[768,384]{1,0:T(8,128)(2,1)} %wk.18, ...), custom_call_target="tpu_custom_call" | custom-call | tf_op jit(solution)/shard_map/enter/pallas_call | solution.py:522
  20.5 2.9 %collective-permute-done.3 = bf16[64,768]{1,0:T(8,128)(2,1)S(1)} collective-permute-done((bf16[64,768]{1,0:T(8,128)(2,1)S(1)}, bf16[64,768]{1,0:T(8,128)(2,1)S(1)}, u32[]{:S(2)}, u32[]{:S(2)}) %collective-permute-start.3) | collective-permute-done | bytes 98336 | tf_op jit(solution)/shard_map/ppermute | solution.py:552
  25.1 2.9 %latent.1 = (bf16[256,768]{1,0:T(8,128)(2,1)}, bf16[256,384]{1,0:T(8,128)(2,1)}, bf16[256,384]{1,0:T(8,128)(2,1)}, bf16[256,384]{1,0:T(8,128)(2,1)}, bf16[16,768]{1,0:T(8,128)(2,1)S(1)}) custom-call(bf16[128,768]{1,0:T(8,128)(2,1)S(1)} %constant_dynamic-update-slice_fusion.one, bf16[128,768]{1,0:T(8,128)(2,1)} %collective-permute-done.4.two, ...), custom_call_target="tpu_custom_call" | custom-call | tf_op jit(solution)/shard_map/latent/pallas_call | solution.py:522
  34.6 2.3 %attend.2 = (bf16[256,768]{1,0:T(8,128)(2,1)S(1)}, bf16[256,384]{1,0:T(8,128)(2,1)}, f32[56,256]{1,0:T(8,128)}, f32[8,1536]{1,0:T(8,128)}, f32[16,768]{1,0:T(8,128)}, /*index=5*/bf16[16,768]{1,0:T(8,128)(2,1)}) custom-call(bf16[256,384]{1,0:T(8,128)(2,1)S(1)} %copy-done.29, bf16[256,384]{1,0:T(8,128)(2,1)S(1)} %copy-done.31, ...), custom_call_target="tpu_custom_call" | custom-call | tf_op jit(solution)/shard_map/attend/pallas_call | solution.py:522
  39.6 2.3 %attend.3 = (bf16[256,768]{1,0:T(8,128)(2,1)S(1)}, bf16[256,384]{1,0:T(8,128)(2,1)}, f32[56,256]{1,0:T(8,128)}, f32[8,1536]{1,0:T(8,128)}, f32[16,768]{1,0:T(8,128)}, /*index=5*/bf16[16,768]{1,0:T(8,128)(2,1)}) custom-call(bf16[256,384]{1,0:T(8,128)(2,1)S(1)} %get-tuple-element.150.q, bf16[256,384]{1,0:T(8,128)(2,1)S(1)} %copy-done.25, ...), custom_call_target="tpu_custom_call" | custom-call | tf_op jit(solution)/shard_map/attend/pallas_call | solution.py:522
  42.4 6.6 %collective-permute-done.7.part_two = bf16[256,768]{1,0:T(8,128)(2,1)S(1)} collective-permute-done((bf16[256,768]{1,0:T(8,128)(2,1)S(1)}, bf16[256,768]{1,0:T(8,128)(2,1)S(1)}, u32[]{:S(2)}, u32[]{:S(2)}) %collective-permute-start.7) | collective-permute-done | bytes 393248 | tf_op jit(solution)/shard_map/ppermute | solution.py:547
  49.0 5.7 %feed.2 = (bf16[256,768]{1,0:T(8,128)(2,1)S(1)}, bf16[256,1536]{1,0:T(8,128)(2,1)S(1)}, bf16[256,1536]{1,0:T(8,128)(2,1)S(1)}, bf16[256,768]{1,0:T(8,128)(2,1)S(...) custom-call(bf16[512,768]{1,0:T(8,128)(2,1)S(1)} %copy-done, ...), custom_call_target="tpu_custom_call" | custom-call | tf_op jit(solution)/shard_map/feed/pallas_call | solution.py:522
  55.4 5.7 %feed.3 = (bf16[256,768]{1,0:T(8,128)(2,1)S(1)}, bf16[256,1536]{1,0:T(8,128)(2,1)S(1)}, bf16[256,1536]{1,0:T(8,128)(2,1)S(1)}, bf16[256,768]{1,0:T(8,128)(2,1)S(...) custom-call(bf16[512,768]{1,0:T(8,128)(2,1)S(1)} %copy-done, ...), custom_call_target="tpu_custom_call" | custom-call | tf_op jit(solution)/shard_map/feed/pallas_call | solution.py:522
  61.1 2.4 %weight_grad.2 = (bf16[8,48,1536]{2,1,0:T(8,128)(2,1)S(1)}, bf16[8,48,1536]{2,1,0:T(8,128)(2,1)}) custom-call(s32[1]{0:T(128)} %bitcast.me, bf16[512,768]{1,0:T(8,128)(2,1)S(1)} %copy-done.3, bf16[512,768]{1,0:T(8,128)(2,1)S(1)} %copy-done.3, bf16[256,1536]{1,0:T(8,128)(2,1)S(1)} %get-tuple-element.172.refs_2_, bf16[256,1536]{1,0:T(8,128)(2,1)S(1)} %get-tuple-element.173.refs_3_), custom_call_target="tpu_custom_call" | custom-call | tf_op jit(solution)/shard_map/weight_grad/pallas_call | solution.py:522
  65.2 9.9 %collective-permute-done.9.part_two = bf16[256,768]{1,0:T(8,128)(2,1)S(1)} collective-permute-done((bf16[256,768]{1,0:T(8,128)(2,1)S(1)}, bf16[256,768]{1,0:T(8,128)(2,1)S(1)}, u32[]{:S(2)}, u32[]{:S(2)}) %collective-permute-start.9) | collective-permute-done | bytes 393248 | tf_op jit(solution)/shard_map/ppermute | solution.py:547
  75.0 4.1 %turn.2 = (bf16[256,384]{1,0:T(8,128)(2,1)S(1)}, f32[8,256]{1,0:T(8,128)S(1)}, bf16[48,256]{1,0:T(8,128)(2,1)S(1)}, f32[8,768]{1,0:T(8,128)S(1)}, f32[8,768]{1,0...) custom-call(bf16[512,768]{1,0:T(8,128)(2,1)S(1)} %copy-done.3, ...), custom_call_target="tpu_custom_call" | custom-call | tf_op jit(solution)/shard_map/turn/pallas_call | solution.py:522
  81.5 2.4 %weight_grad.3 = (bf16[8,48,1536]{2,1,0:T(8,128)(2,1)S(1)}, bf16[8,48,1536]{2,1,0:T(8,128)(2,1)}) custom-call(s32[1]{0:T(128)} %bitcast.me, bf16[256,768]{1,0:T(8,128)(2,1)S(1)} %get-tuple-element.185.refs_0_, bf16[256,768]{1,0:T(8,128)(2,1)S(1)} %get-tuple-element.186.refs_1_, bf16[256,1536]{1,0:T(8,128)(2,1)S(1)} %get-tuple-element.187.refs_2_, ...), custom_call_target="tpu_custom_call" | custom-call | tf_op jit(solution)/shard_map/weight_grad/pallas_call | solution.py:522
  87.1 9.8 %collective-permute-done.8.part_two = bf16[256,768]{1,0:T(8,128)(2,1)S(1)} collective-permute-done((bf16[256,768]{1,0:T(8,128)(2,1)S(1)}, bf16[256,768]{1,0:T(8,128)(2,1)S(1)}, u32[]{:S(2)}, u32[]{:S(2)}) %collective-permute-start.8) | collective-permute-done | bytes 393248 | tf_op jit(solution)/shard_map/ppermute | solution.py:547
  96.8 4.2 %turn.3 = (bf16[256,384]{1,0:T(8,128)(2,1)S(1)}, f32[8,256]{1,0:T(8,128)S(1)}, bf16[48,256]{1,0:T(8,128)(2,1)S(1)}, bf16[16,768]{1,0:T(8,128)(2,1)S(1)}, f32[8,7...) custom-call(bf16[512,768]{1,0:T(8,128)(2,1)S(1)} %copy-done.3, ...), custom_call_target="tpu_custom_call" | custom-call | tf_op jit(solution)/shard_map/turn/pallas_call | solution.py:522
  102.5 2.3 %halve.4 = (bf16[4,48,1536]{2,1,0:T(8,128)(2,1)S(1)}, bf16[4,48,1536]{2,1,0:T(8,128)(2,1)}) custom-call(s32[1]{0:T(128)} %bitcast.me, bf16[4,2,48,1536]{3,2,1,0:T(8,128)(2,1)} %bitcast.22, bf16[4,2,48,1536]{3,2,1,0:T(8,128)(2,1)S(1)} %bitcast.19), custom_call_target="tpu_custom_call" | custom-call | tf_op jit(solution)/shard_map/halve/pallas_call | solution.py:522
  104.8 4.1 %attend_back.2 = (bf16[256,768]{1,0:T(8,128)(2,1)S(1)}, bf16[256,1152]{1,0:T(8,128)(2,1)S(1)}, f32[1,768]{1,0:T(1,128)S(1)}) custom-call(bf16[512,768]{1,0:T(8,128)(2,1)} %tokens.13, bf16[256,1920]{1,0:T(8,128)(2,1)} %get-tuple-element.177.q.k.v.refs_0_, bf16[256,1920]{1,0:T(8,128)(2,1)} %get-tuple-element.177.q.k.v.refs_0_, ...), custom_call_target="tpu_custom_call" | custom-call | tf_op jit(solution)/shard_map/attend_back/pallas_call | solution.py:522
  110.7 4.1 %attend_back.3 = (bf16[256,768]{1,0:T(8,128)(2,1)S(1)}, bf16[256,1152]{1,0:T(8,128)(2,1)S(1)}, f32[1,768]{1,0:T(1,128)S(1)}) custom-call(bf16[512,768]{1,0:T(8,128)(2,1)} %tokens.13, bf16[256,1920]{1,0:T(8,128)(2,1)} %get-tuple-element.149.q.k.v.refs_1_, bf16[256,1920]{1,0:T(8,128)(2,1)} %get-tuple-element.149.q.k.v.refs_1_, ...), custom_call_target="tpu_custom_call" | custom-call | tf_op jit(solution)/shard_map/attend_back/pallas_call | solution.py:522
  118.5 5.5 %attention_grad.1 = (bf16[8,48,1664]{2,1,0:T(8,128)(2,1)S(1)}, bf16[8,48,1664]{2,1,0:T(8,128)(2,1)}) custom-call(s32[1]{0:T(128)} %bitcast.me, f32[1,768]{1,0:T(1,128)S(1)} %get-tuple-element.210.gain_one, f32[1,768]{1,0:T(1,128)S(1)} %collective-permute-done.14.gain_two, bf16[256,1920]{1,0:T(8,128)(2,1)} %get-tuple-element.177.q.k.v.refs_0_, ...), custom_call_target="tpu_custom_call" | custom-call | tf_op jit(solution)/shard_map/attention_grad/pallas_call | solution.py:522
  125.2 3.5 %collective-permute-start.18 = (bf16[16,768]{1,0:T(8,128)(2,1)S(1)}, bf16[16,768]{1,0:T(8,128)(2,1)S(1)}, u32[]{:S(2)}, u32[]{:S(2)}) collective-permute-start(bf16[16,768]{1,0:T(8,128)(2,1)S(1)} %get-tuple-element.206), channel_id=1, source_target_pairs={{0,8},{1,9},{2,10},{3,11},{4,12},{5,13},{6,14},{7,15},{8,0},{9,1},... | collective-permute-start | bytes 73736 | tf_op jit(solution)/shard_map/ppermute | solution.py:552
  131.4 2.9 %collective-permute-done.19 = bf16[16,768]{1,0:T(8,128)(2,1)S(1)} collective-permute-done((bf16[16,768]{1,0:T(8,128)(2,1)S(1)}, bf16[16,768]{1,0:T(8,128)(2,1)S(1)}, u32[]{:S(2)}, u32[]{:S(2)}) %collective-permute-start.19) | collective-permute-done | bytes 24608 | tf_op jit(solution)/shard_map/ppermute | solution.py:552
  135.9 4.2 %collective-permute-done.15.got = bf16[4,48,1536]{2,1,0:T(8,128)(2,1)S(1)} collective-permute-done((bf16[4,48,1536]{2,1,0:T(8,128)(2,1)S(1)}, bf16[4,48,1536]{2,1,0:T(8,128)(2,1)S(1)}, u32[]{:S(2)}, u32[]{:S(2)}) %collective-permute-start.15) | collective-permute-done | bytes 589856 | tf_op jit(solution)/shard_map/ppermute | solution.py:552
  142.0 2.8 %halve.5 = (bf16[4,48,1664]{2,1,0:T(8,128)(2,1)}, bf16[4,48,1664]{2,1,0:T(8,128)(2,1)}) custom-call(s32[1]{0:T(128)} %bitcast.me, bf16[4,2,48,1664]{3,2,1,0:T(8,128)(2,1)} %bitcast.21, bf16[4,2,48,1664]{3,2,1,0:T(8,128)(2,1)S(1)} %bitcast.18), custom_call_target="tpu_custom_call" | custom-call | tf_op jit(solution)/shard_map/halve/pallas_call | solution.py:522
  147.0 3.5 %collective-permute-start.27 = (bf16[48,1536]{1,0:T(8,128)(2,1)}, bf16[48,1536]{1,0:T(8,128)(2,1)}, u32[]{:S(2)}, u32[]{:S(2)}) collective-permute-start(bf16[48,1536]{1,0:T(8,128)(2,1)} %get-tuple-element.250), channel_id=1, source_target_pairs={{0,8},{1,9},{2,10},{3,11},{4,12},{5,13},{6,14},{7,15},{8,0},{9,1},... | collective-permute-start | bytes 442376 | tf_op jit(solution)/shard_map/ppermute | solution.py:552
  155.9 6.7 %latent_back.1 = (bf16[32,768]{1,0:T(8,128)(2,1)S(1)}, f32[48,384]{1,0:T(8,128)}, f32[48,384]{1,0:T(8,128)}, f32[48,384]{1,0:T(8,128)}, f32[48,384]{1,0:T(8,128)}) custom-call(s32[1]{0:T(128)} %bitcast.me, bf16[256,768]{1,0:T(8,128)(2,1)} %get-tuple-element.231.latents, bf16[256,384]{1,0:T(8,128)(2,1)} %get-tuple-element.232.q, ...), custom_call_target="tpu_custom_call" | custom-call | tf_op jit(solution)/shard_map/latent_back/pallas_call | solution.py:522
  165.1 7.1 %collective-permute-done.22.part_two = bf16[32,768]{1,0:T(8,128)(2,1)S(1)} collective-permute-done((bf16[32,768]{1,0:T(8,128)(2,1)S(1)}, bf16[32,768]{1,0:T(8,128)(2,1)S(1)}, u32[]{:S(2)}, u32[]{:S(2)}) %collective-permute-start.22) | collective-permute-done | bytes 49184 | tf_op jit(solution)/shard_map/ppermute | solution.py:547
  172.2 2.8 %collective-permute-start.30 = (bf16[48,1536]{1,0:T(8,128)(2,1)S(1)}, bf16[48,1536]{1,0:T(8,128)(2,1)S(1)}, u32[]{:S(2)}, u32[]{:S(2)}) collective-permute-start(bf16[48,1536]{1,0:T(8,128)(2,1)S(1)} %copy-done.38), channel_id=1, source_target_pairs={{0,8},{1,9},{2,10},{3,11},{4,12},{5,13},{6,14},{7,15},{8,0},{9,1},... | collective-permute-start | bytes 442376 | tf_op jit(solution)/shard_map/ppermute | solution.py:552
  177.2 3.9 %leave.1 = f32[512,768]{1,0:T(8,128)} custom-call(bf16[512,768]{1,0:T(8,128)(2,1)} %tokens.13, f32[1,768]{1,0:T(1,128)S(1)} %reshape.93.gain, bf16[256,768]{1,0:T(8,128)(2,1)S(1)} %copy-done.15, bf16[256,768]{1,0:T(8,128)(2,1)S(1)} %copy-done.19, f32[256,768]{1,0:T(8,128)} %get-tuple-element.239.refs_2_, bf16[256,768]{1,0:T(8,128)(2,1)S(1)} %copy-done.17, ...), custom_call_target="tpu_custom_call" | custom-call | tf_op jit(solution)/shard_map/leave/pallas_call | solution.py:522
  193.7 3.0 %result.1 = bf16[512,768]{1,0:T(8,128)(2,1)} custom-call(f32[1,768]{1,0:T(1,128)S(1)} %reshape.91.bias, f32[256,768]{1,0:T(8,128)} %get-tuple-element.168.middle.refs_0_, bf16[256,768]{1,0:T(8,128)(2,1)} %get-tuple-element.258.refs_1_, bf16[256,768]{1,0:T(8,128)(2,1)} %collective-permute-done.32.refs_2_, f32[256,768]{1,0:T(8,128)} %get-tuple-element.166.middle.refs_3_, ...), custom_call_target="tpu_custom_call" | custom-call | tf_op jit(solution)/shard_map/result/pallas_call | solution.py:522
  196.7 2.6 %collective-permute-done.35.refs_1_ = bf16[48,1664]{1,0:T(8,128)(2,1)S(1)} collective-permute-done((bf16[48,1664]{1,0:T(8,128)(2,1)S(1)}, bf16[48,1664]{1,0:T(8,128)(2,1)S(1)}, u32[]{:S(2)}, u32[]{:S(2)}) %collective-permute-start.35) | collective-permute-done | bytes 159776 | tf_op jit(solution)/shard_map/ppermute | solution.py:552
  (199 shorter events, 68.6 us)
Async XLA Ops:
  0.7 18.0 %collective-permute-start = (bf16[16,768]{1,0:T(8,128)(2,1)}, bf16[16,768]{1,0:T(8,128)(2,1)S(1)}, u32[]{:S(2)}, u32[]{:S(2)}) collective-permute-start(bf16[16,768]{1,0:T(8,128)(2,1)} %latents.5), channel_id=1, source_target_pairs={{0,4},{1,5},{2,6},{3,7},{4,0},{5,1},{6,2},{7,3},{8,12},{9,13},{10,... | collective-permute-start | bytes 73736 | tf_op jit(solution)/shard_map/ppermute | solution.py:552
  3.7 14.9 %collective-permute-start.1 = (bf16[16,768]{1,0:T(8,128)(2,1)}, bf16[16,768]{1,0:T(8,128)(2,1)S(1)}, u32[]{:S(2)}, u32[]{:S(2)}) collective-permute-start(bf16[16,768]{1,0:T(8,128)(2,1)} %latents.5), channel_id=1, source_target_pairs={{0,8},{1,9},{2,10},{3,11},{4,12},{5,13},{6,14},{7,15},{8,0},{9,1},... | collective-permute-start | bytes 73736 | tf_op jit(solution)/shard_map/ppermute | solution.py:552
  6.3 12.3 %collective-permute-start.2 = (bf16[16,768]{1,0:T(8,128)(2,1)}, bf16[16,768]{1,0:T(8,128)(2,1)S(1)}, u32[]{:S(2)}, u32[]{:S(2)}) collective-permute-start(bf16[16,768]{1,0:T(8,128)(2,1)} %latents.5), channel_id=1, source_target_pairs={{0,12},{1,13},{2,14},{3,15},{4,8},{5,9},{6,10},{7,11},{8,4},{9,5},... | collective-permute-start | bytes 73736 | tf_op jit(solution)/shard_map/ppermute | solution.py:552
  37.0 12.1 %collective-permute-start.7 = (bf16[256,768]{1,0:T(8,128)(2,1)S(1)}, bf16[256,768]{1,0:T(8,128)(2,1)S(1)}, u32[]{:S(2)}, u32[]{:S(2)}) collective-permute-start(bf16[256,768]{1,0:T(8,128)(2,1)S(1)} %get-tuple-element.161.part_one), channel_id=1, source_target_pairs={{0,16},{16,0},{1,17},{17,1},{2,18},{18,2},{3,19},{19,3},{4,20},{20... | collective-permute-start | bytes 1179656 | tf_op jit(solution)/shard_map/ppermute | solution.py:547
  41.9 13.5 %collective-permute-start.6 = (bf16[256,768]{1,0:T(8,128)(2,1)S(1)}, bf16[256,768]{1,0:T(8,128)(2,1)S(1)}, u32[]{:S(2)}, u32[]{:S(2)}) collective-permute-start(bf16[256,768]{1,0:T(8,128)(2,1)S(1)} %get-tuple-element.160.part_one), channel_id=1, source_target_pairs={{0,16},{16,0},{1,17},{17,1},{2,18},{18,2},{3,19},{19,3},{4,20},{20... | collective-permute-start | bytes 1179656 | tf_op jit(solution)/shard_map/ppermute | solution.py:547
  63.5 15.7 %collective-permute-start.10 = (bf16[8,48,1536]{2,1,0:T(8,128)(2,1)S(1)}, bf16[8,48,1536]{2,1,0:T(8,128)(2,1)S(1)}, u32[]{:S(2)}, u32[]{:S(2)}) collective-permute-start(bf16[8,48,1536]{2,1,0:T(8,128)(2,1)S(1)} %get-tuple-element.174), channel_id=1, source_target_pairs={{0,1},{1,0},{2,3},{3,2},{4,5},{5,4},{6,7},{7,6},{8,9},{9,8},{10,11... | collective-permute-start | bytes 3538952 | tf_op jit(solution)/shard_map/ppermute | solution.py:552
  63.5 11.5 %collective-permute-start.9 = (bf16[256,768]{1,0:T(8,128)(2,1)S(1)}, bf16[256,768]{1,0:T(8,128)(2,1)S(1)}, u32[]{:S(2)}, u32[]{:S(2)}) collective-permute-start(bf16[256,768]{1,0:T(8,128)(2,1)S(1)} %get-tuple-element.169.part_one), channel_id=1, source_target_pairs={{0,16},{16,0},{1,17},{17,1},{2,18},{18,2},{3,19},{19,3},{4,20},{20... | collective-permute-start | bytes 1179656 | tf_op jit(solution)/shard_map/ppermute | solution.py:547
  83.9 18.6 %collective-permute-start.11 = (bf16[8,48,1536]{2,1,0:T(8,128)(2,1)S(1)}, bf16[8,48,1536]{2,1,0:T(8,128)(2,1)S(1)}, u32[]{:S(2)}, u32[]{:S(2)}) collective-permute-start(bf16[8,48,1536]{2,1,0:T(8,128)(2,1)S(1)} %get-tuple-element.189), channel_id=1, source_target_pairs={{0,1},{1,0},{2,3},{3,2},{4,5},{5,4},{6,7},{7,6},{8,9},{9,8},{10,11... | collective-permute-start | bytes 3538952 | tf_op jit(solution)/shard_map/ppermute | solution.py:552
  83.9 31.5 %collective-permute-start.13 = (bf16[4,48,1536]{2,1,0:T(8,128)(2,1)S(1)}, bf16[4,48,1536]{2,1,0:T(8,128)(2,1)S(1)}, u32[]{:S(2)}, u32[]{:S(2)}) collective-permute-start(bf16[4,48,1536]{2,1,0:T(8,128)(2,1)S(1)} %get-tuple-element.183), channel_id=1, source_target_pairs={{0,2},{1,3},{2,0},{3,1},{4,6},{5,7},{6,4},{7,5},{8,10},{9,11},{10,... | collective-permute-start | bytes 1769480 | tf_op jit(solution)/shard_map/ppermute | solution.py:552
  85.6 11.2 %collective-permute-start.8 = (bf16[256,768]{1,0:T(8,128)(2,1)S(1)}, bf16[256,768]{1,0:T(8,128)(2,1)S(1)}, u32[]{:S(2)}, u32[]{:S(2)}) collective-permute-start(bf16[256,768]{1,0:T(8,128)(2,1)S(1)} %get-tuple-element.167.part_one), channel_id=1, source_target_pairs={{0,16},{16,0},{1,17},{17,1},{2,18},{18,2},{3,19},{19,3},{4,20},{20... | collective-permute-start | bytes 1179656 | tf_op jit(solution)/shard_map/ppermute | solution.py:547
  101.0 7.9 %collective-permute-start.12 = (bf16[16,768]{1,0:T(8,128)(2,1)S(1)}, bf16[16,768]{1,0:T(8,128)(2,1)S(1)}, u32[]{:S(2)}, u32[]{:S(2)}) collective-permute-start(bf16[16,768]{1,0:T(8,128)(2,1)S(1)} %get-tuple-element.204.part_one), channel_id=1, source_target_pairs={{0,16},{16,0},{1,17},{17,1},{2,18},{18,2},{3,19},{19,3},{4,20},{20... | collective-permute-start | bytes 73736 | tf_op jit(solution)/shard_map/ppermute | solution.py:547
  124.0 18.1 %collective-permute-start.16 = (bf16[8,48,1664]{2,1,0:T(8,128)(2,1)S(1)}, bf16[8,48,1664]{2,1,0:T(8,128)(2,1)S(1)}, u32[]{:S(2)}, u32[]{:S(2)}) collective-permute-start(bf16[8,48,1664]{2,1,0:T(8,128)(2,1)S(1)} %get-tuple-element.223), channel_id=1, source_target_pairs={{0,1},{1,0},{2,3},{3,2},{4,5},{5,4},{6,7},{7,6},{8,9},{9,8},{10,11... | collective-permute-start | bytes 3833864 | tf_op jit(solution)/shard_map/ppermute | solution.py:552
  124.0 16.2 %collective-permute-start.15 = (bf16[4,48,1536]{2,1,0:T(8,128)(2,1)S(1)}, bf16[4,48,1536]{2,1,0:T(8,128)(2,1)S(1)}, u32[]{:S(2)}, u32[]{:S(2)}) collective-permute-start(bf16[4,48,1536]{2,1,0:T(8,128)(2,1)S(1)} %get-tuple-element.201), channel_id=1, source_target_pairs={{0,2},{1,3},{2,0},{3,1},{4,6},{5,7},{6,4},{7,5},{8,10},{9,11},{10,... | collective-permute-start | bytes 1769480 | tf_op jit(solution)/shard_map/ppermute | solution.py:552
  125.2 5.3 %collective-permute-start.18 = (bf16[16,768]{1,0:T(8,128)(2,1)S(1)}, bf16[16,768]{1,0:T(8,128)(2,1)S(1)}, u32[]{:S(2)}, u32[]{:S(2)}) collective-permute-start(bf16[16,768]{1,0:T(8,128)(2,1)S(1)} %get-tuple-element.206), channel_id=1, source_target_pairs={{0,8},{1,9},{2,10},{3,11},{4,12},{5,13},{6,14},{7,15},{8,0},{9,1},... | collective-permute-start | bytes 73736 | tf_op jit(solution)/shard_map/ppermute | solution.py:552
  128.7 5.6 %collective-permute-start.19 = (bf16[16,768]{1,0:T(8,128)(2,1)S(1)}, bf16[16,768]{1,0:T(8,128)(2,1)S(1)}, u32[]{:S(2)}, u32[]{:S(2)}) collective-permute-start(bf16[16,768]{1,0:T(8,128)(2,1)S(1)} %get-tuple-element.206), channel_id=1, source_target_pairs={{0,12},{1,13},{2,14},{3,15},{4,8},{5,9},{6,10},{7,11},{8,4},{9,5},... | collective-permute-start | bytes 73736 | tf_op jit(solution)/shard_map/ppermute | solution.py:552
  128.9 17.4 %collective-permute-start.23 = (bf16[256,768]{1,0:T(8,128)(2,1)S(1)}, bf16[256,768]{1,0:T(8,128)(2,1)S(1)}, u32[]{:S(2)}, u32[]{:S(2)}) collective-permute-start(bf16[256,768]{1,0:T(8,128)(2,1)S(1)} %get-tuple-element.238.refs_0_), channel_id=1, source_target_pairs={{0,16},{16,0},{1,17},{17,1},{2,18},{18,2},{3,19},{19,3},{4,20},{20... | collective-permute-start | bytes 1179656 | tf_op jit(solution)/shard_map/ppermute | solution.py:547
  130.5 20.0 %collective-permute-start.24 = (bf16[256,768]{1,0:T(8,128)(2,1)S(1)}, bf16[256,768]{1,0:T(8,128)(2,1)S(1)}, u32[]{:S(2)}, u32[]{:S(2)}) collective-permute-start(bf16[256,768]{1,0:T(8,128)(2,1)S(1)} %get-tuple-element.240.refs_3_), channel_id=1, source_target_pairs={{0,16},{16,0},{1,17},{17,1},{2,18},{18,2},{3,19},{19,3},{4,20},{20... | collective-permute-start | bytes 1179656 | tf_op jit(solution)/shard_map/ppermute | solution.py:547
  134.3 11.1 %collective-permute-start.20 = (bf16[64,768]{1,0:T(8,128)(2,1)S(1)}, bf16[64,768]{1,0:T(8,128)(2,1)S(1)}, u32[]{:S(2)}, u32[]{:S(2)}) collective-permute-start(bf16[64,768]{1,0:T(8,128)(2,1)S(1)} %pad_maximum_fusion.1), channel_id=1, source_target_pairs={{0,2},{1,3},{2,0},{3,1},{4,6},{5,7},{6,4},{7,5},{8,10},{9,11},{10,... | collective-permute-start | bytes 294920 | tf_op jit(solution)/shard_map/ppermute | solution.py:552
  144.8 30.1 %collective-permute-start.25 = (bf16[4,48,1664]{2,1,0:T(8,128)(2,1)}, bf16[4,48,1664]{2,1,0:T(8,128)(2,1)S(1)}, u32[]{:S(2)}, u32[]{:S(2)}) collective-permute-start(bf16[4,48,1664]{2,1,0:T(8,128)(2,1)} %get-tuple-element.229), channel_id=1, source_target_pairs={{0,2},{1,3},{2,0},{3,1},{4,6},{5,7},{6,4},{7,5},{8,10},{9,11},{10,... | collective-permute-start | bytes 1916936 | tf_op jit(solution)/shard_map/ppermute | solution.py:552
  145.5 7.2 %collective-permute-start.21 = (bf16[128,768]{1,0:T(8,128)(2,1)S(1)}, bf16[128,768]{1,0:T(8,128)(2,1)S(1)}, u32[]{:S(2)}, u32[]{:S(2)}) collective-permute-start(bf16[128,768]{1,0:T(8,128)(2,1)S(1)} %constant_dynamic-update-slice_fusion.5.mid_one), channel_id=1, source_target_pairs={{0,1},{1,0},{2,3},{3,2},{4,5},{5,4},{6,7},{7,6},{8,9},{9,8},{10,11... | collective-permute-start | bytes 589832 | tf_op jit(solution)/shard_map/ppermute | solution.py:552
  145.5 6.6 %collective-permute-start.26 = (bf16[48,1536]{1,0:T(8,128)(2,1)S(1)}, bf16[48,1536]{1,0:T(8,128)(2,1)S(1)}, u32[]{:S(2)}, u32[]{:S(2)}) collective-permute-start(bf16[48,1536]{1,0:T(8,128)(2,1)S(1)} %get-tuple-element.249), channel_id=1, source_target_pairs={{0,4},{1,5},{2,6},{3,7},{4,0},{5,1},{6,2},{7,3},{8,12},{9,13},{10,... | collective-permute-start | bytes 442376 | tf_op jit(solution)/shard_map/ppermute | solution.py:552
  147.0 15.6 %collective-permute-start.27 = (bf16[48,1536]{1,0:T(8,128)(2,1)}, bf16[48,1536]{1,0:T(8,128)(2,1)}, u32[]{:S(2)}, u32[]{:S(2)}) collective-permute-start(bf16[48,1536]{1,0:T(8,128)(2,1)} %get-tuple-element.250), channel_id=1, source_target_pairs={{0,8},{1,9},{2,10},{3,11},{4,12},{5,13},{6,14},{7,15},{8,0},{9,1},... | collective-permute-start | bytes 442376 | tf_op jit(solution)/shard_map/ppermute | solution.py:552
  151.3 11.9 %collective-permute-start.28 = (bf16[48,1536]{1,0:T(8,128)(2,1)}, bf16[48,1536]{1,0:T(8,128)(2,1)}, u32[]{:S(2)}, u32[]{:S(2)}) collective-permute-start(bf16[48,1536]{1,0:T(8,128)(2,1)} %get-tuple-element.251), channel_id=1, source_target_pairs={{0,12},{1,13},{2,14},{3,15},{4,8},{5,9},{6,10},{7,11},{8,4},{9,5},... | collective-permute-start | bytes 442376 | tf_op jit(solution)/shard_map/ppermute | solution.py:552
  152.1 41.6 %collective-permute-start.32 = (bf16[256,768]{1,0:T(8,128)(2,1)}, bf16[256,768]{1,0:T(8,128)(2,1)}, u32[]{:S(2)}, u32[]{:S(2)}) collective-permute-start(bf16[256,768]{1,0:T(8,128)(2,1)} %get-tuple-element.258.refs_1_), channel_id=1, source_target_pairs={{0,16},{16,0},{1,17},{17,1},{2,18},{18,2},{3,19},{19,3},{4,20},{20... | collective-permute-start | bytes 1179656 | tf_op jit(solution)/shard_map/ppermute | solution.py:547
  153.4 40.3 %collective-permute-start.33 = (bf16[256,768]{1,0:T(8,128)(2,1)}, bf16[256,768]{1,0:T(8,128)(2,1)}, u32[]{:S(2)}, u32[]{:S(2)}) collective-permute-start(bf16[256,768]{1,0:T(8,128)(2,1)} %get-tuple-element.260.refs_4_), channel_id=1, source_target_pairs={{0,16},{16,0},{1,17},{17,1},{2,18},{18,2},{3,19},{19,3},{4,20},{20... | collective-permute-start | bytes 1179656 | tf_op jit(solution)/shard_map/ppermute | solution.py:547
  162.6 9.5 %collective-permute-start.22 = (bf16[32,768]{1,0:T(8,128)(2,1)S(1)}, bf16[32,768]{1,0:T(8,128)(2,1)S(1)}, u32[]{:S(2)}, u32[]{:S(2)}) collective-permute-start(bf16[32,768]{1,0:T(8,128)(2,1)S(1)} %get-tuple-element.235.part_one), channel_id=1, source_target_pairs={{0,16},{16,0},{1,17},{17,1},{2,18},{18,2},{3,19},{19,3},{4,20},{20... | collective-permute-start | bytes 147464 | tf_op jit(solution)/shard_map/ppermute | solution.py:547
  163.2 21.5 %collective-permute-start.29 = (bf16[48,1536]{1,0:T(8,128)(2,1)S(1)}, bf16[48,1536]{1,0:T(8,128)(2,1)S(1)}, u32[]{:S(2)}, u32[]{:S(2)}) collective-permute-start(bf16[48,1536]{1,0:T(8,128)(2,1)S(1)} %copy-done.40), channel_id=1, source_target_pairs={{0,4},{1,5},{2,6},{3,7},{4,0},{5,1},{6,2},{7,3},{8,12},{9,13},{10,... | collective-permute-start | bytes 442376 | tf_op jit(solution)/shard_map/ppermute | solution.py:552
  172.2 13.5 %collective-permute-start.30 = (bf16[48,1536]{1,0:T(8,128)(2,1)S(1)}, bf16[48,1536]{1,0:T(8,128)(2,1)S(1)}, u32[]{:S(2)}, u32[]{:S(2)}) collective-permute-start(bf16[48,1536]{1,0:T(8,128)(2,1)S(1)} %copy-done.38), channel_id=1, source_target_pairs={{0,8},{1,9},{2,10},{3,11},{4,12},{5,13},{6,14},{7,15},{8,0},{9,1},... | collective-permute-start | bytes 442376 | tf_op jit(solution)/shard_map/ppermute | solution.py:552
  175.0 11.8 %collective-permute-start.31 = (bf16[48,1536]{1,0:T(8,128)(2,1)S(1)}, bf16[48,1536]{1,0:T(8,128)(2,1)S(1)}, u32[]{:S(2)}, u32[]{:S(2)}) collective-permute-start(bf16[48,1536]{1,0:T(8,128)(2,1)S(1)} %copy-done.36), channel_id=1, source_target_pairs={{0,12},{1,13},{2,14},{3,15},{4,8},{5,9},{6,10},{7,11},{8,4},{9,5},... | collective-permute-start | bytes 442376 | tf_op jit(solution)/shard_map/ppermute | solution.py:552
  184.7 12.0 %collective-permute-start.34 = (bf16[48,1664]{1,0:T(8,128)(2,1)S(1)}, bf16[48,1664]{1,0:T(8,128)(2,1)S(1)}, u32[]{:S(2)}, u32[]{:S(2)}) collective-permute-start(bf16[48,1664]{1,0:T(8,128)(2,1)S(1)} %get-tuple-element.267), channel_id=1, source_target_pairs={{0,4},{1,5},{2,6},{3,7},{4,0},{5,1},{6,2},{7,3},{8,12},{9,13},{10,... | collective-permute-start | bytes 479240 | tf_op jit(solution)/shard_map/ppermute | solution.py:552
  185.6 13.7 %collective-permute-start.35 = (bf16[48,1664]{1,0:T(8,128)(2,1)S(1)}, bf16[48,1664]{1,0:T(8,128)(2,1)S(1)}, u32[]{:S(2)}, u32[]{:S(2)}) collective-permute-start(bf16[48,1664]{1,0:T(8,128)(2,1)S(1)} %get-tuple-element.268), channel_id=1, source_target_pairs={{0,8},{1,9},{2,10},{3,11},{4,12},{5,13},{6,14},{7,15},{8,0},{9,1},... | collective-permute-start | bytes 479240 | tf_op jit(solution)/shard_map/ppermute | solution.py:552
  186.8 12.5 %collective-permute-start.36 = (bf16[48,1664]{1,0:T(8,128)(2,1)S(1)}, bf16[48,1664]{1,0:T(8,128)(2,1)S(1)}, u32[]{:S(2)}, u32[]{:S(2)}) collective-permute-start(bf16[48,1664]{1,0:T(8,128)(2,1)S(1)} %get-tuple-element.269), channel_id=1, source_target_pairs={{0,12},{1,13},{2,14},{3,15},{4,8},{5,9},{6,10},{7,11},{8,4},{9,5},... | collective-permute-start | bytes 479240 | tf_op jit(solution)/shard_map/ppermute | solution.py:552
  (51 other events, 462.5 us)
where the time goes:
time: 204 us; the launch traced here: 203 us
  Pallas kernels  87.9 us (43%)
  waiting for transfers between devices  52.8 us (26%)
  starting transfers between devices  45.3 us (22%)
  local copies, waits for them, and re-layouts  15.2 us (7%)
    pallas_call x28, Pallas kernels, call(): pl.pallas_call(kernel, out_shape=[pltpu.HBM(entry[0], entry[1]) if KEPT i...  87.9 us
    ppermute x12, waiting for transfers between devices, swap_tp(): return lax.ppermute(values, 'tp', [(0, 1), (1, 0)])  37.3 us
    ppermute x25, starting transfers between devices, flip(): return lax.ppermute(values, 'dp', [(i, i ^ bits) for i in range(size)])  32.4 us
    ppermute x25, waiting for transfers between devices, flip(): return lax.ppermute(values, 'dp', [(i, i ^ bits) for i in range(size)])  15.4 us
    ppermute x12, starting transfers between devices, swap_tp(): return lax.ppermute(values, 'tp', [(0, 1), (1, 0)])  12.9 us
    unnamed x102, local copies, waits for them, and re-layouts  11.5 us
  transfers between devices with their start and end apart: 37, of which 14 were waited for; matrix products, arithmetic and copies ran while one was open for 2% of the time, Pallas kernels for 31%

commit v1 on v0

v1 whole, which is shorter than its diff:
```python
from functools import partial

import jax
import jax.numpy as jnp
from jax import lax
from jax.experimental import pallas as pl
from jax.experimental.pallas import tpu as pltpu
from jax.sharding import PartitionSpec as P

E = 64
S = 256
L = 8
EPSILON = 1e-05
NEGATIVE = -1000000000.0
FACTOR = E ** (-0.5)
LOG2E = 1.4426950408889634
F32 = jnp.float32
B16 = jnp.bfloat16


def nn(left, right):
    return lax.dot_general(left, right, (((1,), (0,)), ((), ())), preferred_element_type=F32)


def nt(left, right):
    return lax.dot_general(left, right, (((1,), (1,)), ((), ())), preferred_element_type=F32)


def tn(left, right):
    return lax.dot_general(left, right, (((0,), (0,)), ((), ())), preferred_element_type=F32)


def norm_parts(values):
    average = jnp.mean(values, axis=-1, keepdims=True)
    centred = values - average
    spread = jnp.mean(centred * centred, axis=-1, keepdims=True)
    rate = lax.rsqrt(spread + EPSILON)
    return centred * rate, rate


def norm_back(grad, unit, rate, gain):
    scaled = grad * gain
    first = jnp.mean(scaled, axis=-1, keepdims=True)
    second = jnp.mean(scaled * unit, axis=-1, keepdims=True)
    return rate * (scaled - first - unit * second)


def gelu_both(values):
    square = values * values
    wave = jnp.tanh(0.7978845608028654 * values * (1.0 + 0.044715 * square))
    slope = 0.7978845608028654 * (1.0 + 0.134145 * square)
    half = 0.5 * (1.0 + wave)
    return values * half, half + 0.5 * values * (1.0 - wave * wave) * slope


def head_mask(heads, rows, width):
    row = lax.broadcasted_iota(jnp.int32, (heads * rows, width), 0)
    column = lax.broadcasted_iota(jnp.int32, (heads * rows, width), 1)
    return (row // rows) == (column // E)


def spread_heads(values, heads):
    rows, width = values.shape
    stacked = jnp.concatenate([values] * heads, axis=0)
    return jnp.where(head_mask(heads, rows, width), stacked, jnp.zeros_like(stacked))


def fold_heads(values, heads):
    rows, width = values.shape[0] // heads, values.shape[1]
    kept = jnp.where(head_mask(heads, rows, width), values, jnp.zeros_like(values))
    total = kept[:rows]
    for h in range(1, heads):
        total = total + kept[h * rows : (h + 1) * rows]
    return total


def half_mask(width):
    return lax.broadcasted_iota(jnp.int32, (1, width), 1) < E


def head_only(values, second):
    mask = half_mask(values.shape[1])
    zero = jnp.zeros_like(values)
    return jnp.where(mask, zero, values) if second else jnp.where(mask, values, zero)


def load_kernel(*refs):
    count = (len(refs) - 1) // 2
    ready = refs[-1]
    copies = [
        pltpu.make_async_copy(refs[i], refs[count + i], ready.at[i]) for i in range(count)
    ]
    for copy in copies:
        copy.start()
    for copy in copies:
        copy.wait()


def join_kernel(*refs):
    at = 0
    for r in refs[:-1]:
        refs[-1][at : at + r.shape[0], :] = r[...]
        at += r.shape[0]


def enter_kernel(g, tokens, gain, wq, wk, wv, saved_out):
    unit, _ = norm_parts(tokens[g * S : (g + 1) * S, :].astype(F32))
    low = (unit * gain[...]).astype(B16)
    width = wq.shape[1]
    saved_out[:, :width] = nn(low, wq[...]).astype(B16)
    saved_out[:, width : 2 * width] = nn(low, wk[...]).astype(B16)
    saved_out[:, 2 * width : 3 * width] = nn(low, wv[...]).astype(B16)
    saved_out[:, 3 * width :] = low


def image_rows(order, groups, me, group_image):
    count = len(order) * groups * L
    lane = lax.broadcasted_iota(jnp.int32, (8, count), 1) // L
    images = jnp.zeros((8, count), F32)
    for j, bits in enumerate(order):
        for g in range(groups):
            image = group_image[(me ^ bits) * groups + g].astype(F32)
            images = jnp.where(lane == j * groups + g, image, images)
    return images[:1], images.T[:, :1]


def latent_kernel(
    heads, own, order, me, group_image, one, two, gain, wq, wk, wv, wo, latents_out, q_out, k_out, v_out, part_out
):
    latents = jnp.concatenate([one[...], two[...]], axis=0)
    latents_out[...] = latents
    unit, _ = norm_parts(latents.astype(F32))
    low = (unit * gain[...]).astype(B16)
    q = nn(low, wq[...]).astype(B16)
    k = nn(low, wk[...]).astype(B16)
    v = nn(low, wv[...]).astype(B16)
    q_out[...] = q
    k_out[...] = k
    v_out[...] = v
    scores = nt(spread_heads(q[:own], heads), k) * FACTOR
    images, column = image_rows(order, own // L, me[0], group_image)
    member = jnp.concatenate([column[:own]] * heads, axis=0) == images
    scores = jnp.where(member, scores, NEGATIVE)
    weights = jnp.exp(scores - jnp.max(scores, axis=-1, keepdims=True))
    probs = weights / jnp.sum(weights, axis=-1, keepdims=True)
    mixed = fold_heads(nn(probs.astype(B16), v), heads).astype(B16)
    part_out[...] = nn(mixed, wo[...]).astype(B16)


def pair_of(saved, pair, width):
    start = pair * 2 * E
    return [saved[:, i * width + start : i * width + start + 2 * E] for i in range(3)]


def attend_kernel(
    g, heads, saved, latents, part_one, part_two, gain, wk, wv,
    o_out, probs_out, side_out, mid_out, mid_low_out,
):
    mid = latents[...].astype(F32) + (part_one[...].astype(F32) + part_two[...].astype(F32))
    mid_out[...] = mid
    mid_low_out[...] = mid.astype(B16)
    unit, _ = norm_parts(mid[g * L : (g + 1) * L])
    side_low = (unit * gain[...]).astype(B16)
    side_k = nn(side_low, wk[...]).astype(B16).astype(F32)
    side_v = nn(side_low, wv[...]).astype(B16).astype(F32)
    width = side_k.shape[1]
    side_out[:, :width] = side_k
    side_out[:, width : 2 * width] = side_v
    side_out[:, 2 * width :] = side_low.astype(F32)
    side_v = spread_heads(side_v, heads).astype(B16)
    side_scores = nt(spread_heads(side_k, heads).astype(B16), saved[:, :width])
    scale = FACTOR * LOG2E
    outs, side_probs, lses = [], [], []
    for pair in range(heads // 2):
        q_pair, k_pair, v_pair = pair_of(saved, pair, width)
        for second in (0, 1):
            h = 2 * pair + second
            scores = nt(head_only(k_pair, second), q_pair)
            side = side_scores[h * L : (h + 1) * L]
            top = jnp.maximum(
                jnp.max(scores, axis=0, keepdims=True), jnp.max(side, axis=0, keepdims=True)
            )
            weights = jnp.exp2((scores - top) * scale)
            side = jnp.exp2((side - top) * scale)
            total = jnp.sum(weights, axis=0, keepdims=True) + jnp.sum(side, axis=0, keepdims=True)
            inverse = 1.0 / total
            side_probs.append(side * inverse)
            lses.append(top * scale + jnp.log2(total))
            outs.append(tn((weights * inverse).astype(B16), v_pair))
    side_probs = jnp.concatenate(side_probs, axis=0)
    probs_out[: heads * L, :] = side_probs
    probs_out[heads * L :, :] = jnp.concatenate(
        lses + [jnp.zeros_like(lses[0])] * (8 - heads), axis=0
    )
    side_o = tn(side_probs.astype(B16), side_v)
    first = half_mask(2 * E)
    token_o = jnp.concatenate(
        [jnp.where(first, outs[2 * i], outs[2 * i + 1]) for i in range(heads // 2)], axis=1
    )
    o_out[...] = (token_o + side_o).astype(B16)


def feed_kernel(
    g, chunk, extra, place, tokens, o, o_two, wo, wo_two, cotangent, gain, up, up_bias, down, *rest
):
    earlier, outs = rest[:extra], rest[extra:]
    part_outs, outs = outs[:-7], outs[-7:]
    active_out, hidden_grad_out, low_out, middle_out, down_part_out, up_bias_out, down_bias_out = outs
    rows = slice(g * S, (g + 1) * S)
    first = place[0] == 0
    o_first = jnp.where(first, o[...], o_two[...])
    o_second = jnp.where(first, o_two[...], o[...])
    wo_first = jnp.where(first, wo[...], wo_two[...])
    wo_second = jnp.where(first, wo_two[...], wo[...])
    middle = tokens[rows, :].astype(F32) + (nn(o_first, wo_first) + nn(o_second, wo_second))
    middle_out[...] = middle
    unit, _ = norm_parts(middle)
    low = (unit * gain[...]).astype(B16)
    low_out[...] = low
    outer = cotangent[rows, :]
    down_bias_out[...] = jnp.sum(outer.astype(F32), axis=0, keepdims=True)
    part, down_part = None, None
    for start in range(0, up.shape[1], chunk):
        cut = slice(start, start + chunk)
        hidden = nn(low, up[:, cut]) + up_bias[:, cut]
        active, slope = gelu_both(hidden)
        active = active.astype(B16)
        active_out[:, cut] = active
        grad = (slope * nt(outer, down[cut, :])).astype(B16)
        hidden_grad_out[:, cut] = grad
        up_bias_out[:, cut] = jnp.sum(grad.astype(F32), axis=0, keepdims=True)
        one = nt(grad, up[:, cut])
        two = nn(active, down[cut, :])
        part = one if part is None else part + one
        down_part = two if down_part is None else down_part + two
    at = 0
    for out in part_outs:
        out[...] = part[at : at + out.shape[0]].astype(B16)
        at += out.shape[0]
    for i, r in enumerate(earlier):
        down_part_out[i * S : (i + 1) * S, :] = r[...]
    down_part_out[len(earlier) * S :, :] = down_part.astype(B16)


def turn_kernel(
    g, heads, cuts, cotangent, middle, gain, wo, wk, wv, o, saved, probs, side, mid, *rest
):
    parts, rest = rest[: 2 * cuts], rest[2 * cuts :]
    earlier, outs = rest[:g], rest[g:]
    o_grad_out, delta_out, side_score_grad_out, part_out, grads_out, gain_out = outs[:6]
    middle_grad_out, middle_low_out = outs[6:]
    unit, rate = norm_parts(middle[...])
    sides = [jnp.concatenate([r[...] for r in rs], axis=0) for rs in (parts[:cuts], parts[cuts:])]
    grad = sides[0].astype(F32) + sides[1].astype(F32)
    gain_out[0:1, :] = jnp.sum(grad * unit, axis=0, keepdims=True)
    outer = cotangent[g * S : (g + 1) * S, :].astype(F32)
    middle_grad = outer + norm_back(grad, unit, rate, gain[...])
    middle_grad_out[...] = middle_grad
    middle_low = middle_grad.astype(B16)
    middle_low_out[...] = middle_low
    o_grad = nt(middle_low, wo[...]).astype(B16)
    o_grad_out[...] = o_grad
    width = o_grad.shape[1]
    rows8 = lax.broadcasted_iota(jnp.int32, (8, width), 0)
    columns8 = lax.broadcasted_iota(jnp.int32, (8, width), 1) // E
    pick = (rows8 == columns8).astype(B16)
    weighted = o_grad.astype(F32) * o[...].astype(F32)
    high = weighted.astype(B16)
    low = (weighted - high.astype(F32)).astype(B16)
    delta = nt(pick, high) + nt(pick, low)
    delta_out[...] = delta
    side_v = spread_heads(side[:, width : 2 * width], heads).astype(B16)
    side_prob_grad = nt(side_v, o_grad)
    side_probs = probs[: heads * L, :]
    wide = jnp.concatenate(
        [jnp.broadcast_to(delta[h : h + 1], (L, delta.shape[1])) for h in range(heads)], axis=0
    )
    score_grad = (side_probs * (side_prob_grad - wide)).astype(B16)
    side_score_grad_out[...] = score_grad
    k_grad = (fold_heads(nn(score_grad, saved[:, :width]), heads) * FACTOR).astype(B16)
    v_grad = fold_heads(nn(side_probs.astype(B16), o_grad), heads).astype(B16)
    grads_out[:, :width] = k_grad.astype(F32)
    grads_out[:, width:] = v_grad.astype(F32)
    part = nt(k_grad, wk[...]) + nt(v_grad, wv[...])
    side_unit, _ = norm_parts(mid[g * L : (g + 1) * L, :])
    gain_out[1:2, :] = jnp.sum(part * side_unit, axis=0, keepdims=True)
    gain_out[2:, :] = jnp.zeros_like(gain_out[2:, :])
    part = jnp.concatenate([r[...] for r in earlier] + [part], axis=0)
    part_out[...] = part.astype(part_out.dtype)


def side_kernel(part_one, part_two, mid, cotangent, gain, low_out, grad_out):
    unit, rate = norm_parts(mid[...])
    part = part_one[...].astype(F32) + part_two[...].astype(F32)
    grad = cotangent[...].astype(F32) + norm_back(part, unit, rate, gain[...])
    grad_out[...] = grad
    low_out[...] = grad.astype(B16)


def attend_back_kernel(
    g, heads, tokens, saved, o_grad, probs, delta, side_score_grad, side, wq, wk, wv, *rest
):
    part_out, grads_out, gain_out = rest[-3:]
    gains, earlier = rest[: min(g, 1) + 1], rest[min(g, 1) + 1 : -3]
    scale = FACTOR * LOG2E
    first = half_mask(2 * E)
    width = o_grad.shape[1]
    side_k = spread_heads(side[:, :width], heads).astype(B16)
    side_q_grad = tn(side_score_grad[...], side_k)
    at = heads * L
    for pair in range(heads // 2):
        start = pair * 2 * E
        cut = slice(start, start + 2 * E)
        q_pair, k_pair, v_pair = pair_of(saved, pair, width)
        grad_pair = o_grad[:, cut]
        q_grads, k_grads, v_grads = [], [], []
        for second in (0, 1):
            h = 2 * pair + second
            scores = nt(head_only(k_pair, second), q_pair)
            weights = jnp.exp2(scores * scale - probs[at + h : at + h + 1, :])
            prob_grad = nt(head_only(v_pair, second), grad_pair)
            score_grad = (weights * (prob_grad - delta[h : h + 1, :])).astype(B16)
            v_grads.append(nn(weights.astype(B16), grad_pair))
            k_grads.append(nn(score_grad, q_pair))
            q_grads.append(tn(score_grad, k_pair))
        q_pair_grad = jnp.where(first, q_grads[0], q_grads[1]) + side_q_grad[:, cut]
        k_pair_grad = jnp.where(first, k_grads[0], k_grads[1])
        v_pair_grad = jnp.where(first, v_grads[0], v_grads[1])
        grads_out[:, start : start + 2 * E] = (q_pair_grad * FACTOR).astype(B16)
        grads_out[:, width + start : width + start + 2 * E] = (k_pair_grad * FACTOR).astype(B16)
        grads_out[:, 2 * width + start : 2 * width + start + 2 * E] = v_pair_grad.astype(B16)
    part = nt(grads_out[:, :width], wq[...]) + nt(grads_out[:, width : 2 * width], wk[...])
    part = part + nt(grads_out[:, 2 * width :], wv[...])
    for i, r in enumerate(earlier):
        part_out[i * S : (i + 1) * S, :] = r[...]
    part_out[len(earlier) * S :, :] = part.astype(B16)
    unit, _ = norm_parts(tokens[g * S : (g + 1) * S, :].astype(F32))
    total = gains[0][1:2, :] + jnp.sum(part * unit, axis=0, keepdims=True)
    for r in gains[1:]:
        total = total + r[...]
    gain_out[...] = total


def leave_kernel(tokens, gain, part_one, part_two, *refs):
    middle_grad, grad_out = refs[:-1], refs[-1]
    for g in range(len(middle_grad)):
        rows = slice(g * S, (g + 1) * S)
        unit, rate = norm_parts(tokens[rows, :].astype(F32))
        grad = part_one[rows, :].astype(F32) + part_two[rows, :].astype(F32)
        grad_out[rows, :] = middle_grad[g][...] + norm_back(grad, unit, rate, gain[...])


def result_kernel(bias, part_one, part_two, *refs):
    middle, out = refs[:-1], refs[-1]
    for g in range(len(middle)):
        rows = slice(g * S, (g + 1) * S)
        total = part_one[rows, :].astype(F32) + part_two[rows, :].astype(F32)
        out[rows, :] = (middle[g][...] + total + bias[...]).astype(B16)


def latent_leave_kernel(me, latents, part_one, part_two, gain, mid_grad, grad_out, gain_out):
    own = latents.shape[0]
    unit, rate = norm_parts(latents[...].astype(F32))
    total = part_one[...].astype(F32) + part_two[...].astype(F32)
    grad_out[...] = mid_grad[...] + norm_back(total[:own], unit, rate, gain[...])
    share, model = gain_out.shape[1], gain.shape[1]
    row = lax.broadcasted_iota(jnp.int32, (share, model), 0)
    column = lax.broadcasted_iota(jnp.int32, (share, model), 1)
    kept = jnp.where(column == row + me[0] * share, total[own : own + 1], 0.0)
    gain_out[...] = jnp.broadcast_to(jnp.sum(kept, axis=1, keepdims=True), (share, 8)).T


def split_pairs(values, bit, share, send_out, keep_out, cut, keep_cut=None):
    blocks = values.reshape(values.shape[0] // (2 * share), 2, share, values.shape[1])
    even, odd = blocks[:, 0], blocks[:, 1]
    send_out[:, :, cut] = jnp.where(bit == 0, odd, even).astype(B16)
    keep_cut = cut if keep_cut is None else keep_cut
    keep_out[:, :, keep_cut] = jnp.where(bit == 0, even, odd).astype(B16)


def weight_grad_kernel(groups, share, down_pieces, up_pieces, me, cotangent, *refs):
    active, low, hidden_grad = (refs[i * groups : (i + 1) * groups] for i in range(3))
    outs = refs[3 * groups :]
    down_sends, up_sends = outs[:down_pieces], outs[down_pieces:-2]
    down_keep, up_keep = outs[-2:]
    bit = me[0] % 2
    width = active[0].shape[1]
    flat = [cotangent[g * S : (g + 1) * S, :].T for g in range(groups)]
    low_flat = [r[...].T for r in low]

    def total_of(lefts, rights, cut):
        total = nn(lefts[0], rights[0][:, cut])
        for g in range(1, groups):
            total = total + nn(lefts[g], rights[g][:, cut])
        return total

    chunk = width // down_pieces
    for k in range(down_pieces):
        cut = slice(k * chunk, (k + 1) * chunk)
        total = total_of(flat, active, cut)
        split_pairs(total, bit, share, down_sends[k], down_keep, slice(0, chunk), cut)
    chunk = width // up_pieces
    for k in range(up_pieces):
        cut = slice(k * chunk, (k + 1) * chunk)
        total = total_of(low_flat, hidden_grad, cut)
        split_pairs(total, bit, share, up_sends[k], up_keep, slice(0, chunk), cut)


def attention_grad_kernel(groups, share, me, gain_one, gain_two, *refs):
    saved, grads, middle_low, o, side, side_grads, up_bias, down_bias, gains = (
        refs[i * groups : (i + 1) * groups] for i in range(9)
    )
    *send_outs, keep_out = refs[9 * groups :]
    bit = me[0] % 2
    width = o[0].shape[1]
    model = middle_low[0].shape[1]
    stack = [jnp.concatenate([r[...] for r in rs], axis=0) for rs in (side, side_grads)]
    side_low = stack[0][:, 2 * width :].astype(B16)
    side_k, side_v = stack[1][:, :width].astype(B16), stack[1][:, width:].astype(B16)
    flat = [r[:, 3 * width :].T for r in saved]
    low_flat = [r[...].T for r in middle_low]

    def total_of(lefts, rights, cut):
        total = nn(lefts[0], rights[0][:, cut])
        for g in range(1, groups):
            total = total + nn(lefts[g], rights[g][:, cut])
        return total

    def cut_of(i):
        return slice(i * width, (i + 1) * width)

    totals = (
        total_of(flat, grads, cut_of(0)),
        total_of(flat, grads, cut_of(1)) + tn(side_low, side_k),
        total_of(flat, grads, cut_of(2)) + tn(side_low, side_v),
        total_of(low_flat, o, cut_of(0)),
    )
    for i, total in enumerate(totals):
        split_pairs(total, bit, share, send_outs[i], keep_out, cut_of(0), cut_of(i))

    def column(rows):
        return jnp.broadcast_to(rows, (8, rows.shape[1])).T

    def sum_of(parts):
        total = parts[0]
        for part in parts[1:]:
            total = total + part
        return total

    columns = [
        column(sum_of([r[...] for r in down_bias])),
        column(sum_of([r[0:1, :] for r in gains])),
        column(gain_one[...] + gain_two[...]),
    ]
    bias = column(sum_of([r[...] for r in up_bias]))
    times = bias.shape[0] // model
    bias = bias.reshape(model // share, times, share, 8)
    columns += [bias[:, i].reshape(model, 8) for i in range(times)]
    lane = lax.broadcasted_iota(jnp.int32, (model, 128), 1)
    block = jnp.zeros((model, 128), F32)
    for i, one in enumerate(columns):
        block = jnp.where(lane == i, one[:, 0:1], block)
    cut = slice(width, width + 128)
    split_pairs(block, bit, share, send_outs[3], keep_out, cut, slice(4 * width, 4 * width + 128))


def halve_kernel(shift, pieces, cuts, me, keep, *refs):
    gots, outs = refs[: len(pieces)], refs[len(pieces) :]
    bit = (me[0] // shift) % 2
    for got, (first, last) in zip(gots, pieces):
        for k, (start, end) in enumerate(cuts):
            low, high = max(first, start), min(last, end)
            if low >= high:
                continue
            of_got, of_out = slice(low - first, high - first), slice(low - start, high - start)
            for i in range(keep.shape[0]):
                there, here = (
                    keep[i, pl.ds(at, 1), :, low:high].astype(F32)
                    + got[i, pl.ds(at, 1), :, of_got].astype(F32)
                    for at in (1 - bit, bit)
                )
                outs[2 * k][pl.ds(i, 1), :, of_out] = there.astype(B16)
                outs[2 * k + 1][pl.ds(i, 1), :, of_out] = here


def finish_kernel(cuts, keep, got, *outs):
    total = keep[0] + got[0].astype(F32)
    for out, (start, end, flat) in zip(outs, cuts):
        part = total[:, start:end]
        out[...] = part.T[: out.shape[0]] if flat else part


def latent_back_kernel(
    heads, own, order, block, me, group_image, latents, q, k, v, mid_one, mid_two, gain, wq, wk, wv, wo,
    part_out, wq_out, wk_out, wv_out, wo_out, mixed, q_grad, k_grad, v_grad, images,
):
    mid_low = jnp.concatenate([mid_one[...], mid_two[...]], axis=0)
    o_grad = nt(mid_low, wo[...]).astype(B16)
    unit, _ = norm_parts(latents[...].astype(F32))
    low = (unit * gain[...]).astype(B16)
    everyone = low.shape[0]
    images_row, images_column = image_rows(order, own // L, me[0], group_image)

    def rows_of(start, ref_q, ref_grad, ref_images):
        wide_q = spread_heads(ref_q, heads)
        wide_grad = spread_heads(ref_grad, heads)
        scores = nt(wide_q, k[...]) * FACTOR
        member = jnp.concatenate([ref_images] * heads, axis=0) == images_row
        scores = jnp.where(member, scores, NEGATIVE)
        weights = jnp.exp(scores - jnp.max(scores, axis=-1, keepdims=True))
        probs = weights / jnp.sum(weights, axis=-1, keepdims=True)
        probs_low = probs.astype(B16)
        prob_grad = nt(wide_grad, v[...])
        delta = jnp.sum(prob_grad * probs, axis=-1, keepdims=True)
        score_grad = (probs * (prob_grad - delta)).astype(B16)
        mixed[pl.ds(start, block), :] = fold_heads(nn(probs_low, v[...]), heads).astype(B16)
        q_grad[pl.ds(start, block), :] = (
            fold_heads(nn(score_grad, k[...]), heads) * FACTOR
        ).astype(B16)
        return tn(score_grad, wide_q), tn(probs_low, wide_grad)

    if block == everyone:
        k_sum, v_sum = rows_of(0, q[...], o_grad, images_column)
        k_sum, v_sum = k_sum * FACTOR, v_sum
    else:
        v_grad[...] = o_grad
        images[...] = jnp.broadcast_to(images_column, images.shape)

        def step(i, held):
            start = pl.multiple_of(i * block, block)
            here = pl.ds(start, block)
            one, two = rows_of(start, q[here, :], v_grad[here, :], images[here, :][:, :1])
            return held[0] + one, held[1] + two

        zero = jnp.zeros(k.shape, F32)
        k_sum, v_sum = lax.fori_loop(0, everyone // block, step, (zero, zero))
        k_sum = k_sum * FACTOR
    k_grad[...] = k_sum.astype(B16)
    v_grad[...] = v_sum.astype(B16)
    part = nt(q_grad[...], wq[...]) + nt(k_grad[...], wk[...]) + nt(v_grad[...], wv[...])
    gain_part = jnp.sum(part * unit, axis=0, keepdims=True)
    part_out[...] = jnp.concatenate(
        [part[:own], jnp.broadcast_to(gain_part, (16, part.shape[1]))], axis=0
    ).astype(B16)
    share = wq_out.shape[0]
    model = low.shape[1]
    row = lax.broadcasted_iota(jnp.int32, (share, model), 0)
    column = lax.broadcasted_iota(jnp.int32, (share, model), 1)
    pick = (column == row + me[0] * share).astype(B16)
    columns = nt(pick, low).astype(B16)
    wq_out[...] = nn(columns, q_grad[...])
    wk_out[...] = nn(columns, k_grad[...])
    wv_out[...] = nn(columns, v_grad[...])
    wo_out[...] = nn(nt(pick, mid_low).astype(B16), mixed[...])


MIB = 1024 * 1024
OUT = "out"


class Order:
    def __init__(self, pinned):
        self.pinned, self.last = pinned, None

    def call(self, kernel, name, outs, ins, scratch=(), limit=16, behind=()):
        scalars = [isinstance(a, tuple) for a in ins]
        arrays = [a[1] if isinstance(a, tuple) else a for a in ins]
        earlier = tuple(behind) + (() if self.last is None else (self.last,))
        if earlier:
            least = min(range(len(arrays)), key=lambda i: arrays[i].size)
            arrays[least] = after(arrays[least], *earlier)
        if self.pinned:
            arrays = [
                a if scalar else pltpu.with_memory_space_constraint(a, pltpu.VMEM)
                for a, scalar in zip(arrays, scalars)
            ]

        def result(shape, dtype, kind=None):
            if self.pinned and kind != OUT:
                return pltpu.VMEM(shape, dtype)
            return jax.ShapeDtypeStruct(shape, dtype)

        def whole(shape):
            return pl.BlockSpec(tuple(shape), lambda: (0,) * len(shape))

        results = pl.pallas_call(
            kernel,
            out_shape=[result(*out) for out in outs],
            in_specs=[
                pl.BlockSpec(memory_space=pltpu.SMEM) if scalar else whole(a.shape)
                for a, scalar in zip(arrays, scalars)
            ],
            out_specs=[whole(out[0]) for out in outs],
            scratch_shapes=list(scratch),
            compiler_params=pltpu.CompilerParams(vmem_limit_bytes=limit * MIB),
            cost_estimate=pl.CostEstimate(flops=0, bytes_accessed=0, transcendentals=0),
            name=name,
        )(*arrays)
        self.last = min(results, key=lambda a: a.size)
        return results

    def load(self, *arrays, behind=()):
        if not self.pinned:
            return arrays
        sources = list(arrays)
        earlier = tuple(behind) + (() if self.last is None else (self.last,))
        if earlier:
            sources[0] = after(sources[0], *earlier)
        results = pl.pallas_call(
            load_kernel,
            out_shape=[pltpu.VMEM(a.shape, a.dtype) for a in arrays],
            in_specs=[pl.BlockSpec(memory_space=pltpu.HBM)] * len(arrays),
            out_specs=[pl.BlockSpec(memory_space=pltpu.VMEM)] * len(arrays),
            scratch_shapes=[pltpu.SemaphoreType.DMA((len(arrays),))],
            compiler_params=pltpu.CompilerParams(vmem_limit_bytes=MIB),
            cost_estimate=pl.CostEstimate(flops=0, bytes_accessed=0, transcendentals=0),
            name="load",
        )(*[pltpu.with_memory_space_constraint(a, pltpu.HBM) for a in sources])
        self.last = min(results, key=lambda a: a.size)
        return results


def after(value, *earlier):
    return lax.optimization_barrier((value, earlier))[0]


def swap_tp(values, name):
    with jax.named_scope("swap_" + name):
        return lax.ppermute(values, "tp", [(0, 1), (1, 0)])


def flip(values, bits, name):
    size = lax.axis_size("dp")
    with jax.named_scope("flip_" + name):
        return lax.ppermute(values, "dp", [(i, i ^ bits) for i in range(size)])


def gather_steps(size):
    width, steps = 2, []
    while width * 4 < size:
        steps.append([width])
        width *= 2
    if width < size:
        steps.append([width * k for k in range(1, size // width)])
    steps.reverse()
    return steps + [[1]]


def gather_order(size):
    order = [0]
    for step in gather_steps(size):
        order = order + [i ^ bits for bits in [0] + step for i in order][len(order) :]
    return order


def scatter_sum(grads):
    size = lax.axis_size("dp")
    me = lax.axis_index("dp")
    width = 1
    while width * 4 < size:
        bit = (me // width) % 2
        pairs = grads.reshape((grads.shape[0] // 2, 2) + grads.shape[1:])
        send = lax.dynamic_index_in_dim(pairs, 1 - bit, 1, keepdims=False)
        keep = lax.dynamic_index_in_dim(pairs, bit, 1, keepdims=False)
        got = flip(send.astype(B16), width, "sums")
        grads = keep.astype(F32) + got.astype(F32)
        width *= 2
    place = me // width
    total = lax.dynamic_index_in_dim(grads, place, 0, keepdims=False)
    for k in range(1, size // width):
        send = lax.dynamic_index_in_dim(grads, place ^ k, 0, keepdims=False)
        total = total + flip(send.astype(B16), width * k, "sums").astype(F32)
    return total


class Scatter:
    def __init__(self, order, me, width, keep, send, name):
        self.order, self.me, self.width, self.name = order, me, width, name
        sends = send if isinstance(send, list) else [send]
        self.keep, self.gots, self.pieces, at = keep, [flip(a, width, name) for a in sends], [], 0
        for a in sends:
            self.pieces.append((at, at + a.shape[2]))
            at += a.shape[2]

    def halve(self, cuts, behind=()):
        n, share, _ = self.keep.shape
        four = (n // 2, 2) + self.keep.shape[1:]
        shapes = [(n // 2, share, end - start) for start, end in cuts]
        results = self.order.call(
            partial(halve_kernel, 2 * self.width, self.pieces, cuts),
            "halve",
            [out for shape in shapes for out in ((shape, B16), (shape, F32))],
            [("smem", self.me), self.keep.reshape(four)]
            + [a.reshape((n // 2, 2) + a.shape[1:]) for a in self.gots],
            behind=behind,
        )
        return results[::2], results[1::2]

    def next(self, send, keep, name, *ties):
        send = after(send, *ties) if ties else send
        return Scatter(self.order, self.me, 2 * self.width, keep, send, name)

    def whole(self):
        return [(0, self.keep.shape[2])]

    def finish(self, cuts):
        share = self.keep.shape[1]
        shapes = [(8, share) if flat else (share, e - s) for s, e, flat in cuts]
        return self.order.call(
            partial(finish_kernel, cuts),
            "finish",
            [(shape, F32, OUT) for shape in shapes],
            [self.keep, self.gots[0]],
        )


def local(
    tokens,
    latents,
    latent_query,
    latent_key,
    latent_value,
    latent_output,
    query_weight,
    key_weight,
    value_weight,
    output_weight,
    up_weight,
    up_bias,
    down_weight,
    down_bias,
    latent_gain,
    attention_gain,
    feed_gain,
    group_image,
    token_cotangent,
    latent_cotangent,
):
    size = lax.axis_size("dp")
    me = lax.axis_index("dp")
    me_row = me.reshape(1)
    place = lax.axis_index("tp").reshape(1)
    width = latent_query.shape[1]
    heads = width // E
    rows, model = tokens.shape
    hidden_units = up_weight.shape[1]
    groups = rows // S
    own = latents.shape[0]
    everyone = own * size
    share = model // size
    small = everyone <= 512
    aligned = share % 16 == 0 and size >= 8
    each = range(groups)
    latent_gain_row = latent_gain.reshape(1, model)
    attention_gain_row = attention_gain.reshape(1, model)
    feed_gain_row = feed_gain.reshape(1, model)
    up_bias_row = up_bias.reshape(1, hidden_units)
    down_bias_row = down_bias.reshape(1, model)
    chain = Order(small)
    call = chain.call
    latent_limit = 16 if small else 56

    def join(parts):
        if not small:
            return jnp.concatenate(parts, axis=0)
        shape = (sum(p.shape[0] for p in parts), model)
        return call(join_kernel, "join", [(shape, B16)], parts)[0]

    output_weight_two = swap_tp(output_weight, "output_weight")
    gathered = gather_steps(size)
    scalars = (me_row, place)
    gain_rows = (latent_gain_row, attention_gain_row, feed_gain_row, up_bias_row, down_bias_row)
    gathering = latents
    (
        tokens,
        query_weight,
        key_weight,
        value_weight,
        latents,
        latent_cotangent,
        output_weight,
        *latent_weights,
    ) = chain.load(
        tokens,
        query_weight,
        key_weight,
        value_weight,
        latents,
        latent_cotangent,
        output_weight,
        latent_query,
        latent_key,
        latent_value,
        latent_output,
        behind=scalars + gain_rows,
    )
    held = gathering
    held_steps = []
    for step in gathered[:-1]:
        held = join([held] + [flip(held, b, "latents") for b in step])
        held_steps.append(held)
    turns = tuple(gather_order(size))
    saved = []
    for g in each:
        saved += call(
            partial(enter_kernel, g),
            "enter",
            [((S, 3 * width + model), B16)],
            [tokens, attention_gain_row, query_weight, key_weight, value_weight],
            behind=held_steps[:1] if g == groups - 1 else (),
        )
    latents_one, latents_two = held, flip(after(held, saved[0]), 1, "latents")
    latents_all, lat_q, lat_k, lat_v, latent_part = call(
        partial(latent_kernel, heads, own, turns),
        "latent",
        [((everyone, model), B16)] + [((everyone, width), B16)] * 3 + [((own, model), B16)],
        [
            ("smem", me_row),
            ("smem", group_image),
            latents_one,
            latents_two,
            latent_gain_row,
            *latent_weights,
        ],
        limit=latent_limit,
    )
    latent_part_two = swap_tp(latent_part, "latent_part")
    up_weight, down_weight, token_cotangent = chain.load(up_weight, down_weight, token_cotangent)
    o, probs, side, mids, mid_lows = zip(
        *(
            call(
                partial(attend_kernel, g, heads),
                "attend",
                [
                    ((S, width), B16),
                    ((heads * L + 8, S), F32),
                    ((L, 2 * width + model), F32),
                    ((own, model), F32),
                    ((own, model), B16, OUT),
                ],
                [
                    saved[g],
                    latents,
                    latent_part,
                    latent_part_two,
                    attention_gain_row,
                    key_weight,
                    value_weight,
                ],
            )
            for g in each
        )
    )
    mid, mixed_latents = mids[0], mid_lows[0]
    o_two = [swap_tp(a, "o") for a in o]
    fed = []
    cuts_of = [1 if g == groups - 1 else 2 for g in each]
    for g in each:
        last = g == groups - 1
        fed.append(
            call(
                partial(feed_kernel, g, hidden_units // 3, g if last else 0),
                "feed",
                [((S // cuts_of[g], model), B16)] * cuts_of[g]
                + [
                    ((S, hidden_units), B16),
                    ((S, hidden_units), B16),
                    ((S, model), B16),
                    ((S, model), F32),
                    ((rows if last else S, model), B16),
                    ((1, hidden_units), F32),
                    ((1, model), F32),
                ],
                [
                    ("smem", place),
                    tokens,
                    o[g],
                    o_two[g],
                    output_weight,
                    output_weight_two,
                    token_cotangent,
                    feed_gain_row,
                    up_weight,
                    up_bias_row,
                    down_weight,
                ]
                + ([f[-3] for f in fed] if last else []),
            )
        )
    feed_part = [f[:-7] for f in fed]
    active, hidden_grad, feed_low, middle, down_parts, up_bias_sum, down_bias_sum = zip(
        *(f[-7:] for f in fed)
    )
    down_part = down_parts[-1]
    feed_part_two = [[swap_tp(p, "feed_part") for p in parts] for parts in feed_part]

    def turn(g, earlier):
        last = g == groups - 1
        return call(
            partial(turn_kernel, g, heads, cuts_of[g]),
            "turn",
            [
                ((S, width), B16),
                ((8, S), F32),
                ((heads * L, S), B16),
                ((own if last else L, model), B16 if last else F32),
                ((L, 2 * width), F32),
                ((8, model), F32),
                ((S, model), F32),
                ((S, model), B16),
            ],
            [
                token_cotangent,
                middle[g],
                feed_gain_row,
                output_weight,
                key_weight,
                value_weight,
                o[g],
                saved[g],
                probs[g],
                side[g],
                mid,
            ]
            + list(feed_part[g])
            + feed_part_two[g]
            + earlier,
        )

    if aligned:
        down_pieces, up_pieces = 4, 2
        half = (size // 2, share, hidden_units)
        down_piece = (size // 2, share, hidden_units // down_pieces)
        up_piece = (size // 2, share, hidden_units // up_pieces)
        *sends, down_keep, up_keep = call(
            partial(weight_grad_kernel, groups, share, down_pieces, up_pieces),
            "weight_grad",
            [(down_piece, B16)] * down_pieces + [(up_piece, B16)] * up_pieces + [(half, B16)] * 2,
            [("smem", me_row), token_cotangent] + list(active + feed_low + hidden_grad),
        )
    turned = []
    for g in each:
        turned.append(turn(g, [t[3] for t in turned]))
        if aligned and g == 0:
            down_sends = [after(a, turned[0][1]) for a in sends[:down_pieces]]
            down_sum = Scatter(chain, me_row, 1, down_keep, down_sends, "down_core")
            (send,), (keep,) = down_sum.halve(down_sum.whole())
            down_sum = down_sum.next(send, keep, "down_y")
    (
        o_grad,
        delta,
        side_score_grad,
        side_parts,
        side_grads,
        gains,
        middle_grad,
        middle_low,
    ) = zip(*turned)
    side_part = side_parts[-1]
    side_part_two = swap_tp(side_part, "side_part")
    if aligned:
        up_sends = [after(a, delta[-1]) for a in sends[down_pieces:]]
        up_sum = Scatter(chain, me_row, 1, up_keep, up_sends, "up_core")
    back = []
    for g in each:
        last = g == groups - 1
        back.append(
            call(
                partial(attend_back_kernel, g, heads),
                "attend_back",
                [((rows if last else S, model), B16), ((S, 3 * width), B16), ((1, model), F32)],
                [
                    tokens,
                    saved[g],
                    o_grad[g],
                    probs[g],
                    delta[g],
                    side_score_grad[g],
                    side[g],
                    query_weight,
                    key_weight,
                    value_weight,
                    gains[g],
                ]
                + [b[2] for b in back[-1:]]
                + ([b[0] for b in back] if last else []),
            )
        )
        if g == 0:
            if aligned:
                up_sends, up_keeps = up_sum.halve(up_sum.whole())
            mid_low, middle_latent_grad = call(
                side_kernel,
                "side",
                [((own, model), B16), ((own, model), F32)],
                [side_part, side_part_two, mid, latent_cotangent, attention_gain_row],
            )
    if aligned:
        (send,), (keep,) = down_sum.halve(down_sum.whole())
        up_sum = up_sum.next(up_sends[0], up_keeps[0], "up_y", down_sum.gots[0])
        down_sum = down_sum.next(send, keep, "down_z")
    held = mid_low
    held_steps = []
    for step in gathered[:-1]:
        held = join([held] + [flip(held, b, "mid") for b in step])
        held_steps.append(held)
    mid_low_one, mid_low_two = held, flip(held, 1, "mid")
    token_parts, grads, _ = zip(*back)
    token_part = token_parts[-1]
    gain_sum = back[-1][2]
    gain_two = swap_tp(gain_sum, "gain")
    token_part_two = swap_tp(after(token_part, gain_two), "token_part")
    if aligned:
        columns = 4 * width + 128
        arrays = (saved, grads, middle_low, o, side, side_grads, up_bias_sum, down_bias_sum, gains)
        *rest_sends, rest_keep = call(
            partial(attention_grad_kernel, groups, share),
            "attention_grad",
            [((size // 2, share, n), B16) for n in (width, width, width, width + 128, columns)],
            [("smem", me_row), gain_sum, gain_two] + [a for of_groups in arrays for a in of_groups],
        )
        rest_sum = Scatter(chain, me_row, 1, rest_keep, rest_sends, "rest_core")
    else:

        def flat(arrays, start, end):
            return jnp.concatenate([a[:, start:end] for a in arrays], axis=0).astype(B16)

        token_low = flat(saved, 3 * width, 3 * width + model)
        side_low = flat(side, 2 * width, 2 * width + model)
        products = (
            tn(token_cotangent, flat(active, 0, hidden_units)),
            tn(flat(feed_low, 0, model), flat(hidden_grad, 0, hidden_units)),
            tn(token_low, flat(grads, 0, width)),
            tn(token_low, flat(grads, width, 2 * width)) + tn(side_low, flat(side_grads, 0, width)),
            tn(token_low, flat(grads, 2 * width, 3 * width))
            + tn(side_low, flat(side_grads, width, 2 * width)),
            tn(flat(middle_low, 0, model), flat(o, 0, width)),
        )
        vectors = [sum(down_bias_sum), sum(gains)[:1], gain_sum + gain_two]
        vectors.append(sum(up_bias_sum).reshape(size, -1, share).swapaxes(0, 1).reshape(-1, model))
        vectors = jnp.concatenate(vectors, axis=0)
        total = jnp.concatenate([a.astype(B16) for a in products + (vectors.T,)], axis=1)
        total = scatter_sum(total.reshape(size, share, -1))
    block = min(everyone, max(16, 65536 // everyone))
    latent_sum, latent_query_done, latent_key_done, latent_value_done, latent_output_done = call(
        partial(latent_back_kernel, heads, own, turns, block),
        "latent_back",
        [((own + 16, model), B16)] + [((share, width), F32, OUT)] * 4,
        [
            ("smem", me_row),
            ("smem", group_image),
            latents_all,
            lat_q,
            lat_k,
            lat_v,
            mid_low_one,
            mid_low_two,
            latent_gain_row,
            *latent_weights,
        ],
        scratch=[pltpu.VMEM((everyone, width), B16)] * 4 + [pltpu.VMEM((everyone, 128), F32)],
        limit=latent_limit,
    )
    latent_sum_two = swap_tp(latent_sum, "latent_sum")
    down_part_two = swap_tp(after(down_part, latent_sum), "down_part")
    if aligned:
        cuts = [(0, 2 * width), (2 * width, columns)]
        rest_sends, rest_keeps = rest_sum.halve(cuts)
        (send,), (keep,) = down_sum.halve(down_sum.whole())
        down_sum = down_sum.next(send, keep, "down_zz")
        (send,), (keep,) = up_sum.halve(up_sum.whole())
        first = rest_sum.next(rest_sends[0], rest_keeps[0], "first_y", up_sum.gots[0])
        up_sum = up_sum.next(send, keep, "up_z")
    (token_grad,) = call(
        leave_kernel,
        "leave",
        [((rows, model), F32, OUT)],
        [tokens, attention_gain_row, token_part, token_part_two] + list(middle_grad),
    )
    latent_grad, latent_gain_sum = call(
        latent_leave_kernel,
        "latent_leave",
        [((own, model), F32, OUT), ((8, share), F32, OUT)],
        [("smem", me_row), latents, latent_sum, latent_sum_two, latent_gain_row, middle_latent_grad],
    )
    if aligned:
        (down_done,) = down_sum.finish([(0, hidden_units, False)])
        (send,), (keep,) = up_sum.halve(up_sum.whole())
        up_sum = up_sum.next(send, keep, "up_zz")
        (send,), (keep,) = first.halve(first.whole())
        second = rest_sum.next(rest_sends[1], rest_keeps[1], "second_y", first.gots[0])
        first = first.next(send, keep, "first_z")
    (mixed_tokens,) = call(
        result_kernel,
        "result",
        [((rows, model), B16, OUT)],
        [down_bias_row, down_part, down_part_two] + list(middle),
    )
    if aligned:
        (up_done,) = up_sum.finish([(0, hidden_units, False)])
        (send,), (keep,) = first.halve(first.whole())
        first = first.next(send, keep, "first_zz")
        (send,), (keep,) = second.halve(second.whole())
        second = second.next(send, keep, "second_z")
        query_done, key_done = first.finish([(0, width, False), (width, 2 * width, False)])
        (send,), (keep,) = second.halve(second.whole())
        second = second.next(send, keep, "second_zz")
        cuts = [(0, width, False), (width, 2 * width, False), (2 * width, 2 * width + 128, True)]
        value_done, output_done, vectors = second.finish(cuts)
    else:
        ends = [hidden_units, 2 * hidden_units] + [2 * hidden_units + i * width for i in range(1, 5)]
        down_done, up_done, query_done, key_done, value_done, output_done, vectors = jnp.split(
            total, ends, axis=1
        )
        vectors = vectors.T
    return (
        mixed_tokens,
        mixed_latents,
        token_grad,
        latent_grad,
        latent_query_done,
        latent_key_done,
        latent_value_done,
        latent_output_done.T,
        query_done,
        key_done,
        value_done,
        output_done.T,
        up_done,
        vectors[3 : 3 + hidden_units // model].reshape(-1),
        down_done.T,
        vectors[0],
        latent_gain_sum[0],
        vectors[2],
        vectors[1],
    )


def solution(mesh):
    placed = (
        P("dp", None),
        P("dp", None),
        P(None, "tp"),
        P(None, "tp"),
        P(None, "tp"),
        P("tp", None),
        P(None, "tp"),
        P(None, "tp"),
        P(None, "tp"),
        P("tp", None),
        P(None, "tp"),
        P("tp"),
        P("tp", None),
        P(),
        P(),
        P(),
        P(),
        P(),
        P("dp", None),
        P("dp", None),
    )
    return jax.shard_map(
        local,
        mesh=mesh,
        in_specs=placed,
        out_specs=(
            P("dp", None),
            P("dp", None),
            P("dp", None),
            P("dp", None),
            P("dp", "tp"),
            P("dp", "tp"),
            P("dp", "tp"),
            P("tp", "dp"),
            P("dp", "tp"),
            P("dp", "tp"),
            P("dp", "tp"),
            P("tp", "dp"),
            P("dp", "tp"),
            P(("tp", "dp")),
            P("tp", "dp"),
            P("dp"),
            P("dp"),
            P("dp"),
            P("dp"),
        ),
        check_vma=False,
    )
```

time: 204 us -> 150 us (0.74)
  Pallas kernels: 87.9 us -> 51.7 us
  waiting for transfers between devices: 52.8 us -> 40.8 us
  local copies, waits for them, and re-layouts: 15.2 us -> 5.09 us
  starting transfers between devices: 45.3 us -> 51.4 us
    pallas_call x28 -> x39, Pallas kernels: 87.9 us -> 51.7 us  [the longest x37 46.5 us: call(): pl.pallas_call(kernel, out_shape=[result(*out) for out in outs], in_specs...]
    ppermute x12, waiting for transfers between devices: 37.3 us -> 13.2 us  [swap_tp(): return lax.ppermute(values, 'tp', [(0, 1), (1, 0)])]
    ppermute x25 -> x32, waiting for transfers between devices: 15.4 us -> 27.6 us  [flip(): return lax.ppermute(values, 'dp', [(i, i ^ bits) for i in range(size)])]
    unnamed x102 -> x4, local copies, waits for them, and re-layouts: 11.5 us -> 0.01 us
    ppermute x12, starting transfers between devices: 12.9 us -> 16.6 us  [swap_tp(): return lax.ppermute(values, 'tp', [(0, 1), (1, 0)])]
    ppermute x25 -> x32, starting transfers between devices: 32.4 us -> 34.8 us  [flip(): return lax.ppermute(values, 'dp', [(i, i ^ bits) for i in range(size)])]
  transfers between devices with their start and end apart: 37 -> 44, of which waited for: 14 -> 19; matrix products, arithmetic and copies ran while one was open for 2% -> 3% of each run, Pallas kernels for 31% -> 31%
where the time goes in v1:
time: 150 us
  Pallas kernels  51.7 us (34%)
  starting transfers between devices  51.4 us (34%)
  waiting for transfers between devices  40.8 us (27%)
  local copies, waits for them, and re-layouts  5.09 us (3%)
    pallas_call x37, Pallas kernels, call(): pl.pallas_call(kernel, out_shape=[result(*out) for out in outs], in_specs...  46.5 us
    ppermute x32, starting transfers between devices, flip(): return lax.ppermute(values, 'dp', [(i, i ^ bits) for i in range(size)])  34.8 us
    ppermute x32, waiting for transfers between devices, flip(): return lax.ppermute(values, 'dp', [(i, i ^ bits) for i in range(size)])  27.6 us
    ppermute x12, starting transfers between devices, swap_tp(): return lax.ppermute(values, 'tp', [(0, 1), (1, 0)])  16.6 us
    ppermute x12, waiting for transfers between devices, swap_tp(): return lax.ppermute(values, 'tp', [(0, 1), (1, 0)])  13.2 us
    pallas_call x2, Pallas kernels, load(): pl.pallas_call(load_kernel, out_shape=[pltpu.VMEM(a.shape, a.dtype) for a...  5.25 us
  transfers between devices with their start and end apart: 44, of which 19 were waited for; matrix products, arithmetic and copies ran while one was open for 3% of the time, Pallas kernels for 31%

profile of v1, /device:TPU:0, one launch (start us, length us, event | category | flops | bytes accessed | tf_op | source)
XLA Modules:
  0.0 150.0 jit_solution(14749354008328751834)
XLA Ops:
  0.7 3.0 %collective-permute-start.7 = (bf16[384,768]{1,0:T(8,128)(2,1)}, bf16[384,768]{1,0:T(8,128)(2,1)S(1)}, u32[]{:S(2)}, u32[]{:S(2)}) collective-permute-start(bf16[384,768]{1,0:T(8,128)(2,1)} %refs_6_.1), channel_id=1, source_target_pairs={{0,16},{16,0},{1,17},{17,1},{2,18},{18,2},{3,19},{19,3},{4,20},{20... | collective-permute-start | bytes 1769480 | tf_op jit(solution)/shard_map/swap_output_weight/ppermute | solution.py:629
  5.2 2.5 %collective-permute-start.2 = (bf16[16,768]{1,0:T(8,128)(2,1)}, bf16[16,768]{1,0:T(8,128)(2,1)S(1)}, u32[]{:S(2)}, u32[]{:S(2)}) collective-permute-start(bf16[16,768]{1,0:T(8,128)(2,1)} %refs_0_.1), channel_id=1, source_target_pairs={{0,12},{1,13},{2,14},{3,15},{4,8},{5,9},{6,10},{7,11},{8,4},{9,5},... | collective-permute-start | bytes 73736 | tf_op jit(solution)/shard_map/flip_latents/ppermute | solution.py:635
  11.3 2.7 %load.2 = (bf16[512,768]{1,0:T(8,128)(2,1)S(1)}, bf16[768,384]{1,0:T(8,128)(2,1)S(1)}, bf16[768,384]{1,0:T(8,128)(2,1)S(1)}, bf16[768,384]{1,0:T(8,128)(2,1)S(1)...) custom-call(bf16[512,768]{1,0:T(8,128)(2,1)} %refs_0_, ...), custom_call_target="tpu_custom_call" | custom-call | tf_op jit(solution)/shard_map/load/pallas_call | solution.py:609
  15.6 3.1 %collective-permute-done.3.refs_1_ = bf16[64,768]{1,0:T(8,128)(2,1)S(1)} collective-permute-done((bf16[64,768]{1,0:T(8,128)(2,1)S(1)}, bf16[64,768]{1,0:T(8,128)(2,1)S(1)}, u32[]{:S(2)}, u32[]{:S(2)}) %collective-permute-start.3) | collective-permute-done | bytes 98336 | tf_op jit(solution)/shard_map/flip_latents/ppermute | solution.py:635
  21.3 2.1 %latent.1 = (bf16[256,768]{1,0:T(8,128)(2,1)S(1)}, bf16[256,384]{1,0:T(8,128)(2,1)S(1)}, bf16[256,384]{1,0:T(8,128)(2,1)S(1)}, bf16[256,384]{1,0:T(8,128)(2,1)S(1)}, bf16[16,768]{1,0:T(8,128)(2,1)S(1)}) custom-call(s32[1]{0:T(128)} %bitcast.me, s32[32]{0:T(128)S(1)} %copy-done.1, bf16[128,768]{1,0:T(8,128)(2,1)S(1)} %join.5.one, ...), custom_call_target="tpu_custom_call" | custom-call | tf_op jit(solution)/shard_map/latent/pallas_call | solution.py:586
  23.9 2.6 %load.3 = (bf16[768,1536]{1,0:T(8,128)(2,1)S(1)}, bf16[1536,768]{1,0:T(8,128)(2,1)S(1)}, bf16[512,768]{1,0:T(8,128)(2,1)S(1)}) custom-call(bf16[768,1536]{1,0:T(8,128)(2,1)} %refs_0_.2, bf16[1536,768]{1,0:T(8,128)(2,1)} %refs_1_.3, bf16[512,768]{1,0:T(8,128)(2,1)} %refs_2_.3), custom_call_target="tpu_custom_call" | custom-call | tf_op jit(solution)/shard_map/load/pallas_call | solution.py:609
  27.2 1.9 %attend.2 = (bf16[256,384]{1,0:T(8,128)(2,1)S(1)}, f32[56,256]{1,0:T(8,128)S(1)}, f32[8,1536]{1,0:T(8,128)S(1)}, f32[16,768]{1,0:T(8,128)S(1)}, bf16[16,768]{1,0:T(8,128)(2,1)}) custom-call(bf16[256,1920]{1,0:T(8,128)(2,1)S(1)} %enter.2.saved.refs_0_, bf16[16,768]{1,0:T(8,128)(2,1)S(1)} %get-tuple-element.189.latents, ...), custom_call_target="tpu_custom_call" | custom-call | tf_op jit(solution)/shard_map/attend/pallas_call | solution.py:586
  29.9 1.9 %attend.3 = (bf16[256,384]{1,0:T(8,128)(2,1)S(1)}, f32[56,256]{1,0:T(8,128)S(1)}, f32[8,1536]{1,0:T(8,128)S(1)}, f32[16,768]{1,0:T(8,128)}, bf16[16,768]{1,0:T(8,128)(2,1)}) custom-call(bf16[256,1920]{1,0:T(8,128)(2,1)S(1)} %enter.3.saved.refs_1_, bf16[16,768]{1,0:T(8,128)(2,1)S(1)} %get-tuple-element.189.latents, ...), custom_call_target="tpu_custom_call" | custom-call | tf_op jit(solution)/shard_map/attend/pallas_call | solution.py:586
  33.0 3.1 %collective-permute-done.6.o_two = bf16[256,384]{1,0:T(8,128)(2,1)S(1)} collective-permute-done((bf16[256,384]{1,0:T(8,128)(2,1)S(1)}, bf16[256,384]{1,0:T(8,128)(2,1)S(1)}, u32[]{:S(2)}, u32[]{:S(2)}) %collective-permute-start.6) | collective-permute-done | bytes 196640 | tf_op jit(solution)/shard_map/swap_o/ppermute | solution.py:629
  36.1 4.2 %feed.2 = (bf16[128,768]{1,0:T(8,128)(2,1)S(1)}, bf16[128,768]{1,0:T(8,128)(2,1)S(1)}, bf16[256,1536]{1,0:T(8,128)(2,1)S(1)}, bf16[256,1536]{1,0:T(8,128)(2,1)S(...) custom-call(s32[1]{0:T(128)} %bitcast.1.place, ...), custom_call_target="tpu_custom_call" | custom-call | tf_op jit(solution)/shard_map/feed/pallas_call | solution.py:586
  42.4 4.4 %feed.3 = (bf16[256,768]{1,0:T(8,128)(2,1)S(1)}, bf16[256,1536]{1,0:T(8,128)(2,1)S(1)}, bf16[256,1536]{1,0:T(8,128)(2,1)S(1)}, bf16[256,768]{1,0:T(8,128)(2,1)S(...) custom-call(s32[1]{0:T(128)} %bitcast.1.place, ...), custom_call_target="tpu_custom_call" | custom-call | tf_op jit(solution)/shard_map/feed/pallas_call | solution.py:586
  48.4 3.1 %weight_grad.1 = (bf16[8,48,384]{2,1,0:T(8,128)(2,1)S(1)}, bf16[8,48,384]{2,1,0:T(8,128)(2,1)S(1)}, bf16[8,48,384]{2,1,0:T(8,128)(2,1)S(1)}, bf16[8,48,384]{2,1,...) custom-call(s32[1]{0:T(128)} %bitcast.me, ...), custom_call_target="tpu_custom_call" | custom-call | tf_op jit(solution)/shard_map/weight_grad/pallas_call | solution.py:586
  51.5 1.8 %turn.2 = (bf16[256,384]{1,0:T(8,128)(2,1)S(1)}, f32[8,256]{1,0:T(8,128)S(1)}, bf16[48,256]{1,0:T(8,128)(2,1)S(1)}, f32[8,768]{1,0:T(8,128)S(1)}, f32[8,768]{1,0...) custom-call(bf16[512,768]{1,0:T(8,128)(2,1)S(1)} %get-tuple-element.205.cotangent, ...), custom_call_target="tpu_custom_call" | custom-call | tf_op jit(solution)/shard_map/turn/pallas_call | solution.py:586
  57.5 1.8 %turn.3 = (bf16[256,384]{1,0:T(8,128)(2,1)S(1)}, f32[8,256]{1,0:T(8,128)S(1)}, bf16[48,256]{1,0:T(8,128)(2,1)S(1)}, bf16[16,768]{1,0:T(8,128)(2,1)S(1)}, f32[8,7...) custom-call(bf16[512,768]{1,0:T(8,128)(2,1)S(1)} %get-tuple-element.205.cotangent, ...), custom_call_target="tpu_custom_call" | custom-call | tf_op jit(solution)/shard_map/turn/pallas_call | solution.py:586
  63.2 2.9 %attend_back.2 = (bf16[256,768]{1,0:T(8,128)(2,1)S(1)}, bf16[256,1152]{1,0:T(8,128)(2,1)S(1)}, f32[1,768]{1,0:T(1,128)S(1)}) custom-call(bf16[512,768]{1,0:T(8,128)(2,1)S(1)} %get-tuple-element.188.tokens, bf16[256,1920]{1,0:T(8,128)(2,1)S(1)} %enter.2.saved.refs_0_, bf16[256,384]{1,0:T(8,128)(2,1)S(1)} %get-tuple-element.252.o_grad, ...), custom_call_target="tpu_custom_call" | custom-call | tf_op jit(solution)/shard_map/attend_back/pallas_call | solution.py:586
  66.7 3.0 %collective-permute-start.22 = (bf16[16,768]{1,0:T(8,128)(2,1)S(1)}, bf16[16,768]{1,0:T(8,128)(2,1)S(1)}, u32[]{:S(2)}, u32[]{:S(2)}) collective-permute-start(bf16[16,768]{1,0:T(8,128)(2,1)S(1)} %get-tuple-element.276.refs_0_), channel_id=1, source_target_pairs={{0,12},{1,13},{2,14},{3,15},{4,8},{5,9},{6,10},{7,11},{8,4},{9,5},... | collective-permute-start | bytes 73736 | tf_op jit(solution)/shard_map/flip_mid/ppermute | solution.py:635
  71.1 3.1 %attend_back.3 = (bf16[512,768]{1,0:T(8,128)(2,1)S(1)}, bf16[256,1152]{1,0:T(8,128)(2,1)S(1)}, f32[1,768]{1,0:T(1,128)S(1)}) custom-call(bf16[512,768]{1,0:T(8,128)(2,1)S(1)} %get-tuple-element.188.tokens, bf16[256,1920]{1,0:T(8,128)(2,1)S(1)} %enter.3.saved.refs_1_, bf16[256,384]{1,0:T(8,128)(2,1)S(1)} %get-tuple-element.267.o_grad, ...), custom_call_target="tpu_custom_call" | custom-call | tf_op jit(solution)/shard_map/attend_back/pallas_call | solution.py:586
  80.6 2.3 %attention_grad.1 = (bf16[8,48,384]{2,1,0:T(8,128)(2,1)S(1)}, bf16[8,48,384]{2,1,0:T(8,128)(2,1)S(1)}, bf16[8,48,384]{2,1,0:T(8,128)(2,1)S(1)}, bf16[8,48,512]{2,1,0:T(8,128)(2,1)S(1)}, bf16[8,48,1664]{2,1,0:T(8,128)(2,1)S(1)}) custom-call(s32[1]{0:T(128)} %bitcast.me, f32[1,768]{1,0:T(1,128)S(1)} %get-tuple-element.272.gain_one, ...), custom_call_target="tpu_custom_call" | custom-call | tf_op jit(solution)/shard_map/attention_grad/pallas_call | solution.py:586
  86.9 5.9 %latent_back.1 = (bf16[32,768]{1,0:T(8,128)(2,1)S(1)}, f32[48,384]{1,0:T(8,128)}, f32[48,384]{1,0:T(8,128)}, f32[48,384]{1,0:T(8,128)}, f32[48,384]{1,0:T(8,128)}) custom-call(s32[1]{0:T(128)} %bitcast.me, s32[32]{0:T(128)S(1)} %copy-done.1, bf16[256,768]{1,0:T(8,128)(2,1)S(1)} %get-tuple-element.289.latents, bf16[256,384]{1,0:T(8,128)(2,1)S(1)} %get-tuple-element.290.q, ...), custom_call_target="tpu_custom_call" | custom-call | tf_op jit(solution)/shard_map/latent_back/pallas_call | solution.py:586
  95.2 3.6 %collective-permute-done.31 = bf16[4,48,1536]{2,1,0:T(8,128)(2,1)S(1)} collective-permute-done((bf16[4,48,1536]{2,1,0:T(8,128)(2,1)S(1)}, bf16[4,48,1536]{2,1,0:T(8,128)(2,1)S(1)}, u32[]{:S(2)}, u32[]{:S(2)}) %collective-permute-start.31) | collective-permute-done | bytes 589856 | tf_op jit(solution)/shard_map/flip_up_y/ppermute | solution.py:635
  99.9 2.1 %collective-permute-done.30 = bf16[2,48,1536]{2,1,0:T(8,128)(2,1)S(1)} collective-permute-done((bf16[2,48,1536]{2,1,0:T(8,128)(2,1)S(1)}, bf16[2,48,1536]{2,1,0:T(8,128)(2,1)S(1)}, u32[]{:S(2)}, u32[]{:S(2)}) %collective-permute-start.30) | collective-permute-done | bytes 294944 | tf_op jit(solution)/shard_map/flip_down_z/ppermute | solution.py:635
  102.2 1.8 %collective-permute-start.35 = (bf16[2,48,1536]{2,1,0:T(8,128)(2,1)S(1)}, bf16[2,48,1536]{2,1,0:T(8,128)(2,1)S(1)}, u32[]{:S(2)}, u32[]{:S(2)}) collective-permute-start(bf16[2,48,1536]{2,1,0:T(8,128)(2,1)S(1)} %get-tuple-element.307), channel_id=1, source_target_pairs={{0,4},{1,5},{2,6},{3,7},{4,0},{5,1},{6,2},{7,3},{8,12},{9,13},{10,... | collective-permute-start | bytes 884744 | tf_op jit(solution)/shard_map/flip_up_z/ppermute | solution.py:635
  104.0 3.0 %collective-permute-done.36 = bf16[4,48,768]{2,1,0:T(8,128)(2,1)S(1)} collective-permute-done((bf16[4,48,768]{2,1,0:T(8,128)(2,1)S(1)}, bf16[4,48,768]{2,1,0:T(8,128)(2,1)S(1)}, u32[]{:S(2)}, u32[]{:S(2)}) %collective-permute-start.36) | collective-permute-done | bytes 294944 | tf_op jit(solution)/shard_map/flip_first_y/ppermute | solution.py:635
  108.0 2.8 %collective-permute-start.34 = (bf16[1,48,1536]{2,1,0:T(8,128)(2,1)S(1)}, bf16[1,48,1536]{2,1,0:T(8,128)(2,1)S(1)}, u32[]{:S(2)}, u32[]{:S(2)}) collective-permute-start(bf16[1,48,1536]{2,1,0:T(8,128)(2,1)S(1)} %get-tuple-element.303), channel_id=1, source_target_pairs={{0,8},{1,9},{2,10},{3,11},{4,12},{5,13},{6,14},{7,15},{8,0},{9,1},... | collective-permute-start | bytes 442376 | tf_op jit(solution)/shard_map/flip_down_zz/ppermute | solution.py:635
  112.6 2.4 %leave.1 = f32[512,768]{1,0:T(8,128)} custom-call(bf16[512,768]{1,0:T(8,128)(2,1)S(1)} %get-tuple-element.188.tokens, f32[1,768]{1,0:T(1,128)S(1)} %reshape.153.gain, bf16[512,768]{1,0:T(8,128)(2,1)S(1)} %get-tuple-element.310.part_one, bf16[512,768]{1,0:T(8,128)(2,1)S(1)} %collective-permute-done.32.part_two, f32[256,768]{1,0:T(8,128)S(1)} %get-tuple-element.311.refs_0_, ...), custom_call_target="tpu_custom_call" | custom-call | tf_op jit(solution)/shard_map/leave/pallas_call | solution.py:586
  114.9 8.0 %collective-permute-done.33.part_two = bf16[32,768]{1,0:T(8,128)(2,1)S(1)} collective-permute-done((bf16[32,768]{1,0:T(8,128)(2,1)S(1)}, bf16[32,768]{1,0:T(8,128)(2,1)S(1)}, u32[]{:S(2)}, u32[]{:S(2)}) %collective-permute-start.33) | collective-permute-done | bytes 49184 | tf_op jit(solution)/shard_map/swap_latent_sum/ppermute | solution.py:629
  124.6 2.9 %collective-permute-start.38 = (bf16[1,48,1536]{2,1,0:T(8,128)(2,1)S(1)}, bf16[1,48,1536]{2,1,0:T(8,128)(2,1)S(1)}, u32[]{:S(2)}, u32[]{:S(2)}) collective-permute-start(bf16[1,48,1536]{2,1,0:T(8,128)(2,1)S(1)} %get-tuple-element.320), channel_id=1, source_target_pairs={{0,8},{1,9},{2,10},{3,11},{4,12},{5,13},{6,14},{7,15},{8,0},{9,1},... | collective-permute-start | bytes 442376 | tf_op jit(solution)/shard_map/flip_up_zz/ppermute | solution.py:635
  129.5 4.9 %collective-permute-done.38.got = bf16[1,48,1536]{2,1,0:T(8,128)(2,1)S(1)} collective-permute-done((bf16[1,48,1536]{2,1,0:T(8,128)(2,1)S(1)}, bf16[1,48,1536]{2,1,0:T(8,128)(2,1)S(1)}, u32[]{:S(2)}, u32[]{:S(2)}) %collective-permute-start.38) | collective-permute-done | bytes 147488 | tf_op jit(solution)/shard_map/flip_up_zz/ppermute | solution.py:635
  136.3 2.3 %collective-permute-start.41 = (bf16[1,48,768]{2,1,0:T(8,128)(2,1)S(1)}, bf16[1,48,768]{2,1,0:T(8,128)(2,1)S(1)}, u32[]{:S(2)}, u32[]{:S(2)}) collective-permute-start(bf16[1,48,768]{2,1,0:T(8,128)(2,1)S(1)} %get-tuple-element.338), channel_id=1, source_target_pairs={{0,8},{1,9},{2,10},{3,11},{4,12},{5,13},{6,14},{7,15},{8,0},{9,1},... | collective-permute-start | bytes 221192 | tf_op jit(solution)/shard_map/flip_first_zz/ppermute | solution.py:635
  138.6 3.5 %collective-permute-done.41.got = bf16[1,48,768]{2,1,0:T(8,128)(2,1)S(1)} collective-permute-done((bf16[1,48,768]{2,1,0:T(8,128)(2,1)S(1)}, bf16[1,48,768]{2,1,0:T(8,128)(2,1)S(1)}, u32[]{:S(2)}, u32[]{:S(2)}) %collective-permute-start.41) | collective-permute-done | bytes 73760 | tf_op jit(solution)/shard_map/flip_first_zz/ppermute | solution.py:635
  142.7 2.2 %collective-permute-start.43 = (bf16[1,48,896]{2,1,0:T(8,128)(2,1)S(1)}, bf16[1,48,896]{2,1,0:T(8,128)(2,1)S(1)}, u32[]{:S(2)}, u32[]{:S(2)}) collective-permute-start(bf16[1,48,896]{2,1,0:T(8,128)(2,1)S(1)} %get-tuple-element.350), channel_id=1, source_target_pairs={{0,8},{1,9},{2,10},{3,11},{4,12},{5,13},{6,14},{7,15},{8,0},{9,1},... | collective-permute-start | bytes 258056 | tf_op jit(solution)/shard_map/flip_second_zz/ppermute | solution.py:635
  145.5 2.7 %collective-permute-done.43.got = bf16[1,48,896]{2,1,0:T(8,128)(2,1)S(1)} collective-permute-done((bf16[1,48,896]{2,1,0:T(8,128)(2,1)S(1)}, bf16[1,48,896]{2,1,0:T(8,128)(2,1)S(1)}, u32[]{:S(2)}, u32[]{:S(2)}) %collective-permute-start.43) | collective-permute-done | bytes 86048 | tf_op jit(solution)/shard_map/flip_second_zz/ppermute | solution.py:635
  (108 shorter events, 51.5 us)
Async XLA Ops:
  0.7 35.5 %collective-permute-start.7 = (bf16[384,768]{1,0:T(8,128)(2,1)}, bf16[384,768]{1,0:T(8,128)(2,1)S(1)}, u32[]{:S(2)}, u32[]{:S(2)}) collective-permute-start(bf16[384,768]{1,0:T(8,128)(2,1)} %refs_6_.1), channel_id=1, source_target_pairs={{0,16},{16,0},{1,17},{17,1},{2,18},{18,2},{3,19},{19,3},{4,20},{20... | collective-permute-start | bytes 1769480 | tf_op jit(solution)/shard_map/swap_output_weight/ppermute | solution.py:629
  3.7 10.3 %collective-permute-start = (bf16[16,768]{1,0:T(8,128)(2,1)}, bf16[16,768]{1,0:T(8,128)(2,1)S(1)}, u32[]{:S(2)}, u32[]{:S(2)}) collective-permute-start(bf16[16,768]{1,0:T(8,128)(2,1)} %refs_0_.1), channel_id=1, source_target_pairs={{0,4},{1,5},{2,6},{3,7},{4,0},{5,1},{6,2},{7,3},{8,12},{9,13},{10,... | collective-permute-start | bytes 73736 | tf_op jit(solution)/shard_map/flip_latents/ppermute | solution.py:635
  5.2 8.7 %collective-permute-start.2 = (bf16[16,768]{1,0:T(8,128)(2,1)}, bf16[16,768]{1,0:T(8,128)(2,1)S(1)}, u32[]{:S(2)}, u32[]{:S(2)}) collective-permute-start(bf16[16,768]{1,0:T(8,128)(2,1)} %refs_0_.1), channel_id=1, source_target_pairs={{0,12},{1,13},{2,14},{3,15},{4,8},{5,9},{6,10},{7,11},{8,4},{9,5},... | collective-permute-start | bytes 73736 | tf_op jit(solution)/shard_map/flip_latents/ppermute | solution.py:635
  7.7 6.3 %collective-permute-start.1 = (bf16[16,768]{1,0:T(8,128)(2,1)}, bf16[16,768]{1,0:T(8,128)(2,1)S(1)}, u32[]{:S(2)}, u32[]{:S(2)}) collective-permute-start(bf16[16,768]{1,0:T(8,128)(2,1)} %refs_0_.1), channel_id=1, source_target_pairs={{0,8},{1,9},{2,10},{3,11},{4,12},{5,13},{6,14},{7,15},{8,0},{9,1},... | collective-permute-start | bytes 73736 | tf_op jit(solution)/shard_map/flip_latents/ppermute | solution.py:635
  29.1 7.0 %collective-permute-start.6 = (bf16[256,384]{1,0:T(8,128)(2,1)S(1)}, bf16[256,384]{1,0:T(8,128)(2,1)S(1)}, u32[]{:S(2)}, u32[]{:S(2)}) collective-permute-start(bf16[256,384]{1,0:T(8,128)(2,1)S(1)} %get-tuple-element.211.o.refs_6_), channel_id=1, source_target_pairs={{0,16},{16,0},{1,17},{17,1},{2,18},{18,2},{3,19},{19,3},{4,20},{20... | collective-permute-start | bytes 589832 | tf_op jit(solution)/shard_map/swap_o/ppermute | solution.py:629
  31.8 10.6 %collective-permute-start.8 = (bf16[256,384]{1,0:T(8,128)(2,1)S(1)}, bf16[256,384]{1,0:T(8,128)(2,1)S(1)}, u32[]{:S(2)}, u32[]{:S(2)}) collective-permute-start(bf16[256,384]{1,0:T(8,128)(2,1)S(1)} %get-tuple-element.217.o.refs_7_), channel_id=1, source_target_pairs={{0,16},{16,0},{1,17},{17,1},{2,18},{18,2},{3,19},{19,3},{4,20},{20... | collective-permute-start | bytes 589832 | tf_op jit(solution)/shard_map/swap_o/ppermute | solution.py:629
  40.3 11.2 %collective-permute-start.9 = (bf16[128,768]{1,0:T(8,128)(2,1)S(1)}, bf16[128,768]{1,0:T(8,128)(2,1)S(1)}, u32[]{:S(2)}, u32[]{:S(2)}) collective-permute-start(bf16[128,768]{1,0:T(8,128)(2,1)S(1)} %get-tuple-element.233.rest_0_), channel_id=1, source_target_pairs={{0,16},{16,0},{1,17},{17,1},{2,18},{18,2},{3,19},{19,3},{4,20},{20... | collective-permute-start | bytes 589832 | tf_op jit(solution)/shard_map/swap_feed_part/ppermute | solution.py:629
  41.9 9.6 %collective-permute-start.10 = (bf16[128,768]{1,0:T(8,128)(2,1)S(1)}, bf16[128,768]{1,0:T(8,128)(2,1)S(1)}, u32[]{:S(2)}, u32[]{:S(2)}) collective-permute-start(bf16[128,768]{1,0:T(8,128)(2,1)S(1)} %get-tuple-element.234.rest_1_), channel_id=1, source_target_pairs={{0,16},{16,0},{1,17},{17,1},{2,18},{18,2},{3,19},{19,3},{4,20},{20... | collective-permute-start | bytes 589832 | tf_op jit(solution)/shard_map/swap_feed_part/ppermute | solution.py:629
  46.8 10.7 %collective-permute-start.15 = (bf16[256,768]{1,0:T(8,128)(2,1)S(1)}, bf16[256,768]{1,0:T(8,128)(2,1)S(1)}, u32[]{:S(2)}, u32[]{:S(2)}) collective-permute-start(bf16[256,768]{1,0:T(8,128)(2,1)S(1)} %get-tuple-element.248.rest_0_), channel_id=1, source_target_pairs={{0,16},{16,0},{1,17},{17,1},{2,18},{18,2},{3,19},{19,3},{4,20},{20... | collective-permute-start | bytes 1179656 | tf_op jit(solution)/shard_map/swap_feed_part/ppermute | solution.py:629
  59.4 6.7 %collective-permute-start.17 = (bf16[8,48,768]{2,1,0:T(8,128)(2,1)S(1)}, bf16[8,48,768]{2,1,0:T(8,128)(2,1)S(1)}, u32[]{:S(2)}, u32[]{:S(2)}) collective-permute-start(bf16[8,48,768]{2,1,0:T(8,128)(2,1)S(1)} %get-tuple-element.261), channel_id=1, source_target_pairs={{0,1},{1,0},{2,3},{3,2},{4,5},{5,4},{6,7},{7,6},{8,9},{9,8},{10,11... | collective-permute-start | bytes 1769480 | tf_op jit(solution)/shard_map/flip_up_core/ppermute | solution.py:635
  59.4 6.6 %collective-permute-start.18 = (bf16[8,48,768]{2,1,0:T(8,128)(2,1)S(1)}, bf16[8,48,768]{2,1,0:T(8,128)(2,1)S(1)}, u32[]{:S(2)}, u32[]{:S(2)}) collective-permute-start(bf16[8,48,768]{2,1,0:T(8,128)(2,1)S(1)} %get-tuple-element.263), channel_id=1, source_target_pairs={{0,1},{1,0},{2,3},{3,2},{4,5},{5,4},{6,7},{7,6},{8,9},{9,8},{10,11... | collective-permute-start | bytes 1769480 | tf_op jit(solution)/shard_map/flip_up_core/ppermute | solution.py:635
  59.9 15.3 %collective-permute-start.19 = (bf16[4,48,1536]{2,1,0:T(8,128)(2,1)S(1)}, bf16[4,48,1536]{2,1,0:T(8,128)(2,1)S(1)}, u32[]{:S(2)}, u32[]{:S(2)}) collective-permute-start(bf16[4,48,1536]{2,1,0:T(8,128)(2,1)S(1)} %get-tuple-element.245), channel_id=1, source_target_pairs={{0,2},{1,3},{2,0},{3,1},{4,6},{5,7},{6,4},{7,5},{8,10},{9,11},{10,... | collective-permute-start | bytes 1769480 | tf_op jit(solution)/shard_map/flip_down_y/ppermute | solution.py:635
  66.7 8.7 %collective-permute-start.22 = (bf16[16,768]{1,0:T(8,128)(2,1)S(1)}, bf16[16,768]{1,0:T(8,128)(2,1)S(1)}, u32[]{:S(2)}, u32[]{:S(2)}) collective-permute-start(bf16[16,768]{1,0:T(8,128)(2,1)S(1)} %get-tuple-element.276.refs_0_), channel_id=1, source_target_pairs={{0,12},{1,13},{2,14},{3,15},{4,8},{5,9},{6,10},{7,11},{8,4},{9,5},... | collective-permute-start | bytes 73736 | tf_op jit(solution)/shard_map/flip_mid/ppermute | solution.py:635
  69.6 5.8 %collective-permute-start.21 = (bf16[16,768]{1,0:T(8,128)(2,1)S(1)}, bf16[16,768]{1,0:T(8,128)(2,1)S(1)}, u32[]{:S(2)}, u32[]{:S(2)}) collective-permute-start(bf16[16,768]{1,0:T(8,128)(2,1)S(1)} %get-tuple-element.276.refs_0_), channel_id=1, source_target_pairs={{0,8},{1,9},{2,10},{3,11},{4,12},{5,13},{6,14},{7,15},{8,0},{9,1},... | collective-permute-start | bytes 73736 | tf_op jit(solution)/shard_map/flip_mid/ppermute | solution.py:635
  70.0 5.4 %collective-permute-start.20 = (bf16[16,768]{1,0:T(8,128)(2,1)S(1)}, bf16[16,768]{1,0:T(8,128)(2,1)S(1)}, u32[]{:S(2)}, u32[]{:S(2)}) collective-permute-start(bf16[16,768]{1,0:T(8,128)(2,1)S(1)} %get-tuple-element.276.refs_0_), channel_id=1, source_target_pairs={{0,4},{1,5},{2,6},{3,7},{4,0},{5,1},{6,2},{7,3},{8,12},{9,13},{10,... | collective-permute-start | bytes 73736 | tf_op jit(solution)/shard_map/flip_mid/ppermute | solution.py:635
  83.5 15.3 %collective-permute-start.31 = (bf16[4,48,1536]{2,1,0:T(8,128)(2,1)S(1)}, bf16[4,48,1536]{2,1,0:T(8,128)(2,1)S(1)}, u32[]{:S(2)}, u32[]{:S(2)}) collective-permute-start(bf16[4,48,1536]{2,1,0:T(8,128)(2,1)S(1)} %get-tuple-element.306), channel_id=1, source_target_pairs={{0,2},{1,3},{2,0},{3,1},{4,6},{5,7},{6,4},{7,5},{8,10},{9,11},{10,... | collective-permute-start | bytes 1769480 | tf_op jit(solution)/shard_map/flip_up_y/ppermute | solution.py:635
  84.6 8.2 %collective-permute-start.28 = (bf16[8,48,384]{2,1,0:T(8,128)(2,1)S(1)}, bf16[8,48,384]{2,1,0:T(8,128)(2,1)S(1)}, u32[]{:S(2)}, u32[]{:S(2)}) collective-permute-start(bf16[8,48,384]{2,1,0:T(8,128)(2,1)S(1)} %get-tuple-element.297), channel_id=1, source_target_pairs={{0,1},{1,0},{2,3},{3,2},{4,5},{5,4},{6,7},{7,6},{8,9},{9,8},{10,11... | collective-permute-start | bytes 884744 | tf_op jit(solution)/shard_map/flip_rest_core/ppermute | solution.py:635
  84.6 8.5 %collective-permute-start.26 = (bf16[8,48,384]{2,1,0:T(8,128)(2,1)S(1)}, bf16[8,48,384]{2,1,0:T(8,128)(2,1)S(1)}, u32[]{:S(2)}, u32[]{:S(2)}) collective-permute-start(bf16[8,48,384]{2,1,0:T(8,128)(2,1)S(1)} %get-tuple-element.287), channel_id=1, source_target_pairs={{0,1},{1,0},{2,3},{3,2},{4,5},{5,4},{6,7},{7,6},{8,9},{9,8},{10,11... | collective-permute-start | bytes 884744 | tf_op jit(solution)/shard_map/flip_rest_core/ppermute | solution.py:635
  85.1 9.8 %collective-permute-start.29 = (bf16[8,48,512]{2,1,0:T(8,128)(2,1)S(1)}, bf16[8,48,512]{2,1,0:T(8,128)(2,1)S(1)}, u32[]{:S(2)}, u32[]{:S(2)}) collective-permute-start(bf16[8,48,512]{2,1,0:T(8,128)(2,1)S(1)} %get-tuple-element.298), channel_id=1, source_target_pairs={{0,1},{1,0},{2,3},{3,2},{4,5},{5,4},{6,7},{7,6},{8,9},{9,8},{10,11... | collective-permute-start | bytes 1179656 | tf_op jit(solution)/shard_map/flip_rest_core/ppermute | solution.py:635
  85.1 25.8 %collective-permute-start.32 = (bf16[512,768]{1,0:T(8,128)(2,1)S(1)}, bf16[512,768]{1,0:T(8,128)(2,1)S(1)}, u32[]{:S(2)}, u32[]{:S(2)}) collective-permute-start(bf16[512,768]{1,0:T(8,128)(2,1)S(1)} %get-tuple-element.310.part_one), channel_id=1, source_target_pairs={{0,16},{16,0},{1,17},{17,1},{2,18},{18,2},{3,19},{19,3},{4,20},{20... | collective-permute-start | bytes 2359304 | tf_op jit(solution)/shard_map/swap_token_part/ppermute | solution.py:629
  92.8 35.5 %collective-permute-start.37 = (bf16[512,768]{1,0:T(8,128)(2,1)S(1)}, bf16[512,768]{1,0:T(8,128)(2,1)S(1)}, u32[]{:S(2)}, u32[]{:S(2)}) collective-permute-start(bf16[512,768]{1,0:T(8,128)(2,1)S(1)} %get-tuple-element.327.part_one), channel_id=1, source_target_pairs={{0,16},{16,0},{1,17},{17,1},{2,18},{18,2},{3,19},{19,3},{4,20},{20... | collective-permute-start | bytes 2359304 | tf_op jit(solution)/shard_map/swap_down_part/ppermute | solution.py:629
  93.1 8.9 %collective-permute-start.30 = (bf16[2,48,1536]{2,1,0:T(8,128)(2,1)S(1)}, bf16[2,48,1536]{2,1,0:T(8,128)(2,1)S(1)}, u32[]{:S(2)}, u32[]{:S(2)}) collective-permute-start(bf16[2,48,1536]{2,1,0:T(8,128)(2,1)S(1)} %get-tuple-element.275), channel_id=1, source_target_pairs={{0,4},{1,5},{2,6},{3,7},{4,0},{5,1},{6,2},{7,3},{8,12},{9,13},{10,... | collective-permute-start | bytes 884744 | tf_op jit(solution)/shard_map/flip_down_z/ppermute | solution.py:635
  98.8 8.2 %collective-permute-start.36 = (bf16[4,48,768]{2,1,0:T(8,128)(2,1)S(1)}, bf16[4,48,768]{2,1,0:T(8,128)(2,1)S(1)}, u32[]{:S(2)}, u32[]{:S(2)}) collective-permute-start(bf16[4,48,768]{2,1,0:T(8,128)(2,1)S(1)} %get-tuple-element.323), channel_id=1, source_target_pairs={{0,2},{1,3},{2,0},{3,1},{4,6},{5,7},{6,4},{7,5},{8,10},{9,11},{10,... | collective-permute-start | bytes 884744 | tf_op jit(solution)/shard_map/flip_first_y/ppermute | solution.py:635
  102.2 22.4 %collective-permute-start.35 = (bf16[2,48,1536]{2,1,0:T(8,128)(2,1)S(1)}, bf16[2,48,1536]{2,1,0:T(8,128)(2,1)S(1)}, u32[]{:S(2)}, u32[]{:S(2)}) collective-permute-start(bf16[2,48,1536]{2,1,0:T(8,128)(2,1)S(1)} %get-tuple-element.307), channel_id=1, source_target_pairs={{0,4},{1,5},{2,6},{3,7},{4,0},{5,1},{6,2},{7,3},{8,12},{9,13},{10,... | collective-permute-start | bytes 884744 | tf_op jit(solution)/shard_map/flip_up_z/ppermute | solution.py:635
  107.0 28.3 %collective-permute-start.40 = (bf16[4,48,896]{2,1,0:T(8,128)(2,1)S(1)}, bf16[4,48,896]{2,1,0:T(8,128)(2,1)S(1)}, u32[]{:S(2)}, u32[]{:S(2)}) collective-permute-start(bf16[4,48,896]{2,1,0:T(8,128)(2,1)S(1)} %get-tuple-element.342), channel_id=1, source_target_pairs={{0,2},{1,3},{2,0},{3,1},{4,6},{5,7},{6,4},{7,5},{8,10},{9,11},{10,... | collective-permute-start | bytes 1032200 | tf_op jit(solution)/shard_map/flip_second_y/ppermute | solution.py:635
  108.0 15.8 %collective-permute-start.34 = (bf16[1,48,1536]{2,1,0:T(8,128)(2,1)S(1)}, bf16[1,48,1536]{2,1,0:T(8,128)(2,1)S(1)}, u32[]{:S(2)}, u32[]{:S(2)}) collective-permute-start(bf16[1,48,1536]{2,1,0:T(8,128)(2,1)S(1)} %get-tuple-element.303), channel_id=1, source_target_pairs={{0,8},{1,9},{2,10},{3,11},{4,12},{5,13},{6,14},{7,15},{8,0},{9,1},... | collective-permute-start | bytes 442376 | tf_op jit(solution)/shard_map/flip_down_zz/ppermute | solution.py:635
  110.8 12.1 %collective-permute-start.33 = (bf16[32,768]{1,0:T(8,128)(2,1)S(1)}, bf16[32,768]{1,0:T(8,128)(2,1)S(1)}, u32[]{:S(2)}, u32[]{:S(2)}) collective-permute-start(bf16[32,768]{1,0:T(8,128)(2,1)S(1)} %get-tuple-element.314.part_one), channel_id=1, source_target_pairs={{0,16},{16,0},{1,17},{17,1},{2,18},{18,2},{3,19},{19,3},{4,20},{20... | collective-permute-start | bytes 147464 | tf_op jit(solution)/shard_map/swap_latent_sum/ppermute | solution.py:629
  124.6 9.8 %collective-permute-start.38 = (bf16[1,48,1536]{2,1,0:T(8,128)(2,1)S(1)}, bf16[1,48,1536]{2,1,0:T(8,128)(2,1)S(1)}, u32[]{:S(2)}, u32[]{:S(2)}) collective-permute-start(bf16[1,48,1536]{2,1,0:T(8,128)(2,1)S(1)} %get-tuple-element.320), channel_id=1, source_target_pairs={{0,8},{1,9},{2,10},{3,11},{4,12},{5,13},{6,14},{7,15},{8,0},{9,1},... | collective-permute-start | bytes 442376 | tf_op jit(solution)/shard_map/flip_up_zz/ppermute | solution.py:635
  127.6 7.6 %collective-permute-start.39 = (bf16[2,48,768]{2,1,0:T(8,128)(2,1)S(1)}, bf16[2,48,768]{2,1,0:T(8,128)(2,1)S(1)}, u32[]{:S(2)}, u32[]{:S(2)}) collective-permute-start(bf16[2,48,768]{2,1,0:T(8,128)(2,1)S(1)} %get-tuple-element.324), channel_id=1, source_target_pairs={{0,4},{1,5},{2,6},{3,7},{4,0},{5,1},{6,2},{7,3},{8,12},{9,13},{10,... | collective-permute-start | bytes 442376 | tf_op jit(solution)/shard_map/flip_first_z/ppermute | solution.py:635
  135.3 7.4 %collective-permute-start.42 = (bf16[2,48,896]{2,1,0:T(8,128)(2,1)S(1)}, bf16[2,48,896]{2,1,0:T(8,128)(2,1)S(1)}, u32[]{:S(2)}, u32[]{:S(2)}) collective-permute-start(bf16[2,48,896]{2,1,0:T(8,128)(2,1)S(1)} %get-tuple-element.343), channel_id=1, source_target_pairs={{0,4},{1,5},{2,6},{3,7},{4,0},{5,1},{6,2},{7,3},{8,12},{9,13},{10,... | collective-permute-start | bytes 516104 | tf_op jit(solution)/shard_map/flip_second_z/ppermute | solution.py:635
  136.3 5.7 %collective-permute-start.41 = (bf16[1,48,768]{2,1,0:T(8,128)(2,1)S(1)}, bf16[1,48,768]{2,1,0:T(8,128)(2,1)S(1)}, u32[]{:S(2)}, u32[]{:S(2)}) collective-permute-start(bf16[1,48,768]{2,1,0:T(8,128)(2,1)S(1)} %get-tuple-element.338), channel_id=1, source_target_pairs={{0,8},{1,9},{2,10},{3,11},{4,12},{5,13},{6,14},{7,15},{8,0},{9,1},... | collective-permute-start | bytes 221192 | tf_op jit(solution)/shard_map/flip_first_zz/ppermute | solution.py:635
  142.7 5.4 %collective-permute-start.43 = (bf16[1,48,896]{2,1,0:T(8,128)(2,1)S(1)}, bf16[1,48,896]{2,1,0:T(8,128)(2,1)S(1)}, u32[]{:S(2)}, u32[]{:S(2)}) collective-permute-start(bf16[1,48,896]{2,1,0:T(8,128)(2,1)S(1)} %get-tuple-element.350), channel_id=1, source_target_pairs={{0,8},{1,9},{2,10},{3,11},{4,12},{5,13},{6,14},{7,15},{8,0},{9,1},... | collective-permute-start | bytes 258056 | tf_op jit(solution)/shard_map/flip_second_zz/ppermute | solution.py:635
  (14 other events, 39.5 us)

commit v2 on v1

--- a/solution.py
+++ b/solution.py
@@ -201,10 +201,9 @@
 
 
 def feed_kernel(
-    g, chunk, extra, place, tokens, o, o_two, wo, wo_two, cotangent, gain, up, up_bias, down, *rest
+    g, chunk, place, tokens, o, o_two, wo, wo_two, cotangent, gain, up, up_bias, down, *rest
 ):
-    earlier, outs = rest[:extra], rest[extra:]
-    part_outs, outs = outs[:-7], outs[-7:]
+    part_outs, outs = rest[:-7], rest[-7:]
     active_out, hidden_grad_out, low_out, middle_out, down_part_out, up_bias_out, down_bias_out = outs
     rows = slice(g * S, (g + 1) * S)
     first = place[0] == 0
@@ -237,16 +236,14 @@
     for out in part_outs:
         out[...] = part[at : at + out.shape[0]].astype(B16)
         at += out.shape[0]
-    for i, r in enumerate(earlier):
-        down_part_out[i * S : (i + 1) * S, :] = r[...]
-    down_part_out[len(earlier) * S :, :] = down_part.astype(B16)
+    down_part_out[...] = down_part.astype(B16)
 
 
 def turn_kernel(
-    g, heads, cuts, cotangent, middle, gain, wo, wk, wv, o, saved, probs, side, mid, *rest
+    g, heads, cuts, last, cotangent, middle, gain, wo, wk, wv, o, saved, probs, side, mid, *rest
 ):
     parts, rest = rest[: 2 * cuts], rest[2 * cuts :]
-    earlier, outs = rest[:g], rest[g:]
+    earlier, outs = rest[:-8], rest[-8:]
     o_grad_out, delta_out, side_score_grad_out, part_out, grads_out, gain_out = outs[:6]
     middle_grad_out, middle_low_out = outs[6:]
     unit, rate = norm_parts(middle[...])
@@ -285,7 +282,8 @@
     side_unit, _ = norm_parts(mid[g * L : (g + 1) * L, :])
     gain_out[1:2, :] = jnp.sum(part * side_unit, axis=0, keepdims=True)
     gain_out[2:, :] = jnp.zeros_like(gain_out[2:, :])
-    part = jnp.concatenate([r[...] for r in earlier] + [part], axis=0)
+    if last:
+        part = jnp.concatenate([r[...] for r in earlier] + [part], axis=0)
     part_out[...] = part.astype(part_out.dtype)
 
 
@@ -350,18 +348,21 @@
         grad_out[rows, :] = middle_grad[g][...] + norm_back(grad, unit, rate, gain[...])
 
 
-def result_kernel(bias, part_one, part_two, *refs):
-    middle, out = refs[:-1], refs[-1]
-    for g in range(len(middle)):
-        rows = slice(g * S, (g + 1) * S)
-        total = part_one[rows, :].astype(F32) + part_two[rows, :].astype(F32)
-        out[rows, :] = (middle[g][...] + total + bias[...]).astype(B16)
+def result_kernel(middle, part_one, part_two, bias, *refs):
+    earlier, out = refs[:-1], refs[-1]
+    at = 0
+    for r in earlier:
+        out[at : at + S, :] = r[...]
+        at += S
+    total = part_one[...].astype(F32) + part_two[...].astype(F32)
+    out[at:, :] = (middle[...] + total + bias[...]).astype(B16)
 
 
 def latent_leave_kernel(me, latents, part_one, part_two, gain, mid_grad, grad_out, gain_out):
     own = latents.shape[0]
     unit, rate = norm_parts(latents[...].astype(F32))
-    total = part_one[...].astype(F32) + part_two[...].astype(F32)
+    start = part_one.shape[0] - own - 16
+    total = part_one[start:, :].astype(F32) + part_two[start:, :].astype(F32)
     grad_out[...] = mid_grad[...] + norm_back(total[:own], unit, rate, gain[...])
     share, model = gain_out.shape[1], gain.shape[1]
     row = lax.broadcasted_iota(jnp.int32, (share, model), 0)
@@ -370,50 +371,40 @@
     gain_out[...] = jnp.broadcast_to(jnp.sum(kept, axis=1, keepdims=True), (share, 8)).T
 
 
-def split_pairs(values, bit, share, send_out, keep_out, cut, keep_cut=None):
+def split_pairs(values, bit, share, send_out, keep_out):
     blocks = values.reshape(values.shape[0] // (2 * share), 2, share, values.shape[1])
     even, odd = blocks[:, 0], blocks[:, 1]
-    send_out[:, :, cut] = jnp.where(bit == 0, odd, even).astype(B16)
-    keep_cut = cut if keep_cut is None else keep_cut
-    keep_out[:, :, keep_cut] = jnp.where(bit == 0, even, odd).astype(B16)
-
-
-def weight_grad_kernel(groups, share, down_pieces, up_pieces, me, cotangent, *refs):
+    send_out[...] = jnp.where(bit == 0, odd, even).astype(B16)
+    keep_out[...] = jnp.where(bit == 0, even, odd).astype(B16)
+
+
+def weight_grad_kernel(groups, share, pieces, me, cotangent, *refs):
     active, low, hidden_grad = (refs[i * groups : (i + 1) * groups] for i in range(3))
     outs = refs[3 * groups :]
-    down_sends, up_sends = outs[:down_pieces], outs[down_pieces:-2]
-    down_keep, up_keep = outs[-2:]
     bit = me[0] % 2
     width = active[0].shape[1]
-    flat = [cotangent[g * S : (g + 1) * S, :].T for g in range(groups)]
-    low_flat = [r[...].T for r in low]
-
-    def total_of(lefts, rights, cut):
-        total = nn(lefts[0], rights[0][:, cut])
-        for g in range(1, groups):
-            total = total + nn(lefts[g], rights[g][:, cut])
-        return total
-
-    chunk = width // down_pieces
-    for k in range(down_pieces):
-        cut = slice(k * chunk, (k + 1) * chunk)
-        total = total_of(flat, active, cut)
-        split_pairs(total, bit, share, down_sends[k], down_keep, slice(0, chunk), cut)
-    chunk = width // up_pieces
-    for k in range(up_pieces):
-        cut = slice(k * chunk, (k + 1) * chunk)
-        total = total_of(low_flat, hidden_grad, cut)
-        split_pairs(total, bit, share, up_sends[k], up_keep, slice(0, chunk), cut)
-
-
-def attention_grad_kernel(groups, share, me, gain_one, gain_two, *refs):
-    saved, grads, middle_low, o, side, side_grads, up_bias, down_bias, gains = (
-        refs[i * groups : (i + 1) * groups] for i in range(9)
+    at = 0
+    for count, lefts, rights in (
+        (pieces[0], [cotangent[g * S : (g + 1) * S, :].T for g in range(groups)], active),
+        (pieces[1], [r[...].T for r in low], hidden_grad),
+    ):
+        chunk = width // count
+        for k in range(count):
+            cut = slice(k * chunk, (k + 1) * chunk)
+            total = nn(lefts[0], rights[0][:, cut])
+            for g in range(1, groups):
+                total = total + nn(lefts[g], rights[g][:, cut])
+            split_pairs(total, bit, share, outs[at], outs[at + 1])
+            at += 2
+
+
+def attention_grad_kernel(groups, share, me, *refs):
+    saved, grads, middle_low, o, side, side_grads = (
+        refs[i * groups : (i + 1) * groups] for i in range(6)
     )
-    *send_outs, keep_out = refs[9 * groups :]
+    outs = refs[6 * groups :]
     bit = me[0] % 2
     width = o[0].shape[1]
-    model = middle_low[0].shape[1]
     stack = [jnp.concatenate([r[...] for r in rs], axis=0) for rs in (side, side_grads)]
     side_low = stack[0][:, 2 * width :].astype(B16)
     side_k, side_v = stack[1][:, :width].astype(B16), stack[1][:, width:].astype(B16)
@@ -436,21 +427,29 @@
         total_of(low_flat, o, cut_of(0)),
     )
     for i, total in enumerate(totals):
-        split_pairs(total, bit, share, send_outs[i], keep_out, cut_of(0), cut_of(i))
+        split_pairs(total, bit, share, outs[2 * i], outs[2 * i + 1])
+
+
+def sum_of(parts):
+    total = parts[0]
+    for part in parts[1:]:
+        total = total + part
+    return total
+
+
+def vector_kernel(groups, share, me, one, two, *refs):
+    up_bias, down_bias, gains = (refs[i * groups : (i + 1) * groups] for i in range(3))
+    send_out, keep_out = refs[3 * groups :]
+    model = one.shape[1]
+    gain = one[...] + two[...]
 
     def column(rows):
         return jnp.broadcast_to(rows, (8, rows.shape[1])).T
-
-    def sum_of(parts):
-        total = parts[0]
-        for part in parts[1:]:
-            total = total + part
-        return total
 
     columns = [
         column(sum_of([r[...] for r in down_bias])),
         column(sum_of([r[0:1, :] for r in gains])),
-        column(gain_one[...] + gain_two[...]),
+        column(gain),
     ]
     bias = column(sum_of([r[...] for r in up_bias]))
     times = bias.shape[0] // model
@@ -460,23 +459,23 @@
     block = jnp.zeros((model, 128), F32)
     for i, one in enumerate(columns):
         block = jnp.where(lane == i, one[:, 0:1], block)
-    cut = slice(width, width + 128)
-    split_pairs(block, bit, share, send_outs[3], keep_out, cut, slice(4 * width, 4 * width + 128))
-
-
-def halve_kernel(shift, pieces, cuts, me, keep, *refs):
-    gots, outs = refs[: len(pieces)], refs[len(pieces) :]
+    split_pairs(block, me[0] % 2, share, send_out, keep_out)
+
+
+def halve_kernel(shift, pieces, cuts, me, *refs):
+    count = len(pieces)
+    keeps, gots, outs = refs[:count], refs[count : 2 * count], refs[2 * count :]
     bit = (me[0] // shift) % 2
-    for got, (first, last) in zip(gots, pieces):
+    for keep, got, (first, last) in zip(keeps, gots, pieces):
         for k, (start, end) in enumerate(cuts):
             low, high = max(first, start), min(last, end)
             if low >= high:
                 continue
-            of_got, of_out = slice(low - first, high - first), slice(low - start, high - start)
+            of_piece, of_out = slice(low - first, high - first), slice(low - start, high - start)
             for i in range(keep.shape[0]):
                 there, here = (
-                    keep[i, pl.ds(at, 1), :, low:high].astype(F32)
-                    + got[i, pl.ds(at, 1), :, of_got].astype(F32)
+                    keep[i, pl.ds(at, 1), :, of_piece].astype(F32)
+                    + got[i, pl.ds(at, 1), :, of_piece].astype(F32)
                     for at in (1 - bit, bit)
                 )
                 outs[2 * k][pl.ds(i, 1), :, of_out] = there.astype(B16)
@@ -491,7 +490,7 @@
 
 
 def latent_back_kernel(
-    heads, own, order, block, me, group_image, latents, q, k, v, mid_one, mid_two, gain, wq, wk, wv, wo,
+    heads, own, order, block, me, group_image, token_part, latents, q, k, v, mid_one, mid_two, gain, wq, wk, wv, wo,
     part_out, wq_out, wk_out, wv_out, wo_out, mixed, q_grad, k_grad, v_grad, images,
 ):
     mid_low = jnp.concatenate([mid_one[...], mid_two[...]], axis=0)
@@ -539,7 +538,9 @@
     v_grad[...] = v_sum.astype(B16)
     part = nt(q_grad[...], wq[...]) + nt(k_grad[...], wk[...]) + nt(v_grad[...], wv[...])
     gain_part = jnp.sum(part * unit, axis=0, keepdims=True)
-    part_out[...] = jnp.concatenate(
+    rows = token_part.shape[0]
+    part_out[:rows, :] = token_part[...]
+    part_out[rows:, :] = jnp.concatenate(
         [part[:own], jnp.broadcast_to(gain_part, (16, part.shape[1]))], axis=0
     ).astype(B16)
     share = wq_out.shape[0]
@@ -562,10 +563,10 @@
     def __init__(self, pinned):
         self.pinned, self.last = pinned, None
 
-    def call(self, kernel, name, outs, ins, scratch=(), limit=16, behind=()):
+    def call(self, kernel, name, outs, ins, scratch=(), limit=16, behind=(), loose=False):
         scalars = [isinstance(a, tuple) for a in ins]
         arrays = [a[1] if isinstance(a, tuple) else a for a in ins]
-        earlier = tuple(behind) + (() if self.last is None else (self.last,))
+        earlier = tuple(behind) + (() if self.last is None or loose else (self.last,))
         if earlier:
             least = min(range(len(arrays)), key=lambda i: arrays[i].size)
             arrays[least] = after(arrays[least], *earlier)
@@ -596,7 +597,8 @@
             cost_estimate=pl.CostEstimate(flops=0, bytes_accessed=0, transcendentals=0),
             name=name,
         )(*arrays)
-        self.last = min(results, key=lambda a: a.size)
+        if not loose:
+            self.last = min(results, key=lambda a: a.size)
         return results
 
     def load(self, *arrays, behind=()):
@@ -646,6 +648,13 @@
     return steps + [[1]]
 
 
+def one_by_one(steps):
+    result = []
+    for step in steps:
+        result += [[b] for b in step if b & (b - 1) == 0]
+    return result
+
+
 def gather_order(size):
     order = [0]
     for step in gather_steps(size):
@@ -674,44 +683,116 @@
 
 
 class Scatter:
-    def __init__(self, order, me, width, keep, send, name):
-        self.order, self.me, self.width, self.name = order, me, width, name
-        sends = send if isinstance(send, list) else [send]
-        self.keep, self.gots, self.pieces, at = keep, [flip(a, width, name) for a in sends], [], 0
-        for a in sends:
-            self.pieces.append((at, at + a.shape[2]))
-            at += a.shape[2]
-
-    def halve(self, cuts, behind=()):
-        n, share, _ = self.keep.shape
-        four = (n // 2, 2) + self.keep.shape[1:]
+    def __init__(self, order, me, width, keeps, sends, name):
+        self.order, self.me, self.width, self.keeps = order, me, width, list(keeps)
+        self.gots = [flip(a, width, name) for a in sends]
+        self.pieces, self.columns = [], 0
+        for a in self.keeps:
+            self.pieces.append((self.columns, self.columns + a.shape[2]))
+            self.columns += a.shape[2]
+
+    def halve(self, cuts=None, behind=()):
+        cuts = [(0, self.columns)] if cuts is None else cuts
+        n, share, _ = self.keeps[0].shape
         shapes = [(n // 2, share, end - start) for start, end in cuts]
         results = self.order.call(
             partial(halve_kernel, 2 * self.width, self.pieces, cuts),
             "halve",
             [out for shape in shapes for out in ((shape, B16), (shape, F32))],
-            [("smem", self.me), self.keep.reshape(four)]
-            + [a.reshape((n // 2, 2) + a.shape[1:]) for a in self.gots],
+            [("smem", self.me)]
+            + [a.reshape((n // 2, 2) + a.shape[1:]) for a in self.keeps + self.gots],
             behind=behind,
         )
         return results[::2], results[1::2]
 
-    def next(self, send, keep, name, *ties):
+    def next(self, name, *ties):
+        (send,), (keep,) = self.halve()
         send = after(send, *ties) if ties else send
-        return Scatter(self.order, self.me, 2 * self.width, keep, send, name)
-
-    def whole(self):
-        return [(0, self.keep.shape[2])]
+        return Scatter(self.order, self.me, 2 * self.width, [keep], [send], name)
 
     def finish(self, cuts):
-        share = self.keep.shape[1]
+        share = self.keeps[0].shape[1]
         shapes = [(8, share) if flat else (share, e - s) for s, e, flat in cuts]
         return self.order.call(
             partial(finish_kernel, cuts),
             "finish",
             [(shape, F32, OUT) for shape in shapes],
-            [self.keep, self.gots[0]],
-        )
+            self.keeps + self.gots,
+        )
+
+
+ORDER = (
+    "load_small",
+    "gather_0",
+    "load_first",
+    "gather_1",
+    "enter_0",
+    "enter_1",
+    "latent",
+    "load_feed",
+    "attend_0",
+    "attend_1",
+    "feed_0",
+    "feed_1",
+    "weight_grad",
+    "turn_0",
+    "down_y",
+    "turn_1",
+    "back_0",
+    "result_0",
+    "side",
+    "back_1",
+    "gather_mid_0",
+    "attention_grad",
+    "gather_mid_1",
+    "vectors",
+    "gather_mid_2",
+    "up_y",
+    "down_z",
+    "first_y",
+    "second_y",
+    "latent_back",
+    "down_zz",
+    "up_z",
+    "first_z",
+    "up_zz",
+    "down_done",
+    "first_zz",
+    "up_done",
+    "second_z",
+    "result_1",
+    "latent_leave",
+    "leave",
+    "second_zz",
+    "first_done",
+    "second_done",
+)
+SUMS = (
+    "weight_grad",
+    "down_y",
+    "attention_grad",
+    "vectors",
+    "up_y",
+    "down_z",
+    "first_y",
+    "second_y",
+    "down_zz",
+    "up_z",
+    "first_z",
+    "up_zz",
+    "down_done",
+    "first_zz",
+    "up_done",
+    "second_z",
+    "second_zz",
+    "first_done",
+    "second_done",
+)
+PIECES = (4, 2)
+TIE_UP = True
+TIE_DOWN_0 = "turn"
+TIE_DOWN_1 = "gain"
+MID_DIRECT = False
 
 
 def local(
@@ -756,9 +837,13 @@
     feed_gain_row = feed_gain.reshape(1, model)
     up_bias_row = up_bias.reshape(1, hidden_units)
     down_bias_row = down_bias.reshape(1, model)
+    scalars = (me_row, place)
+    gain_rows = (latent_gain_row, attention_gain_row, feed_gain_row, up_bias_row, down_bias_row)
     chain = Order(small)
     call = chain.call
     latent_limit = 16 if small else 56
+    gathered = gather_steps(size)
+    turns = tuple(gather_order(size))
 
     def join(parts):
         if not small:
@@ -766,138 +851,155 @@
         shape = (sum(p.shape[0] for p in parts), model)
         return call(join_kernel, "join", [(shape, B16)], parts)[0]
 
+    at = {}
     output_weight_two = swap_tp(output_weight, "output_weight")
-    gathered = gather_steps(size)
-    scalars = (me_row, place)
-    gain_rows = (latent_gain_row, attention_gain_row, feed_gain_row, up_bias_row, down_bias_row)
-    gathering = latents
-    (
-        tokens,
-        query_weight,
-        key_weight,
-        value_weight,
-        latents,
-        latent_cotangent,
-        output_weight,
-        *latent_weights,
-    ) = chain.load(
-        tokens,
-        query_weight,
-        key_weight,
-        value_weight,
-        latents,
-        latent_cotangent,
-        output_weight,
-        latent_query,
-        latent_key,
-        latent_value,
-        latent_output,
-        behind=scalars + gain_rows,
-    )
-    held = gathering
-    held_steps = []
-    for step in gathered[:-1]:
-        held = join([held] + [flip(held, b, "latents") for b in step])
-        held_steps.append(held)
-    turns = tuple(gather_order(size))
-    saved = []
-    for g in each:
-        saved += call(
+
+    def load_small():
+        at["latents_held"] = latents
+        at["latents"], at["latent_cotangent"] = chain.load(
+            latents, latent_cotangent, behind=scalars + gain_rows
+        )
+
+    def gather(name, steps, first):
+        held = at[name]
+        others = [flip(held, bits, name) for bits in steps]
+        at[name] = join([at["latents"] if first else held] + others)
+
+    def load_all():
+        at["tokens"], *weights = chain.load(
+            tokens,
+            query_weight,
+            key_weight,
+            value_weight,
+            output_weight,
+            latent_query,
+            latent_key,
+            latent_value,
+            latent_output,
+        )
+        at["group_weights"], at["output_weight"], at["latent_weights"] = (
+            weights[:3],
+            weights[3],
+            weights[4:],
+        )
+
+    def enter(g):
+        (at["saved", g],) = call(
             partial(enter_kernel, g),
             "enter",
             [((S, 3 * width + model), B16)],
-            [tokens, attention_gain_row, query_weight, key_weight, value_weight],
-            behind=held_steps[:1] if g == groups - 1 else (),
-        )
-    latents_one, latents_two = held, flip(after(held, saved[0]), 1, "latents")
-    latents_all, lat_q, lat_k, lat_v, latent_part = call(
-        partial(latent_kernel, heads, own, turns),
-        "latent",
-        [((everyone, model), B16)] + [((everyone, width), B16)] * 3 + [((own, model), B16)],
-        [
-            ("smem", me_row),
-            ("smem", group_image),
-            latents_one,
-            latents_two,
-            latent_gain_row,
-            *latent_weights,
-        ],
-        limit=latent_limit,
-    )
-    latent_part_two = swap_tp(latent_part, "latent_part")
-    up_weight, down_weight, token_cotangent = chain.load(up_weight, down_weight, token_cotangent)
-    o, probs, side, mids, mid_lows = zip(
-        *(
-            call(
-                partial(attend_kernel, g, heads),
-                "attend",
-                [
-                    ((S, width), B16),
-                    ((heads * L + 8, S), F32),
-                    ((L, 2 * width + model), F32),
-                    ((own, model), F32),
-                    ((own, model), B16, OUT),
-                ],
-                [
-                    saved[g],
-                    latents,
-                    latent_part,
-                    latent_part_two,
-                    attention_gain_row,
-                    key_weight,
-                    value_weight,
-                ],
-            )
-            for g in each
-        )
-    )
-    mid, mixed_latents = mids[0], mid_lows[0]
-    o_two = [swap_tp(a, "o") for a in o]
-    fed = []
-    cuts_of = [1 if g == groups - 1 else 2 for g in each]
-    for g in each:
+            [at["tokens"], attention_gain_row, *at["group_weights"]],
+        )
+
+    def latent():
+        held = at["latents_held"]
+        at["latents_all"], *at["latent_qkv"], at["latent_part"] = call(
+            partial(latent_kernel, heads, own, turns),
+            "latent",
+            [((everyone, model), B16)] + [((everyone, width), B16)] * 3 + [((own, model), B16)],
+            [
+                ("smem", me_row),
+                ("smem", group_image),
+                held,
+                flip(held, 1, "latents_held"),
+                latent_gain_row,
+                *at["latent_weights"],
+            ],
+            limit=latent_limit,
+        )
+        at["latent_part_two"] = swap_tp(at["latent_part"], "latent_part")
+
+    def load_feed():
+        at["up_weight"], at["down_weight"], at["cotangent"] = chain.load(
+            up_weight, down_weight, token_cotangent
+        )
+
+    def attend(g):
+        at["o", g], at["probs", g], at["side", g], mid, mid_low = call(
+            partial(attend_kernel, g, heads),
+            "attend",
+            [
+                ((S, width), B16),
+                ((heads * L + 8, S), F32),
+                ((L, 2 * width + model), F32),
+                ((own, model), F32),
+                ((own, model), B16, OUT),
+            ],
+            [
+                at["saved", g],
+                at["latents"],
+                at["latent_part"],
+                at["latent_part_two"],
+                attention_gain_row,
+                *at["group_weights"][1:],
+            ],
+        )
+        if g == 0:
+            at["mid"], at["mixed_latents"] = mid, mid_low
+        at["o_two", g] = swap_tp(at["o", g], "o")
+
+    def feed(g):
+        count = 1 if g == groups - 1 else 2
+        results = call(
+            partial(feed_kernel, g, hidden_units // 3),
+            "feed",
+            [((S // count, model), B16)] * count
+            + [
+                ((S, hidden_units), B16),
+                ((S, hidden_units), B16),
+                ((S, model), B16),
+                ((S, model), F32),
+                ((S, model), B16),
+                ((1, hidden_units), F32),
+                ((1, model), F32),
+            ],
+            [
+                ("smem", place),
+                at["tokens"],
+                at["o", g],
+                at["o_two", g],
+                at["output_weight"],
+                output_weight_two,
+                at["cotangent"],
+                feed_gain_row,
+                at["up_weight"],
+                up_bias_row,
+                at["down_weight"],
+            ],
+        )
+        at["feed_part", g] = results[:count]
+        names = ("active", "hidden_grad", "feed_low", "middle", "down_part", "up_bias", "down_bias")
+        for name, value in zip(names, results[count:]):
+            at[name, g] = value
+        at["feed_part_two", g] = [swap_tp(p, "feed_part") for p in results[:count]]
+
+    def weight_grad():
+        outs = []
+        for count in PIECES:
+            outs += [((size // 2, share, hidden_units // count), B16)] * (2 * count)
+        halves = call(
+            partial(weight_grad_kernel, groups, share, PIECES),
+            "weight_grad",
+            outs,
+            [("smem", me_row), at["cotangent"]]
+            + [at[name, g] for name in ("active", "feed_low", "hidden_grad") for g in each],
+        )
+        at["down_halves"], at["up_halves"] = halves[: 2 * PIECES[0]], halves[2 * PIECES[0] :]
+
+    def turn(g):
         last = g == groups - 1
-        fed.append(
-            call(
-                partial(feed_kernel, g, hidden_units // 3, g if last else 0),
-                "feed",
-                [((S // cuts_of[g], model), B16)] * cuts_of[g]
-                + [
-                    ((S, hidden_units), B16),
-                    ((S, hidden_units), B16),
-                    ((S, model), B16),
-                    ((S, model), F32),
-                    ((rows if last else S, model), B16),
-                    ((1, hidden_units), F32),
-                    ((1, model), F32),
-                ],
-                [
-                    ("smem", place),
-                    tokens,
-                    o[g],
-                    o_two[g],
-                    output_weight,
-                    output_weight_two,
-                    token_cotangent,
-                    feed_gain_row,
-                    up_weight,
-                    up_bias_row,
-                    down_weight,
-                ]
-                + ([f[-3] for f in fed] if last else []),
-            )
-        )
-    feed_part = [f[:-7] for f in fed]
-    active, hidden_grad, feed_low, middle, down_parts, up_bias_sum, down_bias_sum = zip(
-        *(f[-7:] for f in fed)
-    )
-    down_part = down_parts[-1]
-    feed_part_two = [[swap_tp(p, "feed_part") for p in parts] for parts in feed_part]
-
-    def turn(g, earlier):
-        last = g == groups - 1
-        return call(
-            partial(turn_kernel, g, heads, cuts_of[g]),
+        names = (
+            "o_grad",
+            "delta",
+            "side_score_grad",
+            "side_part",
+            "side_grads",
+            "gains",
+            "middle_grad",
+            "middle_low",
+        )
+        results = call(
+            partial(turn_kernel, g, heads, len(at["feed_part", g]), last),
             "turn",
             [
                 ((S, width), B16),
@@ -910,214 +1012,270 @@
                 ((S, model), B16),
             ],
             [
-                token_cotangent,
-                middle[g],
+                at["cotangent"],
+                at["middle", g],
                 feed_gain_row,
-                output_weight,
-                key_weight,
-                value_weight,
-                o[g],
-                saved[g],
-                probs[g],
-                side[g],
-                mid,
-            ]
-            + list(feed_part[g])
-            + feed_part_two[g]
-            + earlier,
-        )
-
-    if aligned:
-        down_pieces, up_pieces = 4, 2
-        half = (size // 2, share, hidden_units)
-        down_piece = (size // 2, share, hidden_units // down_pieces)
-        up_piece = (size // 2, share, hidden_units // up_pieces)
-        *sends, down_keep, up_keep = call(
-            partial(weight_grad_kernel, groups, share, down_pieces, up_pieces),
-            "weight_grad",
-            [(down_piece, B16)] * down_pieces + [(up_piece, B16)] * up_pieces + [(half, B16)] * 2,
-            [("smem", me_row), token_cotangent] + list(active + feed_low + hidden_grad),
-        )
-    turned = []
-    for g in each:
-        turned.append(turn(g, [t[3] for t in turned]))
-        if aligned and g == 0:
-            down_sends = [after(a, turned[0][1]) for a in sends[:down_pieces]]
-            down_sum = Scatter(chain, me_row, 1, down_keep, down_sends, "down_core")
-            (send,), (keep,) = down_sum.halve(down_sum.whole())
-            down_sum = down_sum.next(send, keep, "down_y")
-    (
-        o_grad,
-        delta,
-        side_score_grad,
-        side_parts,
-        side_grads,
-        gains,
-        middle_grad,
-        middle_low,
-    ) = zip(*turned)
-    side_part = side_parts[-1]
-    side_part_two = swap_tp(side_part, "side_part")
-    if aligned:
-        up_sends = [after(a, delta[-1]) for a in sends[down_pieces:]]
-        up_sum = Scatter(chain, me_row, 1, up_keep, up_sends, "up_core")
-    back = []
-    for g in each:
+                at["output_weight"],
+                *at["group_weights"][1:],
+                at["o", g],
+                at["saved", g],
+                at["probs", g],
+                at["side", g],
+                at["mid"],
+                *at["feed_part", g],
+                *at["feed_part_two", g],
+                *[at["side_part", i] for i in range(g)],
+            ],
+        )
+        for name, value in zip(names, results):
+            at[name, g] = value
+        if last:
+            at["side_part_two"] = swap_tp(at["side_part", g], "side_part")
+            if aligned:
+                sends = [after(a, at["delta", g]) for a in at["up_halves"][::2]]
+                at["up"] = Scatter(chain, me_row, 1, at["up_halves"][1::2], sends, "up_core")
+        elif aligned and g == 0:
+            sends = [after(a, at["delta", g]) for a in at["down_halves"][::2]]
+            at["down"] = Scatter(chain, me_row, 1, at["down_halves"][1::2], sends, "down_core")
+        if not last:
+            tie = at["delta", 0] if TIE_DOWN_0 == "turn" else at["middle", groups - 1]
+            at["down_part_two", g] = swap_tp(after(at["down_part", g], tie), "down_part")
+
+    def back(g):
         last = g == groups - 1
-        back.append(
-            call(
-                partial(attend_back_kernel, g, heads),
-                "attend_back",
-                [((rows if last else S, model), B16), ((S, 3 * width), B16), ((1, model), F32)],
-                [
-                    tokens,
-                    saved[g],
-                    o_grad[g],
-                    probs[g],
-                    delta[g],
-                    side_score_grad[g],
-                    side[g],
-                    query_weight,
-                    key_weight,
-                    value_weight,
-                    gains[g],
-                ]
-                + [b[2] for b in back[-1:]]
-                + ([b[0] for b in back] if last else []),
-            )
-        )
-        if g == 0:
-            if aligned:
-                up_sends, up_keeps = up_sum.halve(up_sum.whole())
-            mid_low, middle_latent_grad = call(
-                side_kernel,
-                "side",
-                [((own, model), B16), ((own, model), F32)],
-                [side_part, side_part_two, mid, latent_cotangent, attention_gain_row],
-            )
-    if aligned:
-        (send,), (keep,) = down_sum.halve(down_sum.whole())
-        up_sum = up_sum.next(up_sends[0], up_keeps[0], "up_y", down_sum.gots[0])
-        down_sum = down_sum.next(send, keep, "down_z")
-    held = mid_low
-    held_steps = []
-    for step in gathered[:-1]:
-        held = join([held] + [flip(held, b, "mid") for b in step])
-        held_steps.append(held)
-    mid_low_one, mid_low_two = held, flip(held, 1, "mid")
-    token_parts, grads, _ = zip(*back)
-    token_part = token_parts[-1]
-    gain_sum = back[-1][2]
-    gain_two = swap_tp(gain_sum, "gain")
-    token_part_two = swap_tp(after(token_part, gain_two), "token_part")
-    if aligned:
-        columns = 4 * width + 128
-        arrays = (saved, grads, middle_low, o, side, side_grads, up_bias_sum, down_bias_sum, gains)
-        *rest_sends, rest_keep = call(
+        at["token_part", g], at["grads", g], at["gain"] = call(
+            partial(attend_back_kernel, g, heads),
+            "attend_back",
+            [((rows if last else S, model), B16), ((S, 3 * width), B16), ((1, model), F32)],
+            [
+                at["tokens"],
+                at["saved", g],
+                at["o_grad", g],
+                at["probs", g],
+                at["delta", g],
+                at["side_score_grad", g],
+                at["side", g],
+                *at["group_weights"],
+                at["gains", g],
+                *([at["gain"]] if g else []),
+                *([at["token_part", i] for i in range(g)] if last else []),
+            ],
+        )
+        if last:
+            at["gain_two"] = swap_tp(at["gain"], "gain")
+            tie = {"gain": "gain_two", "back": "gain", "side": "side_part_two"}[TIE_DOWN_1]
+            at["down_part_two", g] = swap_tp(after(at["down_part", g], at[tie]), "down_part")
+
+    def result(g):
+        shape, kind = ((rows, model), (OUT,)) if g == groups - 1 else ((S, model), ())
+        (at["result", g],) = call(
+            result_kernel,
+            "result",
+            [(shape, B16) + kind],
+            [
+                at["middle", g],
+                at["down_part", g],
+                at["down_part_two", g],
+                down_bias_row,
+                *[at["result", i] for i in range(g)],
+            ],
+        )
+
+    def side():
+        at["mid_held"], at["middle_latent_grad"] = call(
+            side_kernel,
+            "side",
+            [((own, model), B16), ((own, model), F32)],
+            [
+                at["side_part", groups - 1],
+                at["side_part_two"],
+                at["mid"],
+                at["latent_cotangent"],
+                attention_gain_row,
+            ],
+        )
+
+    def attention_grad():
+        names = ("saved", "grads", "middle_low", "o", "side", "side_grads")
+        halves = call(
             partial(attention_grad_kernel, groups, share),
             "attention_grad",
-            [((size // 2, share, n), B16) for n in (width, width, width, width + 128, columns)],
-            [("smem", me_row), gain_sum, gain_two] + [a for of_groups in arrays for a in of_groups],
-        )
-        rest_sum = Scatter(chain, me_row, 1, rest_keep, rest_sends, "rest_core")
+            [((size // 2, share, width), B16)] * 8,
+            [("smem", me_row)] + [at[name, g] for name in names for g in each],
+        )
+        at["first"] = Scatter(chain, me_row, 1, halves[1:4:2], halves[:4:2], "first_core")
+        at["second_halves"] = halves[4:]
+
+    def vectors():
+        names = ("up_bias", "down_bias", "gains")
+        at["vector_halves"] = call(
+            partial(vector_kernel, groups, share),
+            "vectors",
+            [((size // 2, share, 128), B16)] * 2,
+            [("smem", me_row), at["gain"], at["gain_two"]]
+            + [at[name, g] for name in names for g in each],
+        )
+
+    def second_y():
+        halves = at["second_halves"] + at["vector_halves"]
+        at["second"] = Scatter(chain, me_row, 1, halves[1::2], halves[::2], "second_core")
+        advance("second", "second_y")
+
+    def advance(which, name, *ties):
+        at[which] = at[which].next(name, *ties)
+
+    def latent_back():
+        held = at["mid_held"]
+        block = min(everyone, max(16, 65536 // everyone))
+        at["all_part"], *at["latent_grads"] = call(
+            partial(latent_back_kernel, heads, own, turns, block),
+            "latent_back",
+            [((rows + own + 16, model), B16)] + [((share, width), F32, OUT)] * 4,
+            [
+                ("smem", me_row),
+                ("smem", group_image),
+                at["token_part", groups - 1],
+                at["latents_all"],
+                *at["latent_qkv"],
+                held,
+                flip(held, 1, "mid_held"),
+                latent_gain_row,
+                *at["latent_weights"],
+            ],
+            scratch=[pltpu.VMEM((everyone, width), B16)] * 4 + [pltpu.VMEM((everyone, 128), F32)],
+            limit=latent_limit,
+        )
+        at["all_part_two"] = swap_tp(at["all_part"], "all_part")
+
+    def latent_leave():
+        at["latent_grad"], at["latent_gain"] = call(
+            latent_leave_kernel,
+            "latent_leave",
+            [((own, model), F32, OUT), ((8, share), F32, OUT)],
+            [
+                ("smem", me_row),
+                at["latents"],
+                at["all_part"],
+                at["all_part_two"],
+                latent_gain_row,
+                at["middle_latent_grad"],
+            ],
+        )
+
+    def leave():
+        (at["token_grad"],) = call(
+            leave_kernel,
+            "leave",
+            [((rows, model), F32, OUT)],
+            [at["tokens"], attention_gain_row, at["all_part"], at["all_part_two"]]
+            + [at["middle_grad", g] for g in each],
+        )
+
+    def done(which, *cuts):
+        at[which, "done"] = at[which].finish(cuts)
+
+    steps = {
+        "load_small": load_small,
+        "load_first": load_all,
+        "latent": latent,
+        "load_feed": load_feed,
+        "weight_grad": weight_grad,
+        "side": side,
+        "attention_grad": attention_grad,
+        "vectors": vectors,
+        "second_y": second_y,
+        "latent_back": latent_back,
+        "latent_leave": latent_leave,
+        "leave": leave,
+        "down_done": partial(done, "down", (0, hidden_units, False)),
+        "up_done": partial(done, "up", (0, hidden_units, False)),
+        "first_done": partial(done, "first", (0, width, False), (width, 2 * width, False)),
+        "second_done": partial(
+            done,
+            "second",
+            (0, width, False),
+            (width, 2 * width, False),
+            (2 * width, 2 * width + 128, True),
+        ),
+    }
+    for name, which in (
+        ("down_y", "down"),
+        ("down_z", "down"),
+        ("down_zz", "down"),
+        ("up_z", "up"),
+        ("up_zz", "up"),
+        ("first_y", "first"),
+        ("first_z", "first"),
+        ("first_zz", "first"),
+        ("second_z", "second"),
+        ("second_zz", "second"),
+    ):
+        steps[name] = partial(advance, which, name)
+    steps["up_y"] = lambda: advance("up", "up_y", *(at["down"].gots if TIE_UP else ()))
+    for g in each:
+        for name, step in (
+            ("enter", enter),
+            ("attend", attend),
+            ("feed", feed),
+            ("turn", turn),
+            ("back", back),
+            ("result", result),
+        ):
+            steps[f"{name}_{g}"] = partial(step, g)
+    for i, bits in enumerate(gathered[:-1]):
+        steps[f"gather_{i}"] = partial(gather, "latents_held", bits, i == 0)
+    mid_steps = gathered[:-1] if MID_DIRECT else one_by_one(gathered[:-1])
+    for i, bits in enumerate(mid_steps):
+        steps[f"gather_mid_{i}"] = partial(gather, "mid_held", bits, False)
+    order = [name for name in ORDER if name in steps and (aligned or name not in SUMS)]
+    for name in steps:
+        if name not in order and (aligned or name not in SUMS):
+            kind, _, number = name.rpartition("_")
+            order.insert(order.index(f"{kind}_{int(number) - 1}") + 1, name)
+    for name in order:
+        steps[name]()
+    if aligned:
+        (down_done,), (up_done,) = at["down", "done"], at["up", "done"]
+        query_done, key_done = at["first", "done"]
+        value_done, output_done, vectors_done = at["second", "done"]
     else:
 
-        def flat(arrays, start, end):
-            return jnp.concatenate([a[:, start:end] for a in arrays], axis=0).astype(B16)
-
-        token_low = flat(saved, 3 * width, 3 * width + model)
-        side_low = flat(side, 2 * width, 2 * width + model)
+        def flat(name, start, end):
+            return jnp.concatenate([at[name, g][:, start:end] for g in each], axis=0).astype(B16)
+
+        token_low = flat("saved", 3 * width, 3 * width + model)
+        side_low = flat("side", 2 * width, 2 * width + model)
         products = (
-            tn(token_cotangent, flat(active, 0, hidden_units)),
-            tn(flat(feed_low, 0, model), flat(hidden_grad, 0, hidden_units)),
-            tn(token_low, flat(grads, 0, width)),
-            tn(token_low, flat(grads, width, 2 * width)) + tn(side_low, flat(side_grads, 0, width)),
-            tn(token_low, flat(grads, 2 * width, 3 * width))
-            + tn(side_low, flat(side_grads, width, 2 * width)),
-            tn(flat(middle_low, 0, model), flat(o, 0, width)),
-        )
-        vectors = [sum(down_bias_sum), sum(gains)[:1], gain_sum + gain_two]
-        vectors.append(sum(up_bias_sum).reshape(size, -1, share).swapaxes(0, 1).reshape(-1, model))
-        vectors = jnp.concatenate(vectors, axis=0)
-        total = jnp.concatenate([a.astype(B16) for a in products + (vectors.T,)], axis=1)
+            tn(token_cotangent, flat("active", 0, hidden_units)),
+            tn(flat("feed_low", 0, model), flat("hidden_grad", 0, hidden_units)),
+            tn(token_low, flat("grads", 0, width)),
+            tn(token_low, flat("grads", width, 2 * width))
+            + tn(side_low, flat("side_grads", 0, width)),
+            tn(token_low, flat("grads", 2 * width, 3 * width))
+            + tn(side_low, flat("side_grads", width, 2 * width)),
+            tn(flat("middle_low", 0, model), flat("o", 0, width)),
+        )
+        up_bias_rows = sum(at["up_bias", g] for g in each).reshape(size, -1, share)
+        rows_of = [
+            sum(at["down_bias", g] for g in each),
+            sum(at["gains", g] for g in each)[:1],
+            at["gain"] + at["gain_two"],
+            up_bias_rows.swapaxes(0, 1).reshape(-1, model),
+        ]
+        rows_of = jnp.concatenate(rows_of, axis=0)
+        total = jnp.concatenate([a.astype(B16) for a in products + (rows_of.T,)], axis=1)
         total = scatter_sum(total.reshape(size, share, -1))
-    block = min(everyone, max(16, 65536 // everyone))
-    latent_sum, latent_query_done, latent_key_done, latent_value_done, latent_output_done = call(
-        partial(latent_back_kernel, heads, own, turns, block),
-        "latent_back",
-        [((own + 16, model), B16)] + [((share, width), F32, OUT)] * 4,
-        [
-            ("smem", me_row),
-            ("smem", group_image),
-            latents_all,
-            lat_q,
-            lat_k,
-            lat_v,
-            mid_low_one,
-            mid_low_two,
-            latent_gain_row,
-            *latent_weights,
-        ],
-        scratch=[pltpu.VMEM((everyone, width), B16)] * 4 + [pltpu.VMEM((everyone, 128), F32)],
-        limit=latent_limit,
-    )
-    latent_sum_two = swap_tp(latent_sum, "latent_sum")
-    down_part_two = swap_tp(after(down_part, latent_sum), "down_part")
-    if aligned:
-        cuts = [(0, 2 * width), (2 * width, columns)]
-        rest_sends, rest_keeps = rest_sum.halve(cuts)
-        (send,), (keep,) = down_sum.halve(down_sum.whole())
-        down_sum = down_sum.next(send, keep, "down_zz")
-        (send,), (keep,) = up_sum.halve(up_sum.whole())
-        first = rest_sum.next(rest_sends[0], rest_keeps[0], "first_y", up_sum.gots[0])
-        up_sum = up_sum.next(send, keep, "up_z")
-    (token_grad,) = call(
-        leave_kernel,
-        "leave",
-        [((rows, model), F32, OUT)],
-        [tokens, attention_gain_row, token_part, token_part_two] + list(middle_grad),
-    )
-    latent_grad, latent_gain_sum = call(
-        latent_leave_kernel,
-        "latent_leave",
-        [((own, model), F32, OUT), ((8, share), F32, OUT)],
-        [("smem", me_row), latents, latent_sum, latent_sum_two, latent_gain_row, middle_latent_grad],
-    )
-    if aligned:
-        (down_done,) = down_sum.finish([(0, hidden_units, False)])
-        (send,), (keep,) = up_sum.halve(up_sum.whole())
-        up_sum = up_sum.next(send, keep, "up_zz")
-        (send,), (keep,) = first.halve(first.whole())
-        second = rest_sum.next(rest_sends[1], rest_keeps[1], "second_y", first.gots[0])
-        first = first.next(send, keep, "first_z")
-    (mixed_tokens,) = call(
-        result_kernel,
-        "result",
-        [((rows, model), B16, OUT)],
-        [down_bias_row, down_part, down_part_two] + list(middle),
-    )
-    if aligned:
-        (up_done,) = up_sum.finish([(0, hidden_units, False)])
-        (send,), (keep,) = first.halve(first.whole())
-        first = first.next(send, keep, "first_zz")
-        (send,), (keep,) = second.halve(second.whole())
-        second = second.next(send, keep, "second_z")
-        query_done, key_done = first.finish([(0, width, False), (width, 2 * width, False)])
-        (send,), (keep,) = second.halve(second.whole())
-        second = second.next(send, keep, "second_zz")
-        cuts = [(0, width, False), (width, 2 * width, False), (2 * width, 2 * width + 128, True)]
-        value_done, output_done, vectors = second.finish(cuts)
-    else:
         ends = [hidden_units, 2 * hidden_units] + [2 * hidden_units + i * width for i in range(1, 5)]
-        down_done, up_done, query_done, key_done, value_done, output_done, vectors = jnp.split(
+        down_done, up_done, query_done, key_done, value_done, output_done, vectors_done = jnp.split(
             total, ends, axis=1
         )
-        vectors = vectors.T
+        vectors_done = vectors_done.T
+    latent_query_done, latent_key_done, latent_value_done, latent_output_done = at["latent_grads"]
     return (
-        mixed_tokens,
-        mixed_latents,
-        token_grad,
-        latent_grad,
+        at["result", groups - 1],
+        at["mixed_latents"],
+        at["token_grad"],
+        at["latent_grad"],
         latent_query_done,
         latent_key_done,
         latent_value_done,
@@ -1127,12 +1285,12 @@
         value_done,
         output_done.T,
         up_done,
-        vectors[3 : 3 + hidden_units // model].reshape(-1),
+        vectors_done[3 : 3 + hidden_units // model].reshape(-1),
         down_done.T,
-        vectors[0],
-        latent_gain_sum[0],
-        vectors[2],
-        vectors[1],
+        vectors_done[0],
+        at["latent_gain"][0],
+        vectors_done[2],
+        vectors_done[1],
     )
 
 

time: 150 us -> 134 us (0.89)
  waiting for transfers between devices: 40.8 us -> 28.7 us
  starting transfers between devices: 51.4 us -> 46 us
    ppermute x12, waiting for transfers between devices: 13.2 us -> 5.8 us  [swap_tp(): return lax.ppermute(values, 'tp', [(0, 1), (1, 0)])]
    ppermute x32, starting transfers between devices: 34.8 us -> 29.8 us  [flip(): return lax.ppermute(values, 'dp', [(i, i ^ bits) for i in range(size)])]
    ppermute x32, waiting for transfers between devices: 27.6 us -> 22.9 us  [flip(): return lax.ppermute(values, 'dp', [(i, i ^ bits) for i in range(size)])]
    pallas_call x2 -> x3, Pallas kernels: 5.25 us -> 5.97 us  [load(): pl.pallas_call(load_kernel, out_shape=[pltpu.VMEM(a.shape, a.dtype) for a...]
    pallas_call x37 -> x41, Pallas kernels: 46.5 us -> 46.9 us  [call(): pl.pallas_call(kernel, out_shape=[result(*out) for out in outs], in_specs...]
  transfers between devices with their start and end apart: 44 -> 44, of which waited for: 19 -> 17; matrix products, arithmetic and copies ran while one was open for 3% -> 3% of each run, Pallas kernels for 31% -> 39%
where the time goes in v2:
time: 134 us
  Pallas kernels  52.9 us (39%)
  starting transfers between devices  46 us (34%)
  waiting for transfers between devices  28.7 us (21%)
  local copies, waits for them, and re-layouts  5.09 us (4%)
    pallas_call x41, Pallas kernels, call(): pl.pallas_call(kernel, out_shape=[result(*out) for out in outs], in_specs...  46.9 us
    ppermute x32, starting transfers between devices, flip(): return lax.ppermute(values, 'dp', [(i, i ^ bits) for i in range(size)])  29.8 us
    ppermute x32, waiting for transfers between devices, flip(): return lax.ppermute(values, 'dp', [(i, i ^ bits) for i in range(size)])  22.9 us
    ppermute x12, starting transfers between devices, swap_tp(): return lax.ppermute(values, 'tp', [(0, 1), (1, 0)])  16.2 us
    pallas_call x3, Pallas kernels, load(): pl.pallas_call(load_kernel, out_shape=[pltpu.VMEM(a.shape, a.dtype) for a...  5.97 us
    ppermute x12, waiting for transfers between devices, swap_tp(): return lax.ppermute(values, 'tp', [(0, 1), (1, 0)])  5.8 us
  transfers between devices with their start and end apart: 44, of which 17 were waited for; matrix products, arithmetic and copies ran while one was open for 3% of the time, Pallas kernels for 39%

profile of v2, /device:TPU:0, one launch (start us, length us, event | category | flops | bytes accessed | tf_op | source)
XLA Modules:
  0.0 133.6 jit_solution(16319620865919596718)
XLA Ops:
  0.7 3.0 %collective-permute-start.7 = (bf16[384,768]{1,0:T(8,128)(2,1)}, bf16[384,768]{1,0:T(8,128)(2,1)S(1)}, u32[]{:S(2)}, u32[]{:S(2)}) collective-permute-start(bf16[384,768]{1,0:T(8,128)(2,1)} %refs_4_.1), channel_id=1, source_target_pairs={{0,16},{16,0},{1,17},{17,1},{2,18},{18,2},{3,19},{19,3},{4,20},{20... | collective-permute-start | bytes 1769480 | tf_op jit(solution)/shard_map/swap_output_weight/ppermute | solution.py:631
  5.2 2.5 %collective-permute-start.2 = (bf16[16,768]{1,0:T(8,128)(2,1)}, bf16[16,768]{1,0:T(8,128)(2,1)S(1)}, u32[]{:S(2)}, u32[]{:S(2)}) collective-permute-start(bf16[16,768]{1,0:T(8,128)(2,1)} %refs_0_), channel_id=1, source_target_pairs={{0,12},{1,13},{2,14},{3,15},{4,8},{5,9},{6,10},{7,11},{8,4},{9,5},... | collective-permute-start | bytes 73736 | tf_op jit(solution)/shard_map/flip_latents_held/ppermute | solution.py:637
  12.9 1.6 %collective-permute-start.3 = (bf16[64,768]{1,0:T(8,128)(2,1)S(1)}, bf16[64,768]{1,0:T(8,128)(2,1)S(1)}, u32[]{:S(2)}, u32[]{:S(2)}) collective-permute-start(bf16[64,768]{1,0:T(8,128)(2,1)S(1)} %join.5.refs_0_), channel_id=1, source_target_pairs={{0,2},{1,3},{2,0},{3,1},{4,6},{5,7},{6,4},{7,5},{8,10},{9,11},{10,... | collective-permute-start | bytes 294920 | tf_op jit(solution)/shard_map/flip_latents_held/ppermute | solution.py:637
  14.5 2.6 %load.4 = (bf16[512,768]{1,0:T(8,128)(2,1)S(1)}, bf16[768,384]{1,0:T(8,128)(2,1)S(1)}, bf16[768,384]{1,0:T(8,128)(2,1)S(1)}, bf16[768,384]{1,0:T(8,128)(2,1)S(1)...) custom-call(bf16[512,768]{1,0:T(8,128)(2,1)} %refs_0_.1, ...), custom_call_target="tpu_custom_call" | custom-call | tf_op jit(solution)/shard_map/load/pallas_call | solution.py:611
  19.8 2.1 %latent.1 = (bf16[256,768]{1,0:T(8,128)(2,1)S(1)}, bf16[256,384]{1,0:T(8,128)(2,1)S(1)}, bf16[256,384]{1,0:T(8,128)(2,1)S(1)}, bf16[256,384]{1,0:T(8,128)(2,1)S(1)}, bf16[16,768]{1,0:T(8,128)(2,1)S(1)}) custom-call(s32[1]{0:T(128)} %bitcast.1.me, s32[32]{0:T(128)S(1)} %copy-done, bf16[128,768]{1,0:T(8,128)(2,1)S(1)} %join.6.one, ...), custom_call_target="tpu_custom_call" | custom-call | tf_op jit(solution)/shard_map/latent/pallas_call | solution.py:587
  22.4 2.6 %load.5 = (bf16[768,1536]{1,0:T(8,128)(2,1)S(1)}, bf16[1536,768]{1,0:T(8,128)(2,1)S(1)}, bf16[512,768]{1,0:T(8,128)(2,1)S(1)}) custom-call(bf16[768,1536]{1,0:T(8,128)(2,1)} %refs_0_.2, bf16[1536,768]{1,0:T(8,128)(2,1)} %refs_1_.5, bf16[512,768]{1,0:T(8,128)(2,1)} %refs_2_.3), custom_call_target="tpu_custom_call" | custom-call | tf_op jit(solution)/shard_map/load/pallas_call | solution.py:611
  25.7 1.9 %attend.2 = (bf16[256,384]{1,0:T(8,128)(2,1)S(1)}, f32[56,256]{1,0:T(8,128)S(1)}, f32[8,1536]{1,0:T(8,128)S(1)}, f32[16,768]{1,0:T(8,128)S(1)}, bf16[16,768]{1,0:T(8,128)(2,1)}) custom-call(bf16[256,1920]{1,0:T(8,128)(2,1)S(1)} %enter.2.saved.refs_0_, bf16[16,768]{1,0:T(8,128)(2,1)S(1)} %get-tuple-element.200.refs_0_.latents, ...), custom_call_target="tpu_custom_call" | custom-call | tf_op jit(solution)/shard_map/attend/pallas_call | solution.py:587
  28.4 1.9 %attend.3 = (bf16[256,384]{1,0:T(8,128)(2,1)S(1)}, f32[56,256]{1,0:T(8,128)S(1)}, f32[8,1536]{1,0:T(8,128)S(1)}, f32[16,768]{1,0:T(8,128)}, bf16[16,768]{1,0:T(8,128)(2,1)}) custom-call(bf16[256,1920]{1,0:T(8,128)(2,1)S(1)} %enter.3.saved.refs_1_, bf16[16,768]{1,0:T(8,128)(2,1)S(1)} %get-tuple-element.200.refs_0_.latents, ...), custom_call_target="tpu_custom_call" | custom-call | tf_op jit(solution)/shard_map/attend/pallas_call | solution.py:587
  31.5 3.4 %collective-permute-done.6.o_two = bf16[256,384]{1,0:T(8,128)(2,1)S(1)} collective-permute-done((bf16[256,384]{1,0:T(8,128)(2,1)S(1)}, bf16[256,384]{1,0:T(8,128)(2,1)S(1)}, u32[]{:S(2)}, u32[]{:S(2)}) %collective-permute-start.6) | collective-permute-done | bytes 196640 | tf_op jit(solution)/shard_map/swap_o/ppermute | solution.py:631
  35.0 4.2 %feed.2 = (bf16[128,768]{1,0:T(8,128)(2,1)S(1)}, bf16[128,768]{1,0:T(8,128)(2,1)S(1)}, bf16[256,1536]{1,0:T(8,128)(2,1)S(1)}, bf16[256,1536]{1,0:T(8,128)(2,1)S(...) custom-call(s32[1]{0:T(128)} %bitcast.place, ...), custom_call_target="tpu_custom_call" | custom-call | tf_op jit(solution)/shard_map/feed/pallas_call | solution.py:587
  41.2 4.4 %feed.3 = (bf16[256,768]{1,0:T(8,128)(2,1)S(1)}, bf16[256,1536]{1,0:T(8,128)(2,1)S(1)}, bf16[256,1536]{1,0:T(8,128)(2,1)S(1)}, bf16[256,768]{1,0:T(8,128)(2,1)S(...) custom-call(s32[1]{0:T(128)} %bitcast.place, ...), custom_call_target="tpu_custom_call" | custom-call | tf_op jit(solution)/shard_map/feed/pallas_call | solution.py:587
  46.9 3.1 %weight_grad.1 = (bf16[8,48,384]{2,1,0:T(8,128)(2,1)S(1)}, bf16[8,48,384]{2,1,0:T(8,128)(2,1)S(1)}, bf16[8,48,384]{2,1,0:T(8,128)(2,1)S(1)}, bf16[8,48,384]{2,1,...) custom-call(s32[1]{0:T(128)} %bitcast.1.me, ...), custom_call_target="tpu_custom_call" | custom-call | tf_op jit(solution)/shard_map/weight_grad/pallas_call | solution.py:587
  50.7 1.8 %turn.2 = (bf16[256,384]{1,0:T(8,128)(2,1)S(1)}, f32[8,256]{1,0:T(8,128)S(1)}, bf16[48,256]{1,0:T(8,128)(2,1)S(1)}, f32[8,768]{1,0:T(8,128)S(1)}, f32[8,768]{1,0...) custom-call(bf16[512,768]{1,0:T(8,128)(2,1)S(1)} %get-tuple-element.216.cotangent, ...), custom_call_target="tpu_custom_call" | custom-call | tf_op jit(solution)/shard_map/turn/pallas_call | solution.py:587
  54.2 1.7 %collective-permute-start.17 = (bf16[256,768]{1,0:T(8,128)(2,1)S(1)}, bf16[256,768]{1,0:T(8,128)(2,1)S(1)}, u32[]{:S(2)}, u32[]{:S(2)}) collective-permute-start(bf16[256,768]{1,0:T(8,128)(2,1)S(1)} %get-tuple-element.276.part_one), channel_id=1, source_target_pairs={{0,16},{16,0},{1,17},{17,1},{2,18},{18,2},{3,19},{19,3},{4,20},{20... | collective-permute-start | bytes 1179656 | tf_op jit(solution)/shard_map/swap_down_part/ppermute | solution.py:631
  56.8 1.8 %turn.3 = (bf16[256,384]{1,0:T(8,128)(2,1)S(1)}, f32[8,256]{1,0:T(8,128)S(1)}, bf16[48,256]{1,0:T(8,128)(2,1)S(1)}, bf16[16,768]{1,0:T(8,128)(2,1)S(1)}, f32[8,7...) custom-call(bf16[512,768]{1,0:T(8,128)(2,1)S(1)} %get-tuple-element.216.cotangent, ...), custom_call_target="tpu_custom_call" | custom-call | tf_op jit(solution)/shard_map/turn/pallas_call | solution.py:587
  60.8 1.7 %collective-permute-start.16 = (bf16[16,768]{1,0:T(8,128)(2,1)S(1)}, bf16[16,768]{1,0:T(8,128)(2,1)S(1)}, u32[]{:S(2)}, u32[]{:S(2)}) collective-permute-start(bf16[16,768]{1,0:T(8,128)(2,1)S(1)} %get-tuple-element.273.part_one), channel_id=1, source_target_pairs={{0,16},{16,0},{1,17},{17,1},{2,18},{18,2},{3,19},{19,3},{4,20},{20... | collective-permute-start | bytes 73736 | tf_op jit(solution)/shard_map/swap_side_part/ppermute | solution.py:631
  62.5 2.9 %attend_back.2 = (bf16[256,768]{1,0:T(8,128)(2,1)S(1)}, bf16[256,1152]{1,0:T(8,128)(2,1)S(1)}, f32[1,768]{1,0:T(1,128)S(1)}) custom-call(bf16[512,768]{1,0:T(8,128)(2,1)S(1)} %get-tuple-element.202.tokens, bf16[256,1920]{1,0:T(8,128)(2,1)S(1)} %enter.2.saved.refs_0_, bf16[256,384]{1,0:T(8,128)(2,1)S(1)} %get-tuple-element.268.o_grad, ...), custom_call_target="tpu_custom_call" | custom-call | tf_op jit(solution)/shard_map/attend_back/pallas_call | solution.py:587
  67.2 3.1 %attend_back.3 = (bf16[512,768]{1,0:T(8,128)(2,1)S(1)}, bf16[256,1152]{1,0:T(8,128)(2,1)S(1)}, f32[1,768]{1,0:T(1,128)S(1)}) custom-call(bf16[512,768]{1,0:T(8,128)(2,1)S(1)} %get-tuple-element.202.tokens, bf16[256,1920]{1,0:T(8,128)(2,1)S(1)} %enter.3.saved.refs_1_, bf16[256,384]{1,0:T(8,128)(2,1)S(1)} %get-tuple-element.264.o_grad, ...), custom_call_target="tpu_custom_call" | custom-call | tf_op jit(solution)/shard_map/attend_back/pallas_call | solution.py:587
  70.4 1.8 %collective-permute-start.21 = (bf16[32,768]{1,0:T(8,128)(2,1)S(1)}, bf16[32,768]{1,0:T(8,128)(2,1)S(1)}, u32[]{:S(2)}, u32[]{:S(2)}) collective-permute-start(bf16[32,768]{1,0:T(8,128)(2,1)S(1)} %join.7.refs_0_), channel_id=1, source_target_pairs={{0,8},{1,9},{2,10},{3,11},{4,12},{5,13},{6,14},{7,15},{8,0},{9,1},... | collective-permute-start | bytes 147464 | tf_op jit(solution)/shard_map/flip_mid_held/ppermute | solution.py:637
  72.1 1.7 %collective-permute-start.18 = (f32[1,768]{1,0:T(1,128)S(1)}, f32[1,768]{1,0:T(1,128)S(1)}, u32[]{:S(2)}, u32[]{:S(2)}) collective-permute-start(f32[1,768]{1,0:T(1,128)S(1)} %get-tuple-element.282.one), channel_id=1, source_target_pairs={{0,16},{16,0},{1,17},{17,1},{2,18},{18,2},{3,19},{19,3},{4,20},{20... | collective-permute-start | bytes 9224 | tf_op jit(solution)/shard_map/swap_gain/ppermute | solution.py:631
  73.8 2.1 %attention_grad.1 = (bf16[8,48,384]{2,1,0:T(8,128)(2,1)S(1)}, bf16[8,48,384]{2,1,0:T(8,128)(2,1)S(1)}, bf16[8,48,384]{2,1,0:T(8,128)(2,1)S(1)}, bf16[8,48,384]{2...) custom-call(s32[1]{0:T(128)} %bitcast.1.me, ...), custom_call_target="tpu_custom_call" | custom-call | tf_op jit(solution)/shard_map/attention_grad/pallas_call | solution.py:587
  78.3 2.4 %collective-permute-done.22.refs_1_ = bf16[64,768]{1,0:T(8,128)(2,1)S(1)} collective-permute-done((bf16[64,768]{1,0:T(8,128)(2,1)S(1)}, bf16[64,768]{1,0:T(8,128)(2,1)S(1)}, u32[]{:S(2)}, u32[]{:S(2)}) %collective-permute-start.22) | collective-permute-done | bytes 98336 | tf_op jit(solution)/shard_map/flip_mid_held/ppermute | solution.py:637
  85.6 5.9 %latent_back.1 = (bf16[544,768]{1,0:T(8,128)(2,1)S(1)}, f32[48,384]{1,0:T(8,128)}, f32[48,384]{1,0:T(8,128)}, f32[48,384]{1,0:T(8,128)}, f32[48,384]{1,0:T(8,128)}) custom-call(s32[1]{0:T(128)} %bitcast.1.me, s32[32]{0:T(128)S(1)} %copy-done, bf16[512,768]{1,0:T(8,128)(2,1)S(1)} %get-tuple-element.323.token_part, ...), custom_call_target="tpu_custom_call" | custom-call | tf_op jit(solution)/shard_map/latent_back/pallas_call | solution.py:587
  93.3 4.5 %collective-permute-done.33 = bf16[4,48,1536]{2,1,0:T(8,128)(2,1)S(1)} collective-permute-done((bf16[4,48,1536]{2,1,0:T(8,128)(2,1)S(1)}, bf16[4,48,1536]{2,1,0:T(8,128)(2,1)S(1)}, u32[]{:S(2)}, u32[]{:S(2)}) %collective-permute-start.33) | collective-permute-done | bytes 589856 | tf_op jit(solution)/shard_map/flip_up_y/ppermute | solution.py:637
  100.9 1.6 %collective-permute-start.36 = (bf16[1,48,1536]{2,1,0:T(8,128)(2,1)S(1)}, bf16[1,48,1536]{2,1,0:T(8,128)(2,1)S(1)}, u32[]{:S(2)}, u32[]{:S(2)}) collective-permute-start(bf16[1,48,1536]{2,1,0:T(8,128)(2,1)S(1)} %get-tuple-element.331), channel_id=1, source_target_pairs={{0,8},{1,9},{2,10},{3,11},{4,12},{5,13},{6,14},{7,15},{8,0},{9,1},... | collective-permute-start | bytes 442376 | tf_op jit(solution)/shard_map/flip_down_zz/ppermute | solution.py:637
  102.5 1.7 %collective-permute-done.34 = bf16[4,48,768]{2,1,0:T(8,128)(2,1)S(1)} collective-permute-done((bf16[4,48,768]{2,1,0:T(8,128)(2,1)S(1)}, bf16[4,48,768]{2,1,0:T(8,128)(2,1)S(1)}, u32[]{:S(2)}, u32[]{:S(2)}) %collective-permute-start.34) | collective-permute-done | bytes 294944 | tf_op jit(solution)/shard_map/flip_first_y/ppermute | solution.py:637
  105.4 4.3 %collective-permute-done.35 = bf16[2,48,1536]{2,1,0:T(8,128)(2,1)S(1)} collective-permute-done((bf16[2,48,1536]{2,1,0:T(8,128)(2,1)S(1)}, bf16[2,48,1536]{2,1,0:T(8,128)(2,1)S(1)}, u32[]{:S(2)}, u32[]{:S(2)}) %collective-permute-start.35) | collective-permute-done | bytes 294944 | tf_op jit(solution)/shard_map/flip_up_z/ppermute | solution.py:637
  109.8 3.7 %collective-permute-start.38 = (bf16[1,48,1536]{2,1,0:T(8,128)(2,1)S(1)}, bf16[1,48,1536]{2,1,0:T(8,128)(2,1)S(1)}, u32[]{:S(2)}, u32[]{:S(2)}) collective-permute-start(bf16[1,48,1536]{2,1,0:T(8,128)(2,1)S(1)} %get-tuple-element.343), channel_id=1, source_target_pairs={{0,8},{1,9},{2,10},{3,11},{4,12},{5,13},{6,14},{7,15},{8,0},{9,1},... | collective-permute-start | bytes 442376 | tf_op jit(solution)/shard_map/flip_up_zz/ppermute | solution.py:637
  114.8 3.9 %collective-permute-done.38.got = bf16[1,48,1536]{2,1,0:T(8,128)(2,1)S(1)} collective-permute-done((bf16[1,48,1536]{2,1,0:T(8,128)(2,1)S(1)}, bf16[1,48,1536]{2,1,0:T(8,128)(2,1)S(1)}, u32[]{:S(2)}, u32[]{:S(2)}) %collective-permute-start.38) | collective-permute-done | bytes 147488 | tf_op jit(solution)/shard_map/flip_up_zz/ppermute | solution.py:637
  119.7 2.4 %collective-permute-start.42 = (bf16[1,48,768]{2,1,0:T(8,128)(2,1)S(1)}, bf16[1,48,768]{2,1,0:T(8,128)(2,1)S(1)}, u32[]{:S(2)}, u32[]{:S(2)}) collective-permute-start(bf16[1,48,768]{2,1,0:T(8,128)(2,1)S(1)} %get-tuple-element.347), channel_id=1, source_target_pairs={{0,8},{1,9},{2,10},{3,11},{4,12},{5,13},{6,14},{7,15},{8,0},{9,1},... | collective-permute-start | bytes 221192 | tf_op jit(solution)/shard_map/flip_first_zz/ppermute | solution.py:637
  124.0 2.3 %leave.1 = f32[512,768]{1,0:T(8,128)} custom-call(bf16[512,768]{1,0:T(8,128)(2,1)S(1)} %get-tuple-element.202.tokens, f32[1,768]{1,0:T(1,128)S(1)} %reshape.179.gain, bf16[544,768]{1,0:T(8,128)(2,1)S(1)} %get-tuple-element.355.part_one, bf16[544,768]{1,0:T(8,128)(2,1)S(1)} %collective-permute-done.40.part_two, f32[256,768]{1,0:T(8,128)S(1)} %get-tuple-element.359.refs_0_, ...), custom_call_target="tpu_custom_call" | custom-call | tf_op jit(solution)/shard_map/leave/pallas_call | solution.py:587
  128.7 3.2 %collective-permute-done.43.got = bf16[1,48,896]{2,1,0:T(8,128)(2,1)S(1)} collective-permute-done((bf16[1,48,896]{2,1,0:T(8,128)(2,1)S(1)}, bf16[1,48,896]{2,1,0:T(8,128)(2,1)S(1)}, u32[]{:S(2)}, u32[]{:S(2)}) %collective-permute-start.43) | collective-permute-done | bytes 86048 | tf_op jit(solution)/shard_map/flip_second_zz/ppermute | solution.py:637
  (111 shorter events, 44.7 us)
Async XLA Ops:
  0.7 34.3 %collective-permute-start.7 = (bf16[384,768]{1,0:T(8,128)(2,1)}, bf16[384,768]{1,0:T(8,128)(2,1)S(1)}, u32[]{:S(2)}, u32[]{:S(2)}) collective-permute-start(bf16[384,768]{1,0:T(8,128)(2,1)} %refs_4_.1), channel_id=1, source_target_pairs={{0,16},{16,0},{1,17},{17,1},{2,18},{18,2},{3,19},{19,3},{4,20},{20... | collective-permute-start | bytes 1769480 | tf_op jit(solution)/shard_map/swap_output_weight/ppermute | solution.py:631
  3.7 8.4 %collective-permute-start = (bf16[16,768]{1,0:T(8,128)(2,1)}, bf16[16,768]{1,0:T(8,128)(2,1)S(1)}, u32[]{:S(2)}, u32[]{:S(2)}) collective-permute-start(bf16[16,768]{1,0:T(8,128)(2,1)} %refs_0_), channel_id=1, source_target_pairs={{0,4},{1,5},{2,6},{3,7},{4,0},{5,1},{6,2},{7,3},{8,12},{9,13},{10,... | collective-permute-start | bytes 73736 | tf_op jit(solution)/shard_map/flip_latents_held/ppermute | solution.py:637
  5.2 6.8 %collective-permute-start.2 = (bf16[16,768]{1,0:T(8,128)(2,1)}, bf16[16,768]{1,0:T(8,128)(2,1)S(1)}, u32[]{:S(2)}, u32[]{:S(2)}) collective-permute-start(bf16[16,768]{1,0:T(8,128)(2,1)} %refs_0_), channel_id=1, source_target_pairs={{0,12},{1,13},{2,14},{3,15},{4,8},{5,9},{6,10},{7,11},{8,4},{9,5},... | collective-permute-start | bytes 73736 | tf_op jit(solution)/shard_map/flip_latents_held/ppermute | solution.py:637
  7.7 5.2 %collective-permute-start.1 = (bf16[16,768]{1,0:T(8,128)(2,1)}, bf16[16,768]{1,0:T(8,128)(2,1)S(1)}, u32[]{:S(2)}, u32[]{:S(2)}) collective-permute-start(bf16[16,768]{1,0:T(8,128)(2,1)} %refs_0_), channel_id=1, source_target_pairs={{0,8},{1,9},{2,10},{3,11},{4,12},{5,13},{6,14},{7,15},{8,0},{9,1},... | collective-permute-start | bytes 73736 | tf_op jit(solution)/shard_map/flip_latents_held/ppermute | solution.py:637
  12.9 4.7 %collective-permute-start.3 = (bf16[64,768]{1,0:T(8,128)(2,1)S(1)}, bf16[64,768]{1,0:T(8,128)(2,1)S(1)}, u32[]{:S(2)}, u32[]{:S(2)}) collective-permute-start(bf16[64,768]{1,0:T(8,128)(2,1)S(1)} %join.5.refs_0_), channel_id=1, source_target_pairs={{0,2},{1,3},{2,0},{3,1},{4,6},{5,7},{6,4},{7,5},{8,10},{9,11},{10,... | collective-permute-start | bytes 294920 | tf_op jit(solution)/shard_map/flip_latents_held/ppermute | solution.py:637
  27.6 7.4 %collective-permute-start.6 = (bf16[256,384]{1,0:T(8,128)(2,1)S(1)}, bf16[256,384]{1,0:T(8,128)(2,1)S(1)}, u32[]{:S(2)}, u32[]{:S(2)}) collective-permute-start(bf16[256,384]{1,0:T(8,128)(2,1)S(1)} %get-tuple-element.222.o.refs_6_), channel_id=1, source_target_pairs={{0,16},{16,0},{1,17},{17,1},{2,18},{18,2},{3,19},{19,3},{4,20},{20... | collective-permute-start | bytes 589832 | tf_op jit(solution)/shard_map/swap_o/ppermute | solution.py:631
  30.3 10.9 %collective-permute-start.8 = (bf16[256,384]{1,0:T(8,128)(2,1)S(1)}, bf16[256,384]{1,0:T(8,128)(2,1)S(1)}, u32[]{:S(2)}, u32[]{:S(2)}) collective-permute-start(bf16[256,384]{1,0:T(8,128)(2,1)S(1)} %get-tuple-element.228.o.refs_7_), channel_id=1, source_target_pairs={{0,16},{16,0},{1,17},{17,1},{2,18},{18,2},{3,19},{19,3},{4,20},{20... | collective-permute-start | bytes 589832 | tf_op jit(solution)/shard_map/swap_o/ppermute | solution.py:631
  39.1 10.8 %collective-permute-start.9 = (bf16[128,768]{1,0:T(8,128)(2,1)S(1)}, bf16[128,768]{1,0:T(8,128)(2,1)S(1)}, u32[]{:S(2)}, u32[]{:S(2)}) collective-permute-start(bf16[128,768]{1,0:T(8,128)(2,1)S(1)} %get-tuple-element.244.rest_0_), channel_id=1, source_target_pairs={{0,16},{16,0},{1,17},{17,1},{2,18},{18,2},{3,19},{19,3},{4,20},{20... | collective-permute-start | bytes 589832 | tf_op jit(solution)/shard_map/swap_feed_part/ppermute | solution.py:631
  40.4 10.3 %collective-permute-start.10 = (bf16[128,768]{1,0:T(8,128)(2,1)S(1)}, bf16[128,768]{1,0:T(8,128)(2,1)S(1)}, u32[]{:S(2)}, u32[]{:S(2)}) collective-permute-start(bf16[128,768]{1,0:T(8,128)(2,1)S(1)} %get-tuple-element.245.rest_1_), channel_id=1, source_target_pairs={{0,16},{16,0},{1,17},{17,1},{2,18},{18,2},{3,19},{19,3},{4,20},{20... | collective-permute-start | bytes 589832 | tf_op jit(solution)/shard_map/swap_feed_part/ppermute | solution.py:631
  45.6 11.1 %collective-permute-start.15 = (bf16[256,768]{1,0:T(8,128)(2,1)S(1)}, bf16[256,768]{1,0:T(8,128)(2,1)S(1)}, u32[]{:S(2)}, u32[]{:S(2)}) collective-permute-start(bf16[256,768]{1,0:T(8,128)(2,1)S(1)} %get-tuple-element.262.rest_0_), channel_id=1, source_target_pairs={{0,16},{16,0},{1,17},{17,1},{2,18},{18,2},{3,19},{19,3},{4,20},{20... | collective-permute-start | bytes 1179656 | tf_op jit(solution)/shard_map/swap_feed_part/ppermute | solution.py:631
  54.2 11.4 %collective-permute-start.17 = (bf16[256,768]{1,0:T(8,128)(2,1)S(1)}, bf16[256,768]{1,0:T(8,128)(2,1)S(1)}, u32[]{:S(2)}, u32[]{:S(2)}) collective-permute-start(bf16[256,768]{1,0:T(8,128)(2,1)S(1)} %get-tuple-element.276.part_one), channel_id=1, source_target_pairs={{0,16},{16,0},{1,17},{17,1},{2,18},{18,2},{3,19},{19,3},{4,20},{20... | collective-permute-start | bytes 1179656 | tf_op jit(solution)/shard_map/swap_down_part/ppermute | solution.py:631
  58.6 22.1 %collective-permute-start.23 = (bf16[8,48,768]{2,1,0:T(8,128)(2,1)S(1)}, bf16[8,48,768]{2,1,0:T(8,128)(2,1)S(1)}, u32[]{:S(2)}, u32[]{:S(2)}) collective-permute-start(bf16[8,48,768]{2,1,0:T(8,128)(2,1)S(1)} %get-tuple-element.303), channel_id=1, source_target_pairs={{0,1},{1,0},{2,3},{3,2},{4,5},{5,4},{6,7},{7,6},{8,9},{9,8},{10,11... | collective-permute-start | bytes 1769480 | tf_op jit(solution)/shard_map/flip_up_core/ppermute | solution.py:637
  58.7 22.6 %collective-permute-start.24 = (bf16[8,48,768]{2,1,0:T(8,128)(2,1)S(1)}, bf16[8,48,768]{2,1,0:T(8,128)(2,1)S(1)}, u32[]{:S(2)}, u32[]{:S(2)}) collective-permute-start(bf16[8,48,768]{2,1,0:T(8,128)(2,1)S(1)} %get-tuple-element.305), channel_id=1, source_target_pairs={{0,1},{1,0},{2,3},{3,2},{4,5},{5,4},{6,7},{7,6},{8,9},{9,8},{10,11... | collective-permute-start | bytes 1769480 | tf_op jit(solution)/shard_map/flip_up_core/ppermute | solution.py:637
  59.2 22.4 %collective-permute-start.25 = (bf16[4,48,1536]{2,1,0:T(8,128)(2,1)S(1)}, bf16[4,48,1536]{2,1,0:T(8,128)(2,1)S(1)}, u32[]{:S(2)}, u32[]{:S(2)}) collective-permute-start(bf16[4,48,1536]{2,1,0:T(8,128)(2,1)S(1)} %get-tuple-element.259), channel_id=1, source_target_pairs={{0,2},{1,3},{2,0},{3,1},{4,6},{5,7},{6,4},{7,5},{8,10},{9,11},{10,... | collective-permute-start | bytes 1769480 | tf_op jit(solution)/shard_map/flip_down_y/ppermute | solution.py:637
  60.8 5.1 %collective-permute-start.16 = (bf16[16,768]{1,0:T(8,128)(2,1)S(1)}, bf16[16,768]{1,0:T(8,128)(2,1)S(1)}, u32[]{:S(2)}, u32[]{:S(2)}) collective-permute-start(bf16[16,768]{1,0:T(8,128)(2,1)S(1)} %get-tuple-element.273.part_one), channel_id=1, source_target_pairs={{0,16},{16,0},{1,17},{17,1},{2,18},{18,2},{3,19},{19,3},{4,20},{20... | collective-permute-start | bytes 73736 | tf_op jit(solution)/shard_map/swap_side_part/ppermute | solution.py:631
  70.4 5.7 %collective-permute-start.21 = (bf16[32,768]{1,0:T(8,128)(2,1)S(1)}, bf16[32,768]{1,0:T(8,128)(2,1)S(1)}, u32[]{:S(2)}, u32[]{:S(2)}) collective-permute-start(bf16[32,768]{1,0:T(8,128)(2,1)S(1)} %join.7.refs_0_), channel_id=1, source_target_pairs={{0,8},{1,9},{2,10},{3,11},{4,12},{5,13},{6,14},{7,15},{8,0},{9,1},... | collective-permute-start | bytes 147464 | tf_op jit(solution)/shard_map/flip_mid_held/ppermute | solution.py:637
  72.1 5.5 %collective-permute-start.18 = (f32[1,768]{1,0:T(1,128)S(1)}, f32[1,768]{1,0:T(1,128)S(1)}, u32[]{:S(2)}, u32[]{:S(2)}) collective-permute-start(f32[1,768]{1,0:T(1,128)S(1)} %get-tuple-element.282.one), channel_id=1, source_target_pairs={{0,16},{16,0},{1,17},{17,1},{2,18},{18,2},{3,19},{19,3},{4,20},{20... | collective-permute-start | bytes 9224 | tf_op jit(solution)/shard_map/swap_gain/ppermute | solution.py:631
  76.0 4.7 %collective-permute-start.22 = (bf16[64,768]{1,0:T(8,128)(2,1)S(1)}, bf16[64,768]{1,0:T(8,128)(2,1)S(1)}, u32[]{:S(2)}, u32[]{:S(2)}) collective-permute-start(bf16[64,768]{1,0:T(8,128)(2,1)S(1)} %join.8.refs_0_), channel_id=1, source_target_pairs={{0,2},{1,3},{2,0},{3,1},{4,6},{5,7},{6,4},{7,5},{8,10},{9,11},{10,... | collective-permute-start | bytes 294920 | tf_op jit(solution)/shard_map/flip_mid_held/ppermute | solution.py:637
  77.6 6.1 %collective-permute-start.27 = (bf16[8,48,384]{2,1,0:T(8,128)(2,1)S(1)}, bf16[8,48,384]{2,1,0:T(8,128)(2,1)S(1)}, u32[]{:S(2)}, u32[]{:S(2)}) collective-permute-start(bf16[8,48,384]{2,1,0:T(8,128)(2,1)S(1)} %get-tuple-element.313), channel_id=1, source_target_pairs={{0,1},{1,0},{2,3},{3,2},{4,5},{5,4},{6,7},{7,6},{8,9},{9,8},{10,11... | collective-permute-start | bytes 884744 | tf_op jit(solution)/shard_map/flip_first_core/ppermute | solution.py:637
  81.6 16.3 %collective-permute-start.33 = (bf16[4,48,1536]{2,1,0:T(8,128)(2,1)S(1)}, bf16[4,48,1536]{2,1,0:T(8,128)(2,1)S(1)}, u32[]{:S(2)}, u32[]{:S(2)}) collective-permute-start(bf16[4,48,1536]{2,1,0:T(8,128)(2,1)S(1)} %get-tuple-element.334), channel_id=1, source_target_pairs={{0,2},{1,3},{2,0},{3,1},{4,6},{5,7},{6,4},{7,5},{8,10},{9,11},{10,... | collective-permute-start | bytes 1769480 | tf_op jit(solution)/shard_map/flip_up_y/ppermute | solution.py:637
  83.8 9.4 %collective-permute-start.32 = (bf16[2,48,1536]{2,1,0:T(8,128)(2,1)S(1)}, bf16[2,48,1536]{2,1,0:T(8,128)(2,1)S(1)}, u32[]{:S(2)}, u32[]{:S(2)}) collective-permute-start(bf16[2,48,1536]{2,1,0:T(8,128)(2,1)S(1)} %get-tuple-element.309), channel_id=1, source_target_pairs={{0,4},{1,5},{2,6},{3,7},{4,0},{5,1},{6,2},{7,3},{8,12},{9,13},{10,... | collective-permute-start | bytes 884744 | tf_op jit(solution)/shard_map/flip_down_z/ppermute | solution.py:637
  91.5 31.6 %collective-permute-start.40 = (bf16[544,768]{1,0:T(8,128)(2,1)S(1)}, bf16[544,768]{1,0:T(8,128)(2,1)S(1)}, u32[]{:S(2)}, u32[]{:S(2)}) collective-permute-start(bf16[544,768]{1,0:T(8,128)(2,1)S(1)} %get-tuple-element.355.part_one), channel_id=1, source_target_pairs={{0,16},{16,0},{1,17},{17,1},{2,18},{18,2},{3,19},{19,3},{4,20},{20... | collective-permute-start | bytes 2506760 | tf_op jit(solution)/shard_map/swap_all_part/ppermute | solution.py:631
  92.5 11.7 %collective-permute-start.34 = (bf16[4,48,768]{2,1,0:T(8,128)(2,1)S(1)}, bf16[4,48,768]{2,1,0:T(8,128)(2,1)S(1)}, u32[]{:S(2)}, u32[]{:S(2)}) collective-permute-start(bf16[4,48,768]{2,1,0:T(8,128)(2,1)S(1)} %get-tuple-element.314), channel_id=1, source_target_pairs={{0,2},{1,3},{2,0},{3,1},{4,6},{5,7},{6,4},{7,5},{8,10},{9,11},{10,... | collective-permute-start | bytes 884744 | tf_op jit(solution)/shard_map/flip_first_y/ppermute | solution.py:637
  97.9 11.7 %collective-permute-start.35 = (bf16[2,48,1536]{2,1,0:T(8,128)(2,1)S(1)}, bf16[2,48,1536]{2,1,0:T(8,128)(2,1)S(1)}, u32[]{:S(2)}, u32[]{:S(2)}) collective-permute-start(bf16[2,48,1536]{2,1,0:T(8,128)(2,1)S(1)} %get-tuple-element.335), channel_id=1, source_target_pairs={{0,4},{1,5},{2,6},{3,7},{4,0},{5,1},{6,2},{7,3},{8,12},{9,13},{10,... | collective-permute-start | bytes 884744 | tf_op jit(solution)/shard_map/flip_up_z/ppermute | solution.py:637
  99.3 20.2 %collective-permute-start.39 = (bf16[4,48,896]{2,1,0:T(8,128)(2,1)S(1)}, bf16[4,48,896]{2,1,0:T(8,128)(2,1)S(1)}, u32[]{:S(2)}, u32[]{:S(2)}) collective-permute-start(bf16[4,48,896]{2,1,0:T(8,128)(2,1)S(1)} %get-tuple-element.321), channel_id=1, source_target_pairs={{0,2},{1,3},{2,0},{3,1},{4,6},{5,7},{6,4},{7,5},{8,10},{9,11},{10,... | collective-permute-start | bytes 1032200 | tf_op jit(solution)/shard_map/flip_second_y/ppermute | solution.py:637
  100.9 8.9 %collective-permute-start.36 = (bf16[1,48,1536]{2,1,0:T(8,128)(2,1)S(1)}, bf16[1,48,1536]{2,1,0:T(8,128)(2,1)S(1)}, u32[]{:S(2)}, u32[]{:S(2)}) collective-permute-start(bf16[1,48,1536]{2,1,0:T(8,128)(2,1)S(1)} %get-tuple-element.331), channel_id=1, source_target_pairs={{0,8},{1,9},{2,10},{3,11},{4,12},{5,13},{6,14},{7,15},{8,0},{9,1},... | collective-permute-start | bytes 442376 | tf_op jit(solution)/shard_map/flip_down_zz/ppermute | solution.py:637
  104.2 17.9 %collective-permute-start.19 = (bf16[256,768]{1,0:T(8,128)(2,1)S(1)}, bf16[256,768]{1,0:T(8,128)(2,1)S(1)}, u32[]{:S(2)}, u32[]{:S(2)}) collective-permute-start(bf16[256,768]{1,0:T(8,128)(2,1)S(1)} %get-tuple-element.283.part_one), channel_id=1, source_target_pairs={{0,16},{16,0},{1,17},{17,1},{2,18},{18,2},{3,19},{19,3},{4,20},{20... | collective-permute-start | bytes 1179656 | tf_op jit(solution)/shard_map/swap_down_part/ppermute | solution.py:631
  109.7 5.1 %collective-permute-start.37 = (bf16[2,48,768]{2,1,0:T(8,128)(2,1)S(1)}, bf16[2,48,768]{2,1,0:T(8,128)(2,1)S(1)}, u32[]{:S(2)}, u32[]{:S(2)}) collective-permute-start(bf16[2,48,768]{2,1,0:T(8,128)(2,1)S(1)} %get-tuple-element.338), channel_id=1, source_target_pairs={{0,4},{1,5},{2,6},{3,7},{4,0},{5,1},{6,2},{7,3},{8,12},{9,13},{10,... | collective-permute-start | bytes 442376 | tf_op jit(solution)/shard_map/flip_first_z/ppermute | solution.py:637
  109.8 9.0 %collective-permute-start.38 = (bf16[1,48,1536]{2,1,0:T(8,128)(2,1)S(1)}, bf16[1,48,1536]{2,1,0:T(8,128)(2,1)S(1)}, u32[]{:S(2)}, u32[]{:S(2)}) collective-permute-start(bf16[1,48,1536]{2,1,0:T(8,128)(2,1)S(1)} %get-tuple-element.343), channel_id=1, source_target_pairs={{0,8},{1,9},{2,10},{3,11},{4,12},{5,13},{6,14},{7,15},{8,0},{9,1},... | collective-permute-start | bytes 442376 | tf_op jit(solution)/shard_map/flip_up_zz/ppermute | solution.py:637
  119.6 6.8 %collective-permute-start.41 = (bf16[2,48,896]{2,1,0:T(8,128)(2,1)S(1)}, bf16[2,48,896]{2,1,0:T(8,128)(2,1)S(1)}, u32[]{:S(2)}, u32[]{:S(2)}) collective-permute-start(bf16[2,48,896]{2,1,0:T(8,128)(2,1)S(1)} %get-tuple-element.351), channel_id=1, source_target_pairs={{0,4},{1,5},{2,6},{3,7},{4,0},{5,1},{6,2},{7,3},{8,12},{9,13},{10,... | collective-permute-start | bytes 516104 | tf_op jit(solution)/shard_map/flip_second_z/ppermute | solution.py:637
  119.7 8.3 %collective-permute-start.42 = (bf16[1,48,768]{2,1,0:T(8,128)(2,1)S(1)}, bf16[1,48,768]{2,1,0:T(8,128)(2,1)S(1)}, u32[]{:S(2)}, u32[]{:S(2)}) collective-permute-start(bf16[1,48,768]{2,1,0:T(8,128)(2,1)S(1)} %get-tuple-element.347), channel_id=1, source_target_pairs={{0,8},{1,9},{2,10},{3,11},{4,12},{5,13},{6,14},{7,15},{8,0},{9,1},... | collective-permute-start | bytes 221192 | tf_op jit(solution)/shard_map/flip_first_zz/ppermute | solution.py:637
  126.4 5.4 %collective-permute-start.43 = (bf16[1,48,896]{2,1,0:T(8,128)(2,1)S(1)}, bf16[1,48,896]{2,1,0:T(8,128)(2,1)S(1)}, u32[]{:S(2)}, u32[]{:S(2)}) collective-permute-start(bf16[1,48,896]{2,1,0:T(8,128)(2,1)S(1)} %get-tuple-element.368), channel_id=1, source_target_pairs={{0,8},{1,9},{2,10},{3,11},{4,12},{5,13},{6,14},{7,15},{8,0},{9,1},... | collective-permute-start | bytes 258056 | tf_op jit(solution)/shard_map/flip_second_zz/ppermute | solution.py:637
  (13 other events, 33.7 us)

commit v3 on v2

--- a/solution.py
+++ b/solution.py
@@ -105,7 +105,7 @@
 
 def enter_kernel(g, tokens, gain, wq, wk, wv, saved_out):
     unit, _ = norm_parts(tokens[g * S : (g + 1) * S, :].astype(F32))
-    low = (unit * gain[...]).astype(B16)
+    low = (unit * gain[...].reshape(1, -1)).astype(B16)
     width = wq.shape[1]
     saved_out[:, :width] = nn(low, wq[...]).astype(B16)
     saved_out[:, width : 2 * width] = nn(low, wk[...]).astype(B16)
@@ -130,7 +130,7 @@
     latents = jnp.concatenate([one[...], two[...]], axis=0)
     latents_out[...] = latents
     unit, _ = norm_parts(latents.astype(F32))
-    low = (unit * gain[...]).astype(B16)
+    low = (unit * gain[...].reshape(1, -1)).astype(B16)
     q = nn(low, wq[...]).astype(B16)
     k = nn(low, wk[...]).astype(B16)
     v = nn(low, wv[...]).astype(B16)
@@ -160,7 +160,7 @@
     mid_out[...] = mid
     mid_low_out[...] = mid.astype(B16)
     unit, _ = norm_parts(mid[g * L : (g + 1) * L])
-    side_low = (unit * gain[...]).astype(B16)
+    side_low = (unit * gain[...].reshape(1, -1)).astype(B16)
     side_k = nn(side_low, wk[...]).astype(B16).astype(F32)
     side_v = nn(side_low, wv[...]).astype(B16).astype(F32)
     width = side_k.shape[1]
@@ -214,14 +214,14 @@
     middle = tokens[rows, :].astype(F32) + (nn(o_first, wo_first) + nn(o_second, wo_second))
     middle_out[...] = middle
     unit, _ = norm_parts(middle)
-    low = (unit * gain[...]).astype(B16)
+    low = (unit * gain[...].reshape(1, -1)).astype(B16)
     low_out[...] = low
     outer = cotangent[rows, :]
     down_bias_out[...] = jnp.sum(outer.astype(F32), axis=0, keepdims=True)
     part, down_part = None, None
     for start in range(0, up.shape[1], chunk):
         cut = slice(start, start + chunk)
-        hidden = nn(low, up[:, cut]) + up_bias[:, cut]
+        hidden = nn(low, up[:, cut]) + up_bias[cut].reshape(1, -1)
         active, slope = gelu_both(hidden)
         active = active.astype(B16)
         active_out[:, cut] = active
@@ -251,7 +251,7 @@
     grad = sides[0].astype(F32) + sides[1].astype(F32)
     gain_out[0:1, :] = jnp.sum(grad * unit, axis=0, keepdims=True)
     outer = cotangent[g * S : (g + 1) * S, :].astype(F32)
-    middle_grad = outer + norm_back(grad, unit, rate, gain[...])
+    middle_grad = outer + norm_back(grad, unit, rate, gain[...].reshape(1, -1))
     middle_grad_out[...] = middle_grad
     middle_low = middle_grad.astype(B16)
     middle_low_out[...] = middle_low
@@ -290,7 +290,7 @@
 def side_kernel(part_one, part_two, mid, cotangent, gain, low_out, grad_out):
     unit, rate = norm_parts(mid[...])
     part = part_one[...].astype(F32) + part_two[...].astype(F32)
-    grad = cotangent[...].astype(F32) + norm_back(part, unit, rate, gain[...])
+    grad = cotangent[...].astype(F32) + norm_back(part, unit, rate, gain[...].reshape(1, -1))
     grad_out[...] = grad
     low_out[...] = grad.astype(B16)
 
@@ -345,7 +345,7 @@
         rows = slice(g * S, (g + 1) * S)
         unit, rate = norm_parts(tokens[rows, :].astype(F32))
         grad = part_one[rows, :].astype(F32) + part_two[rows, :].astype(F32)
-        grad_out[rows, :] = middle_grad[g][...] + norm_back(grad, unit, rate, gain[...])
+        grad_out[rows, :] = middle_grad[g][...] + norm_back(grad, unit, rate, gain[...].reshape(1, -1))
 
 
 def result_kernel(middle, part_one, part_two, bias, *refs):
@@ -355,7 +355,7 @@
         out[at : at + S, :] = r[...]
         at += S
     total = part_one[...].astype(F32) + part_two[...].astype(F32)
-    out[at:, :] = (middle[...] + total + bias[...]).astype(B16)
+    out[at:, :] = (middle[...] + total + bias[...].reshape(1, -1)).astype(B16)
 
 
 def latent_leave_kernel(me, latents, part_one, part_two, gain, mid_grad, grad_out, gain_out):
@@ -363,8 +363,8 @@
     unit, rate = norm_parts(latents[...].astype(F32))
     start = part_one.shape[0] - own - 16
     total = part_one[start:, :].astype(F32) + part_two[start:, :].astype(F32)
-    grad_out[...] = mid_grad[...] + norm_back(total[:own], unit, rate, gain[...])
-    share, model = gain_out.shape[1], gain.shape[1]
+    grad_out[...] = mid_grad[...] + norm_back(total[:own], unit, rate, gain[...].reshape(1, -1))
+    share, model = gain_out.shape[1], gain.shape[0]
     row = lax.broadcasted_iota(jnp.int32, (share, model), 0)
     column = lax.broadcasted_iota(jnp.int32, (share, model), 1)
     kept = jnp.where(column == row + me[0] * share, total[own : own + 1], 0.0)
@@ -496,7 +496,7 @@
     mid_low = jnp.concatenate([mid_one[...], mid_two[...]], axis=0)
     o_grad = nt(mid_low, wo[...]).astype(B16)
     unit, _ = norm_parts(latents[...].astype(F32))
-    low = (unit * gain[...]).astype(B16)
+    low = (unit * gain[...].reshape(1, -1)).astype(B16)
     everyone = low.shape[0]
     images_row, images_column = image_rows(order, own // L, me[0], group_image)
 
@@ -725,8 +725,8 @@
     "load_small",
     "gather_0",
     "load_first",
+    "enter_0",
     "gather_1",
-    "enter_0",
     "enter_1",
     "latent",
     "load_feed",
@@ -832,13 +832,7 @@
     small = everyone <= 512
     aligned = share % 16 == 0 and size >= 8
     each = range(groups)
-    latent_gain_row = latent_gain.reshape(1, model)
-    attention_gain_row = attention_gain.reshape(1, model)
-    feed_gain_row = feed_gain.reshape(1, model)
-    up_bias_row = up_bias.reshape(1, hidden_units)
-    down_bias_row = down_bias.reshape(1, model)
     scalars = (me_row, place)
-    gain_rows = (latent_gain_row, attention_gain_row, feed_gain_row, up_bias_row, down_bias_row)
     chain = Order(small)
     call = chain.call
     latent_limit = 16 if small else 56
@@ -856,9 +850,19 @@
 
     def load_small():
         at["latents_held"] = latents
-        at["latents"], at["latent_cotangent"] = chain.load(
-            latents, latent_cotangent, behind=scalars + gain_rows
-        )
+        names = ("latents", "latent_cotangent", "latent_gain", "attention_gain", "feed_gain")
+        values = chain.load(
+            latents,
+            latent_cotangent,
+            latent_gain,
+            attention_gain,
+            feed_gain,
+            up_bias,
+            down_bias,
+            behind=scalars,
+        )
+        for name, value in zip(names + ("up_bias_row", "down_bias_row"), values):
+            at[name] = value
 
     def gather(name, steps, first):
         held = at[name]
@@ -888,7 +892,7 @@
             partial(enter_kernel, g),
             "enter",
             [((S, 3 * width + model), B16)],
-            [at["tokens"], attention_gain_row, *at["group_weights"]],
+            [at["tokens"], at["attention_gain"], *at["group_weights"]],
         )
 
     def latent():
@@ -902,7 +906,7 @@
                 ("smem", group_image),
                 held,
                 flip(held, 1, "latents_held"),
-                latent_gain_row,
+                at["latent_gain"],
                 *at["latent_weights"],
             ],
             limit=latent_limit,
@@ -930,7 +934,7 @@
                 at["latents"],
                 at["latent_part"],
                 at["latent_part_two"],
-                attention_gain_row,
+                at["attention_gain"],
                 *at["group_weights"][1:],
             ],
         )
@@ -961,9 +965,9 @@
                 at["output_weight"],
                 output_weight_two,
                 at["cotangent"],
-                feed_gain_row,
+                at["feed_gain"],
                 at["up_weight"],
-                up_bias_row,
+                at["up_bias_row"],
                 at["down_weight"],
             ],
         )
@@ -1014,7 +1018,7 @@
             [
                 at["cotangent"],
                 at["middle", g],
-                feed_gain_row,
+                at["feed_gain"],
                 at["output_weight"],
                 *at["group_weights"][1:],
                 at["o", g],
@@ -1076,7 +1080,7 @@
                 at["middle", g],
                 at["down_part", g],
                 at["down_part_two", g],
-                down_bias_row,
+                at["down_bias_row"],
                 *[at["result", i] for i in range(g)],
             ],
         )
@@ -1091,7 +1095,7 @@
                 at["side_part_two"],
                 at["mid"],
                 at["latent_cotangent"],
-                attention_gain_row,
+                at["attention_gain"],
             ],
         )
 
@@ -1139,7 +1143,7 @@
                 *at["latent_qkv"],
                 held,
                 flip(held, 1, "mid_held"),
-                latent_gain_row,
+                at["latent_gain"],
                 *at["latent_weights"],
             ],
             scratch=[pltpu.VMEM((everyone, width), B16)] * 4 + [pltpu.VMEM((everyone, 128), F32)],
@@ -1148,7 +1152,7 @@
         at["all_part_two"] = swap_tp(at["all_part"], "all_part")
 
     def latent_leave():
-        at["latent_grad"], at["latent_gain"] = call(
+        at["latent_grad"], at["latent_gain_sum"] = call(
             latent_leave_kernel,
             "latent_leave",
             [((own, model), F32, OUT), ((8, share), F32, OUT)],
@@ -1157,7 +1161,7 @@
                 at["latents"],
                 at["all_part"],
                 at["all_part_two"],
-                latent_gain_row,
+                at["latent_gain"],
                 at["middle_latent_grad"],
             ],
         )
@@ -1167,7 +1171,7 @@
             leave_kernel,
             "leave",
             [((rows, model), F32, OUT)],
-            [at["tokens"], attention_gain_row, at["all_part"], at["all_part_two"]]
+            [at["tokens"], at["attention_gain"], at["all_part"], at["all_part_two"]]
             + [at["middle_grad", g] for g in each],
         )
 
@@ -1255,12 +1259,12 @@
             + tn(side_low, flat("side_grads", width, 2 * width)),
             tn(flat("middle_low", 0, model), flat("o", 0, width)),
         )
-        up_bias_rows = sum(at["up_bias", g] for g in each).reshape(size, -1, share)
+        bias_rows = sum(at["up_bias", g] for g in each).reshape(size, -1, share)
         rows_of = [
             sum(at["down_bias", g] for g in each),
             sum(at["gains", g] for g in each)[:1],
             at["gain"] + at["gain_two"],
-            up_bias_rows.swapaxes(0, 1).reshape(-1, model),
+            bias_rows.swapaxes(0, 1).reshape(-1, model),
         ]
         rows_of = jnp.concatenate(rows_of, axis=0)
         total = jnp.concatenate([a.astype(B16) for a in products + (rows_of.T,)], axis=1)
@@ -1288,7 +1292,7 @@
         vectors_done[3 : 3 + hidden_units // model].reshape(-1),
         down_done.T,
         vectors_done[0],
-        at["latent_gain"][0],
+        at["latent_gain_sum"][0],
         vectors_done[2],
         vectors_done[1],
     )

time: 134 us -> 131 us (0.978)
  local copies, waits for them, and re-layouts: 5.09 us -> 1.63 us
  starting transfers between devices: 46 us -> 44.5 us
  waiting for transfers between devices: 28.7 us -> 30.2 us
    reshape x5 -> x0, local copies, waits for them, and re-layouts: 3.46 us -> none  [the longest x1 0.7 us: local(): up_bias_row = up_bias.reshape(1, hidden_units)]
    ppermute x32, starting transfers between devices: 29.8 us -> 26.7 us  [flip(): return lax.ppermute(values, 'dp', [(i, i ^ bits) for i in range(size)])]
    ppermute x32, waiting for transfers between devices: 22.9 us -> 24.8 us  [flip(): return lax.ppermute(values, 'dp', [(i, i ^ bits) for i in range(size)])]
    ppermute x12, starting transfers between devices: 16.2 us -> 17.8 us  [swap_tp(): return lax.ppermute(values, 'tp', [(0, 1), (1, 0)])]
  transfers between devices with their start and end apart: 44 -> 44, of which waited for: 17 -> 18; matrix products, arithmetic and copies ran while one was open for 3% -> 0% of each run, Pallas kernels for 39% -> 40%
where the time goes in v3:
time: 131 us; the launch traced here: 130 us
  Pallas kernels  53 us (40%)
  starting transfers between devices  44.5 us (34%)
  waiting for transfers between devices  30.2 us (23%)
  local copies, waits for them, and re-layouts  1.63 us (1%)
    pallas_call x41, Pallas kernels, call(): pl.pallas_call(kernel, out_shape=[result(*out) for out in outs], in_specs...  46.9 us
    ppermute x32, starting transfers between devices, flip(): return lax.ppermute(values, 'dp', [(i, i ^ bits) for i in range(size)])  26.7 us
    ppermute x32, waiting for transfers between devices, flip(): return lax.ppermute(values, 'dp', [(i, i ^ bits) for i in range(size)])  24.8 us
    ppermute x12, starting transfers between devices, swap_tp(): return lax.ppermute(values, 'tp', [(0, 1), (1, 0)])  17.8 us
    pallas_call x3, Pallas kernels, load(): pl.pallas_call(load_kernel, out_shape=[pltpu.VMEM(a.shape, a.dtype) for a...  6.04 us
    ppermute x12, waiting for transfers between devices, swap_tp(): return lax.ppermute(values, 'tp', [(0, 1), (1, 0)])  5.37 us
  transfers between devices with their start and end apart: 44, of which 18 were waited for; matrix products, arithmetic and copies ran while one was open for 0% of the time, Pallas kernels for 40%

profile of v3, /device:TPU:0, one launch (start us, length us, event | category | flops | bytes accessed | tf_op | source)
XLA Modules:
  0.0 130.3 jit_solution(15147123036846958917)
XLA Ops:
  0.7 3.0 %collective-permute-start.7 = (bf16[384,768]{1,0:T(8,128)(2,1)}, bf16[384,768]{1,0:T(8,128)(2,1)S(1)}, u32[]{:S(2)}, u32[]{:S(2)}) collective-permute-start(bf16[384,768]{1,0:T(8,128)(2,1)} %refs_4_.3), channel_id=1, source_target_pairs={{0,16},{16,0},{1,17},{17,1},{2,18},{18,2},{3,19},{19,3},{4,20},{20... | collective-permute-start | bytes 1769480 | tf_op jit(solution)/shard_map/swap_output_weight/ppermute | solution.py:631
  5.2 2.5 %collective-permute-start.2 = (bf16[16,768]{1,0:T(8,128)(2,1)}, bf16[16,768]{1,0:T(8,128)(2,1)S(1)}, u32[]{:S(2)}, u32[]{:S(2)}) collective-permute-start(bf16[16,768]{1,0:T(8,128)(2,1)} %refs_0_), channel_id=1, source_target_pairs={{0,12},{1,13},{2,14},{3,15},{4,8},{5,9},{6,10},{7,11},{8,4},{9,5},... | collective-permute-start | bytes 73736 | tf_op jit(solution)/shard_map/flip_latents_held/ppermute | solution.py:637
  8.7 2.5 %collective-permute-done.2.refs_3_ = bf16[16,768]{1,0:T(8,128)(2,1)S(1)} collective-permute-done((bf16[16,768]{1,0:T(8,128)(2,1)}, bf16[16,768]{1,0:T(8,128)(2,1)S(1)}, u32[]{:S(2)}, u32[]{:S(2)}) %collective-permute-start.2) | collective-permute-done | bytes 24608 | tf_op jit(solution)/shard_map/flip_latents_held/ppermute | solution.py:637
  11.2 1.8 %collective-permute-done.1.refs_2_ = bf16[16,768]{1,0:T(8,128)(2,1)S(1)} collective-permute-done((bf16[16,768]{1,0:T(8,128)(2,1)}, bf16[16,768]{1,0:T(8,128)(2,1)S(1)}, u32[]{:S(2)}, u32[]{:S(2)}) %collective-permute-start.1) | collective-permute-done | bytes 24608 | tf_op jit(solution)/shard_map/flip_latents_held/ppermute | solution.py:637
  14.5 2.6 %load.4 = (bf16[512,768]{1,0:T(8,128)(2,1)S(1)}, bf16[768,384]{1,0:T(8,128)(2,1)S(1)}, bf16[768,384]{1,0:T(8,128)(2,1)S(1)}, bf16[768,384]{1,0:T(8,128)(2,1)S(1)...) custom-call(bf16[512,768]{1,0:T(8,128)(2,1)} %refs_0_.1, ...), custom_call_target="tpu_custom_call" | custom-call | tf_op jit(solution)/shard_map/load/pallas_call | solution.py:611
  19.7 2.1 %latent.1 = (bf16[256,768]{1,0:T(8,128)(2,1)S(1)}, bf16[256,384]{1,0:T(8,128)(2,1)S(1)}, bf16[256,384]{1,0:T(8,128)(2,1)S(1)}, bf16[256,384]{1,0:T(8,128)(2,1)S(1)}, bf16[16,768]{1,0:T(8,128)(2,1)S(1)}) custom-call(s32[1]{0:T(128)} %bitcast.1.me, s32[32]{0:T(128)S(1)} %copy-done, bf16[128,768]{1,0:T(8,128)(2,1)S(1)} %join.6.one, ...), custom_call_target="tpu_custom_call" | custom-call | tf_op jit(solution)/shard_map/latent/pallas_call | solution.py:587
  22.4 2.6 %load.5 = (bf16[768,1536]{1,0:T(8,128)(2,1)S(1)}, bf16[1536,768]{1,0:T(8,128)(2,1)S(1)}, bf16[512,768]{1,0:T(8,128)(2,1)S(1)}) custom-call(bf16[768,1536]{1,0:T(8,128)(2,1)} %refs_0_.2, bf16[1536,768]{1,0:T(8,128)(2,1)} %refs_1_.5, bf16[512,768]{1,0:T(8,128)(2,1)} %refs_2_.5), custom_call_target="tpu_custom_call" | custom-call | tf_op jit(solution)/shard_map/load/pallas_call | solution.py:611
  25.6 1.9 %attend.2 = (bf16[256,384]{1,0:T(8,128)(2,1)S(1)}, f32[56,256]{1,0:T(8,128)S(1)}, f32[8,1536]{1,0:T(8,128)S(1)}, f32[16,768]{1,0:T(8,128)S(1)}, bf16[16,768]{1,0:T(8,128)(2,1)}) custom-call(bf16[256,1920]{1,0:T(8,128)(2,1)S(1)} %enter.2.saved.refs_0_, bf16[16,768]{1,0:T(8,128)(2,1)S(1)} %get-tuple-element.206.refs_0_.latents, ...), custom_call_target="tpu_custom_call" | custom-call | tf_op jit(solution)/shard_map/attend/pallas_call | solution.py:587
  28.3 1.9 %attend.3 = (bf16[256,384]{1,0:T(8,128)(2,1)S(1)}, f32[56,256]{1,0:T(8,128)S(1)}, f32[8,1536]{1,0:T(8,128)S(1)}, f32[16,768]{1,0:T(8,128)}, bf16[16,768]{1,0:T(8,128)(2,1)}) custom-call(bf16[256,1920]{1,0:T(8,128)(2,1)S(1)} %enter.3.saved.refs_1_, bf16[16,768]{1,0:T(8,128)(2,1)S(1)} %get-tuple-element.206.refs_0_.latents, ...), custom_call_target="tpu_custom_call" | custom-call | tf_op jit(solution)/shard_map/attend/pallas_call | solution.py:587
  31.5 3.1 %collective-permute-done.6.o_two = bf16[256,384]{1,0:T(8,128)(2,1)S(1)} collective-permute-done((bf16[256,384]{1,0:T(8,128)(2,1)S(1)}, bf16[256,384]{1,0:T(8,128)(2,1)S(1)}, u32[]{:S(2)}, u32[]{:S(2)}) %collective-permute-start.6) | collective-permute-done | bytes 196640 | tf_op jit(solution)/shard_map/swap_o/ppermute | solution.py:631
  34.6 4.2 %feed.2 = (bf16[128,768]{1,0:T(8,128)(2,1)S(1)}, bf16[128,768]{1,0:T(8,128)(2,1)S(1)}, bf16[256,1536]{1,0:T(8,128)(2,1)S(1)}, bf16[256,1536]{1,0:T(8,128)(2,1)S(...) custom-call(s32[1]{0:T(128)} %bitcast.place, ...), custom_call_target="tpu_custom_call" | custom-call | tf_op jit(solution)/shard_map/feed/pallas_call | solution.py:587
  40.8 4.4 %feed.3 = (bf16[256,768]{1,0:T(8,128)(2,1)S(1)}, bf16[256,1536]{1,0:T(8,128)(2,1)S(1)}, bf16[256,1536]{1,0:T(8,128)(2,1)S(1)}, bf16[256,768]{1,0:T(8,128)(2,1)S(...) custom-call(s32[1]{0:T(128)} %bitcast.place, ...), custom_call_target="tpu_custom_call" | custom-call | tf_op jit(solution)/shard_map/feed/pallas_call | solution.py:587
  46.9 3.1 %weight_grad.1 = (bf16[8,48,384]{2,1,0:T(8,128)(2,1)S(1)}, bf16[8,48,384]{2,1,0:T(8,128)(2,1)S(1)}, bf16[8,48,384]{2,1,0:T(8,128)(2,1)S(1)}, bf16[8,48,384]{2,1,...) custom-call(s32[1]{0:T(128)} %bitcast.1.me, ...), custom_call_target="tpu_custom_call" | custom-call | tf_op jit(solution)/shard_map/weight_grad/pallas_call | solution.py:587
  50.0 1.8 %turn.2 = (bf16[256,384]{1,0:T(8,128)(2,1)S(1)}, f32[8,256]{1,0:T(8,128)S(1)}, bf16[48,256]{1,0:T(8,128)(2,1)S(1)}, f32[8,768]{1,0:T(8,128)S(1)}, f32[8,768]{1,0...) custom-call(bf16[512,768]{1,0:T(8,128)(2,1)S(1)} %get-tuple-element.223.cotangent, ...), custom_call_target="tpu_custom_call" | custom-call | tf_op jit(solution)/shard_map/turn/pallas_call | solution.py:587
  53.5 1.7 %collective-permute-start.17 = (bf16[256,768]{1,0:T(8,128)(2,1)S(1)}, bf16[256,768]{1,0:T(8,128)(2,1)S(1)}, u32[]{:S(2)}, u32[]{:S(2)}) collective-permute-start(bf16[256,768]{1,0:T(8,128)(2,1)S(1)} %get-tuple-element.285.part_one), channel_id=1, source_target_pairs={{0,16},{16,0},{1,17},{17,1},{2,18},{18,2},{3,19},{19,3},{4,20},{20... | collective-permute-start | bytes 1179656 | tf_op jit(solution)/shard_map/swap_down_part/ppermute | solution.py:631
  56.0 1.8 %turn.3 = (bf16[256,384]{1,0:T(8,128)(2,1)S(1)}, f32[8,256]{1,0:T(8,128)S(1)}, bf16[48,256]{1,0:T(8,128)(2,1)S(1)}, bf16[16,768]{1,0:T(8,128)(2,1)S(1)}, f32[8,7...) custom-call(bf16[512,768]{1,0:T(8,128)(2,1)S(1)} %get-tuple-element.223.cotangent, ...), custom_call_target="tpu_custom_call" | custom-call | tf_op jit(solution)/shard_map/turn/pallas_call | solution.py:587
  59.3 1.7 %collective-permute-start.16 = (bf16[16,768]{1,0:T(8,128)(2,1)S(1)}, bf16[16,768]{1,0:T(8,128)(2,1)S(1)}, u32[]{:S(2)}, u32[]{:S(2)}) collective-permute-start(bf16[16,768]{1,0:T(8,128)(2,1)S(1)} %get-tuple-element.282.part_one), channel_id=1, source_target_pairs={{0,16},{16,0},{1,17},{17,1},{2,18},{18,2},{3,19},{19,3},{4,20},{20... | collective-permute-start | bytes 73736 | tf_op jit(solution)/shard_map/swap_side_part/ppermute | solution.py:631
  61.0 2.9 %attend_back.2 = (bf16[256,768]{1,0:T(8,128)(2,1)S(1)}, bf16[256,1152]{1,0:T(8,128)(2,1)S(1)}, f32[1,768]{1,0:T(1,128)S(1)}) custom-call(bf16[512,768]{1,0:T(8,128)(2,1)S(1)} %get-tuple-element.208.tokens, bf16[256,1920]{1,0:T(8,128)(2,1)S(1)} %enter.2.saved.refs_0_, bf16[256,384]{1,0:T(8,128)(2,1)S(1)} %get-tuple-element.277.o_grad, ...), custom_call_target="tpu_custom_call" | custom-call | tf_op jit(solution)/shard_map/attend_back/pallas_call | solution.py:587
  66.0 3.1 %attend_back.3 = (bf16[512,768]{1,0:T(8,128)(2,1)S(1)}, bf16[256,1152]{1,0:T(8,128)(2,1)S(1)}, f32[1,768]{1,0:T(1,128)S(1)}) custom-call(bf16[512,768]{1,0:T(8,128)(2,1)S(1)} %get-tuple-element.208.tokens, bf16[256,1920]{1,0:T(8,128)(2,1)S(1)} %enter.3.saved.refs_1_, bf16[256,384]{1,0:T(8,128)(2,1)S(1)} %get-tuple-element.273.o_grad, ...), custom_call_target="tpu_custom_call" | custom-call | tf_op jit(solution)/shard_map/attend_back/pallas_call | solution.py:587
  72.1 2.1 %attention_grad.1 = (bf16[8,48,384]{2,1,0:T(8,128)(2,1)S(1)}, bf16[8,48,384]{2,1,0:T(8,128)(2,1)S(1)}, bf16[8,48,384]{2,1,0:T(8,128)(2,1)S(1)}, bf16[8,48,384]{2...) custom-call(s32[1]{0:T(128)} %bitcast.1.me, ...), custom_call_target="tpu_custom_call" | custom-call | tf_op jit(solution)/shard_map/attention_grad/pallas_call | solution.py:587
  76.0 3.0 %collective-permute-done.22.refs_1_ = bf16[64,768]{1,0:T(8,128)(2,1)S(1)} collective-permute-done((bf16[64,768]{1,0:T(8,128)(2,1)S(1)}, bf16[64,768]{1,0:T(8,128)(2,1)S(1)}, u32[]{:S(2)}, u32[]{:S(2)}) %collective-permute-start.22) | collective-permute-done | bytes 98336 | tf_op jit(solution)/shard_map/flip_mid_held/ppermute | solution.py:637
  83.4 5.9 %latent_back.1 = (bf16[544,768]{1,0:T(8,128)(2,1)S(1)}, f32[48,384]{1,0:T(8,128)}, f32[48,384]{1,0:T(8,128)}, f32[48,384]{1,0:T(8,128)}, f32[48,384]{1,0:T(8,128)}) custom-call(s32[1]{0:T(128)} %bitcast.1.me, s32[32]{0:T(128)S(1)} %copy-done, bf16[512,768]{1,0:T(8,128)(2,1)S(1)} %get-tuple-element.333.token_part, ...), custom_call_target="tpu_custom_call" | custom-call | tf_op jit(solution)/shard_map/latent_back/pallas_call | solution.py:587
  89.3 1.7 %collective-permute-start.40 = (bf16[544,768]{1,0:T(8,128)(2,1)S(1)}, bf16[544,768]{1,0:T(8,128)(2,1)S(1)}, u32[]{:S(2)}, u32[]{:S(2)}) collective-permute-start(bf16[544,768]{1,0:T(8,128)(2,1)S(1)} %get-tuple-element.365.part_one), channel_id=1, source_target_pairs={{0,16},{16,0},{1,17},{17,1},{2,18},{18,2},{3,19},{19,3},{4,20},{20... | collective-permute-start | bytes 2506760 | tf_op jit(solution)/shard_map/swap_all_part/ppermute | solution.py:631
  92.1 4.0 %collective-permute-done.33 = bf16[4,48,1536]{2,1,0:T(8,128)(2,1)S(1)} collective-permute-done((bf16[4,48,1536]{2,1,0:T(8,128)(2,1)S(1)}, bf16[4,48,1536]{2,1,0:T(8,128)(2,1)S(1)}, u32[]{:S(2)}, u32[]{:S(2)}) %collective-permute-start.33) | collective-permute-done | bytes 589856 | tf_op jit(solution)/shard_map/flip_up_y/ppermute | solution.py:637
  98.6 1.8 %collective-permute-start.36 = (bf16[1,48,1536]{2,1,0:T(8,128)(2,1)S(1)}, bf16[1,48,1536]{2,1,0:T(8,128)(2,1)S(1)}, u32[]{:S(2)}, u32[]{:S(2)}) collective-permute-start(bf16[1,48,1536]{2,1,0:T(8,128)(2,1)S(1)} %get-tuple-element.341), channel_id=1, source_target_pairs={{0,8},{1,9},{2,10},{3,11},{4,12},{5,13},{6,14},{7,15},{8,0},{9,1},... | collective-permute-start | bytes 442376 | tf_op jit(solution)/shard_map/flip_down_zz/ppermute | solution.py:637
  100.4 2.1 %collective-permute-done.34 = bf16[4,48,768]{2,1,0:T(8,128)(2,1)S(1)} collective-permute-done((bf16[4,48,768]{2,1,0:T(8,128)(2,1)S(1)}, bf16[4,48,768]{2,1,0:T(8,128)(2,1)S(1)}, u32[]{:S(2)}, u32[]{:S(2)}) %collective-permute-start.34) | collective-permute-done | bytes 294944 | tf_op jit(solution)/shard_map/flip_first_y/ppermute | solution.py:637
  104.2 3.4 %collective-permute-done.35 = bf16[2,48,1536]{2,1,0:T(8,128)(2,1)S(1)} collective-permute-done((bf16[2,48,1536]{2,1,0:T(8,128)(2,1)S(1)}, bf16[2,48,1536]{2,1,0:T(8,128)(2,1)S(1)}, u32[]{:S(2)}, u32[]{:S(2)}) %collective-permute-start.35) | collective-permute-done | bytes 294944 | tf_op jit(solution)/shard_map/flip_up_z/ppermute | solution.py:637
  107.7 3.1 %collective-permute-start.38 = (bf16[1,48,1536]{2,1,0:T(8,128)(2,1)S(1)}, bf16[1,48,1536]{2,1,0:T(8,128)(2,1)S(1)}, u32[]{:S(2)}, u32[]{:S(2)}) collective-permute-start(bf16[1,48,1536]{2,1,0:T(8,128)(2,1)S(1)} %get-tuple-element.353), channel_id=1, source_target_pairs={{0,8},{1,9},{2,10},{3,11},{4,12},{5,13},{6,14},{7,15},{8,0},{9,1},... | collective-permute-start | bytes 442376 | tf_op jit(solution)/shard_map/flip_up_zz/ppermute | solution.py:637
  111.5 2.8 %collective-permute-done.37 = bf16[2,48,768]{2,1,0:T(8,128)(2,1)S(1)} collective-permute-done((bf16[2,48,768]{2,1,0:T(8,128)(2,1)S(1)}, bf16[2,48,768]{2,1,0:T(8,128)(2,1)S(1)}, u32[]{:S(2)}, u32[]{:S(2)}) %collective-permute-start.37) | collective-permute-done | bytes 147488 | tf_op jit(solution)/shard_map/flip_first_z/ppermute | solution.py:637
  116.8 1.9 %collective-permute-start.42 = (bf16[1,48,768]{2,1,0:T(8,128)(2,1)S(1)}, bf16[1,48,768]{2,1,0:T(8,128)(2,1)S(1)}, u32[]{:S(2)}, u32[]{:S(2)}) collective-permute-start(bf16[1,48,768]{2,1,0:T(8,128)(2,1)S(1)} %get-tuple-element.357), channel_id=1, source_target_pairs={{0,8},{1,9},{2,10},{3,11},{4,12},{5,13},{6,14},{7,15},{8,0},{9,1},... | collective-permute-start | bytes 221192 | tf_op jit(solution)/shard_map/flip_first_zz/ppermute | solution.py:637
  120.7 2.3 %leave.1 = f32[512,768]{1,0:T(8,128)} custom-call(bf16[512,768]{1,0:T(8,128)(2,1)S(1)} %get-tuple-element.208.tokens, f32[768]{0:T(1024)S(1)} %get-tuple-element.368.gain, bf16[544,768]{1,0:T(8,128)(2,1)S(1)} %get-tuple-element.365.part_one, bf16[544,768]{1,0:T(8,128)(2,1)S(1)} %collective-permute-done.40.part_two, ...), custom_call_target="tpu_custom_call" | custom-call | tf_op jit(solution)/shard_map/leave/pallas_call | solution.py:587
  125.8 2.7 %collective-permute-done.43.got = bf16[1,48,896]{2,1,0:T(8,128)(2,1)S(1)} collective-permute-done((bf16[1,48,896]{2,1,0:T(8,128)(2,1)S(1)}, bf16[1,48,896]{2,1,0:T(8,128)(2,1)S(1)}, u32[]{:S(2)}, u32[]{:S(2)}) %collective-permute-start.43) | collective-permute-done | bytes 86048 | tf_op jit(solution)/shard_map/flip_second_zz/ppermute | solution.py:637
  (106 shorter events, 43.9 us)
Async XLA Ops:
  0.7 33.9 %collective-permute-start.7 = (bf16[384,768]{1,0:T(8,128)(2,1)}, bf16[384,768]{1,0:T(8,128)(2,1)S(1)}, u32[]{:S(2)}, u32[]{:S(2)}) collective-permute-start(bf16[384,768]{1,0:T(8,128)(2,1)} %refs_4_.3), channel_id=1, source_target_pairs={{0,16},{16,0},{1,17},{17,1},{2,18},{18,2},{3,19},{19,3},{4,20},{20... | collective-permute-start | bytes 1769480 | tf_op jit(solution)/shard_map/swap_output_weight/ppermute | solution.py:631
  3.7 5.0 %collective-permute-start = (bf16[16,768]{1,0:T(8,128)(2,1)}, bf16[16,768]{1,0:T(8,128)(2,1)S(1)}, u32[]{:S(2)}, u32[]{:S(2)}) collective-permute-start(bf16[16,768]{1,0:T(8,128)(2,1)} %refs_0_), channel_id=1, source_target_pairs={{0,4},{1,5},{2,6},{3,7},{4,0},{5,1},{6,2},{7,3},{8,12},{9,13},{10,... | collective-permute-start | bytes 73736 | tf_op jit(solution)/shard_map/flip_latents_held/ppermute | solution.py:637
  5.2 5.9 %collective-permute-start.2 = (bf16[16,768]{1,0:T(8,128)(2,1)}, bf16[16,768]{1,0:T(8,128)(2,1)S(1)}, u32[]{:S(2)}, u32[]{:S(2)}) collective-permute-start(bf16[16,768]{1,0:T(8,128)(2,1)} %refs_0_), channel_id=1, source_target_pairs={{0,12},{1,13},{2,14},{3,15},{4,8},{5,9},{6,10},{7,11},{8,4},{9,5},... | collective-permute-start | bytes 73736 | tf_op jit(solution)/shard_map/flip_latents_held/ppermute | solution.py:637
  7.7 5.2 %collective-permute-start.1 = (bf16[16,768]{1,0:T(8,128)(2,1)}, bf16[16,768]{1,0:T(8,128)(2,1)S(1)}, u32[]{:S(2)}, u32[]{:S(2)}) collective-permute-start(bf16[16,768]{1,0:T(8,128)(2,1)} %refs_0_), channel_id=1, source_target_pairs={{0,8},{1,9},{2,10},{3,11},{4,12},{5,13},{6,14},{7,15},{8,0},{9,1},... | collective-permute-start | bytes 73736 | tf_op jit(solution)/shard_map/flip_latents_held/ppermute | solution.py:637
  12.9 5.3 %collective-permute-start.3 = (bf16[64,768]{1,0:T(8,128)(2,1)S(1)}, bf16[64,768]{1,0:T(8,128)(2,1)S(1)}, u32[]{:S(2)}, u32[]{:S(2)}) collective-permute-start(bf16[64,768]{1,0:T(8,128)(2,1)S(1)} %join.5.refs_0_), channel_id=1, source_target_pairs={{0,2},{1,3},{2,0},{3,1},{4,6},{5,7},{6,4},{7,5},{8,10},{9,11},{10,... | collective-permute-start | bytes 294920 | tf_op jit(solution)/shard_map/flip_latents_held/ppermute | solution.py:637
  27.5 7.0 %collective-permute-start.6 = (bf16[256,384]{1,0:T(8,128)(2,1)S(1)}, bf16[256,384]{1,0:T(8,128)(2,1)S(1)}, u32[]{:S(2)}, u32[]{:S(2)}) collective-permute-start(bf16[256,384]{1,0:T(8,128)(2,1)S(1)} %get-tuple-element.229.o.refs_6_), channel_id=1, source_target_pairs={{0,16},{16,0},{1,17},{17,1},{2,18},{18,2},{3,19},{19,3},{4,20},{20... | collective-permute-start | bytes 589832 | tf_op jit(solution)/shard_map/swap_o/ppermute | solution.py:631
  30.2 10.6 %collective-permute-start.8 = (bf16[256,384]{1,0:T(8,128)(2,1)S(1)}, bf16[256,384]{1,0:T(8,128)(2,1)S(1)}, u32[]{:S(2)}, u32[]{:S(2)}) collective-permute-start(bf16[256,384]{1,0:T(8,128)(2,1)S(1)} %get-tuple-element.237.o.refs_7_), channel_id=1, source_target_pairs={{0,16},{16,0},{1,17},{17,1},{2,18},{18,2},{3,19},{19,3},{4,20},{20... | collective-permute-start | bytes 589832 | tf_op jit(solution)/shard_map/swap_o/ppermute | solution.py:631
  38.8 11.2 %collective-permute-start.9 = (bf16[128,768]{1,0:T(8,128)(2,1)S(1)}, bf16[128,768]{1,0:T(8,128)(2,1)S(1)}, u32[]{:S(2)}, u32[]{:S(2)}) collective-permute-start(bf16[128,768]{1,0:T(8,128)(2,1)S(1)} %get-tuple-element.253.rest_0_), channel_id=1, source_target_pairs={{0,16},{16,0},{1,17},{17,1},{2,18},{18,2},{3,19},{19,3},{4,20},{20... | collective-permute-start | bytes 589832 | tf_op jit(solution)/shard_map/swap_feed_part/ppermute | solution.py:631
  40.4 9.6 %collective-permute-start.10 = (bf16[128,768]{1,0:T(8,128)(2,1)S(1)}, bf16[128,768]{1,0:T(8,128)(2,1)S(1)}, u32[]{:S(2)}, u32[]{:S(2)}) collective-permute-start(bf16[128,768]{1,0:T(8,128)(2,1)S(1)} %get-tuple-element.254.rest_1_), channel_id=1, source_target_pairs={{0,16},{16,0},{1,17},{17,1},{2,18},{18,2},{3,19},{19,3},{4,20},{20... | collective-permute-start | bytes 589832 | tf_op jit(solution)/shard_map/swap_feed_part/ppermute | solution.py:631
  45.3 10.7 %collective-permute-start.15 = (bf16[256,768]{1,0:T(8,128)(2,1)S(1)}, bf16[256,768]{1,0:T(8,128)(2,1)S(1)}, u32[]{:S(2)}, u32[]{:S(2)}) collective-permute-start(bf16[256,768]{1,0:T(8,128)(2,1)S(1)} %get-tuple-element.271.rest_0_), channel_id=1, source_target_pairs={{0,16},{16,0},{1,17},{17,1},{2,18},{18,2},{3,19},{19,3},{4,20},{20... | collective-permute-start | bytes 1179656 | tf_op jit(solution)/shard_map/swap_feed_part/ppermute | solution.py:631
  53.5 11.4 %collective-permute-start.17 = (bf16[256,768]{1,0:T(8,128)(2,1)S(1)}, bf16[256,768]{1,0:T(8,128)(2,1)S(1)}, u32[]{:S(2)}, u32[]{:S(2)}) collective-permute-start(bf16[256,768]{1,0:T(8,128)(2,1)S(1)} %get-tuple-element.285.part_one), channel_id=1, source_target_pairs={{0,16},{16,0},{1,17},{17,1},{2,18},{18,2},{3,19},{19,3},{4,20},{20... | collective-permute-start | bytes 1179656 | tf_op jit(solution)/shard_map/swap_down_part/ppermute | solution.py:631
  57.8 21.2 %collective-permute-start.23 = (bf16[8,48,768]{2,1,0:T(8,128)(2,1)S(1)}, bf16[8,48,768]{2,1,0:T(8,128)(2,1)S(1)}, u32[]{:S(2)}, u32[]{:S(2)}) collective-permute-start(bf16[8,48,768]{2,1,0:T(8,128)(2,1)S(1)} %get-tuple-element.313), channel_id=1, source_target_pairs={{0,1},{1,0},{2,3},{3,2},{4,5},{5,4},{6,7},{7,6},{8,9},{9,8},{10,11... | collective-permute-start | bytes 1769480 | tf_op jit(solution)/shard_map/flip_up_core/ppermute | solution.py:637
  57.9 21.7 %collective-permute-start.24 = (bf16[8,48,768]{2,1,0:T(8,128)(2,1)S(1)}, bf16[8,48,768]{2,1,0:T(8,128)(2,1)S(1)}, u32[]{:S(2)}, u32[]{:S(2)}) collective-permute-start(bf16[8,48,768]{2,1,0:T(8,128)(2,1)S(1)} %get-tuple-element.315), channel_id=1, source_target_pairs={{0,1},{1,0},{2,3},{3,2},{4,5},{5,4},{6,7},{7,6},{8,9},{9,8},{10,11... | collective-permute-start | bytes 1769480 | tf_op jit(solution)/shard_map/flip_up_core/ppermute | solution.py:637
  58.4 21.5 %collective-permute-start.25 = (bf16[4,48,1536]{2,1,0:T(8,128)(2,1)S(1)}, bf16[4,48,1536]{2,1,0:T(8,128)(2,1)S(1)}, u32[]{:S(2)}, u32[]{:S(2)}) collective-permute-start(bf16[4,48,1536]{2,1,0:T(8,128)(2,1)S(1)} %get-tuple-element.268), channel_id=1, source_target_pairs={{0,2},{1,3},{2,0},{3,1},{4,6},{5,7},{6,4},{7,5},{8,10},{9,11},{10,... | collective-permute-start | bytes 1769480 | tf_op jit(solution)/shard_map/flip_down_y/ppermute | solution.py:637
  59.3 5.9 %collective-permute-start.16 = (bf16[16,768]{1,0:T(8,128)(2,1)S(1)}, bf16[16,768]{1,0:T(8,128)(2,1)S(1)}, u32[]{:S(2)}, u32[]{:S(2)}) collective-permute-start(bf16[16,768]{1,0:T(8,128)(2,1)S(1)} %get-tuple-element.282.part_one), channel_id=1, source_target_pairs={{0,16},{16,0},{1,17},{17,1},{2,18},{18,2},{3,19},{19,3},{4,20},{20... | collective-permute-start | bytes 73736 | tf_op jit(solution)/shard_map/swap_side_part/ppermute | solution.py:631
  69.3 5.0 %collective-permute-start.21 = (bf16[32,768]{1,0:T(8,128)(2,1)S(1)}, bf16[32,768]{1,0:T(8,128)(2,1)S(1)}, u32[]{:S(2)}, u32[]{:S(2)}) collective-permute-start(bf16[32,768]{1,0:T(8,128)(2,1)S(1)} %join.7.refs_0_), channel_id=1, source_target_pairs={{0,8},{1,9},{2,10},{3,11},{4,12},{5,13},{6,14},{7,15},{8,0},{9,1},... | collective-permute-start | bytes 147464 | tf_op jit(solution)/shard_map/flip_mid_held/ppermute | solution.py:637
  70.4 4.9 %collective-permute-start.18 = (f32[1,768]{1,0:T(1,128)S(1)}, f32[1,768]{1,0:T(1,128)S(1)}, u32[]{:S(2)}, u32[]{:S(2)}) collective-permute-start(f32[1,768]{1,0:T(1,128)S(1)} %get-tuple-element.292.one), channel_id=1, source_target_pairs={{0,16},{16,0},{1,17},{17,1},{2,18},{18,2},{3,19},{19,3},{4,20},{20... | collective-permute-start | bytes 9224 | tf_op jit(solution)/shard_map/swap_gain/ppermute | solution.py:631
  74.3 4.7 %collective-permute-start.22 = (bf16[64,768]{1,0:T(8,128)(2,1)S(1)}, bf16[64,768]{1,0:T(8,128)(2,1)S(1)}, u32[]{:S(2)}, u32[]{:S(2)}) collective-permute-start(bf16[64,768]{1,0:T(8,128)(2,1)S(1)} %join.8.refs_0_), channel_id=1, source_target_pairs={{0,2},{1,3},{2,0},{3,1},{4,6},{5,7},{6,4},{7,5},{8,10},{9,11},{10,... | collective-permute-start | bytes 294920 | tf_op jit(solution)/shard_map/flip_mid_held/ppermute | solution.py:637
  75.3 6.1 %collective-permute-start.27 = (bf16[8,48,384]{2,1,0:T(8,128)(2,1)S(1)}, bf16[8,48,384]{2,1,0:T(8,128)(2,1)S(1)}, u32[]{:S(2)}, u32[]{:S(2)}) collective-permute-start(bf16[8,48,384]{2,1,0:T(8,128)(2,1)S(1)} %get-tuple-element.323), channel_id=1, source_target_pairs={{0,1},{1,0},{2,3},{3,2},{4,5},{5,4},{6,7},{7,6},{8,9},{9,8},{10,11... | collective-permute-start | bytes 884744 | tf_op jit(solution)/shard_map/flip_first_core/ppermute | solution.py:637
  79.9 16.3 %collective-permute-start.33 = (bf16[4,48,1536]{2,1,0:T(8,128)(2,1)S(1)}, bf16[4,48,1536]{2,1,0:T(8,128)(2,1)S(1)}, u32[]{:S(2)}, u32[]{:S(2)}) collective-permute-start(bf16[4,48,1536]{2,1,0:T(8,128)(2,1)S(1)} %get-tuple-element.344), channel_id=1, source_target_pairs={{0,2},{1,3},{2,0},{3,1},{4,6},{5,7},{6,4},{7,5},{8,10},{9,11},{10,... | collective-permute-start | bytes 1769480 | tf_op jit(solution)/shard_map/flip_up_y/ppermute | solution.py:637
  81.6 10.5 %collective-permute-start.32 = (bf16[2,48,1536]{2,1,0:T(8,128)(2,1)S(1)}, bf16[2,48,1536]{2,1,0:T(8,128)(2,1)S(1)}, u32[]{:S(2)}, u32[]{:S(2)}) collective-permute-start(bf16[2,48,1536]{2,1,0:T(8,128)(2,1)S(1)} %get-tuple-element.319), channel_id=1, source_target_pairs={{0,4},{1,5},{2,6},{3,7},{4,0},{5,1},{6,2},{7,3},{8,12},{9,13},{10,... | collective-permute-start | bytes 884744 | tf_op jit(solution)/shard_map/flip_down_z/ppermute | solution.py:637
  89.3 30.5 %collective-permute-start.40 = (bf16[544,768]{1,0:T(8,128)(2,1)S(1)}, bf16[544,768]{1,0:T(8,128)(2,1)S(1)}, u32[]{:S(2)}, u32[]{:S(2)}) collective-permute-start(bf16[544,768]{1,0:T(8,128)(2,1)S(1)} %get-tuple-element.365.part_one), channel_id=1, source_target_pairs={{0,16},{16,0},{1,17},{17,1},{2,18},{18,2},{3,19},{19,3},{4,20},{20... | collective-permute-start | bytes 2506760 | tf_op jit(solution)/shard_map/swap_all_part/ppermute | solution.py:631
  91.0 11.5 %collective-permute-start.34 = (bf16[4,48,768]{2,1,0:T(8,128)(2,1)S(1)}, bf16[4,48,768]{2,1,0:T(8,128)(2,1)S(1)}, u32[]{:S(2)}, u32[]{:S(2)}) collective-permute-start(bf16[4,48,768]{2,1,0:T(8,128)(2,1)S(1)} %get-tuple-element.324), channel_id=1, source_target_pairs={{0,2},{1,3},{2,0},{3,1},{4,6},{5,7},{6,4},{7,5},{8,10},{9,11},{10,... | collective-permute-start | bytes 884744 | tf_op jit(solution)/shard_map/flip_first_y/ppermute | solution.py:637
  96.2 11.4 %collective-permute-start.35 = (bf16[2,48,1536]{2,1,0:T(8,128)(2,1)S(1)}, bf16[2,48,1536]{2,1,0:T(8,128)(2,1)S(1)}, u32[]{:S(2)}, u32[]{:S(2)}) collective-permute-start(bf16[2,48,1536]{2,1,0:T(8,128)(2,1)S(1)} %get-tuple-element.345), channel_id=1, source_target_pairs={{0,4},{1,5},{2,6},{3,7},{4,0},{5,1},{6,2},{7,3},{8,12},{9,13},{10,... | collective-permute-start | bytes 884744 | tf_op jit(solution)/shard_map/flip_up_z/ppermute | solution.py:637
  97.7 18.7 %collective-permute-start.39 = (bf16[4,48,896]{2,1,0:T(8,128)(2,1)S(1)}, bf16[4,48,896]{2,1,0:T(8,128)(2,1)S(1)}, u32[]{:S(2)}, u32[]{:S(2)}) collective-permute-start(bf16[4,48,896]{2,1,0:T(8,128)(2,1)S(1)} %get-tuple-element.331), channel_id=1, source_target_pairs={{0,2},{1,3},{2,0},{3,1},{4,6},{5,7},{6,4},{7,5},{8,10},{9,11},{10,... | collective-permute-start | bytes 1032200 | tf_op jit(solution)/shard_map/flip_second_y/ppermute | solution.py:637
  98.6 9.1 %collective-permute-start.36 = (bf16[1,48,1536]{2,1,0:T(8,128)(2,1)S(1)}, bf16[1,48,1536]{2,1,0:T(8,128)(2,1)S(1)}, u32[]{:S(2)}, u32[]{:S(2)}) collective-permute-start(bf16[1,48,1536]{2,1,0:T(8,128)(2,1)S(1)} %get-tuple-element.341), channel_id=1, source_target_pairs={{0,8},{1,9},{2,10},{3,11},{4,12},{5,13},{6,14},{7,15},{8,0},{9,1},... | collective-permute-start | bytes 442376 | tf_op jit(solution)/shard_map/flip_down_zz/ppermute | solution.py:637
  102.5 16.2 %collective-permute-start.19 = (bf16[256,768]{1,0:T(8,128)(2,1)S(1)}, bf16[256,768]{1,0:T(8,128)(2,1)S(1)}, u32[]{:S(2)}, u32[]{:S(2)}) collective-permute-start(bf16[256,768]{1,0:T(8,128)(2,1)S(1)} %get-tuple-element.293.part_one), channel_id=1, source_target_pairs={{0,16},{16,0},{1,17},{17,1},{2,18},{18,2},{3,19},{19,3},{4,20},{20... | collective-permute-start | bytes 1179656 | tf_op jit(solution)/shard_map/swap_down_part/ppermute | solution.py:631
  107.6 6.7 %collective-permute-start.37 = (bf16[2,48,768]{2,1,0:T(8,128)(2,1)S(1)}, bf16[2,48,768]{2,1,0:T(8,128)(2,1)S(1)}, u32[]{:S(2)}, u32[]{:S(2)}) collective-permute-start(bf16[2,48,768]{2,1,0:T(8,128)(2,1)S(1)} %get-tuple-element.348), channel_id=1, source_target_pairs={{0,4},{1,5},{2,6},{3,7},{4,0},{5,1},{6,2},{7,3},{8,12},{9,13},{10,... | collective-permute-start | bytes 442376 | tf_op jit(solution)/shard_map/flip_first_z/ppermute | solution.py:637
  107.7 7.9 %collective-permute-start.38 = (bf16[1,48,1536]{2,1,0:T(8,128)(2,1)S(1)}, bf16[1,48,1536]{2,1,0:T(8,128)(2,1)S(1)}, u32[]{:S(2)}, u32[]{:S(2)}) collective-permute-start(bf16[1,48,1536]{2,1,0:T(8,128)(2,1)S(1)} %get-tuple-element.353), channel_id=1, source_target_pairs={{0,8},{1,9},{2,10},{3,11},{4,12},{5,13},{6,14},{7,15},{8,0},{9,1},... | collective-permute-start | bytes 442376 | tf_op jit(solution)/shard_map/flip_up_zz/ppermute | solution.py:637
  116.4 6.6 %collective-permute-start.41 = (bf16[2,48,896]{2,1,0:T(8,128)(2,1)S(1)}, bf16[2,48,896]{2,1,0:T(8,128)(2,1)S(1)}, u32[]{:S(2)}, u32[]{:S(2)}) collective-permute-start(bf16[2,48,896]{2,1,0:T(8,128)(2,1)S(1)} %get-tuple-element.361), channel_id=1, source_target_pairs={{0,4},{1,5},{2,6},{3,7},{4,0},{5,1},{6,2},{7,3},{8,12},{9,13},{10,... | collective-permute-start | bytes 516104 | tf_op jit(solution)/shard_map/flip_second_z/ppermute | solution.py:637
  116.8 8.3 %collective-permute-start.42 = (bf16[1,48,768]{2,1,0:T(8,128)(2,1)S(1)}, bf16[1,48,768]{2,1,0:T(8,128)(2,1)S(1)}, u32[]{:S(2)}, u32[]{:S(2)}) collective-permute-start(bf16[1,48,768]{2,1,0:T(8,128)(2,1)S(1)} %get-tuple-element.357), channel_id=1, source_target_pairs={{0,8},{1,9},{2,10},{3,11},{4,12},{5,13},{6,14},{7,15},{8,0},{9,1},... | collective-permute-start | bytes 221192 | tf_op jit(solution)/shard_map/flip_first_zz/ppermute | solution.py:637
  123.0 5.4 %collective-permute-start.43 = (bf16[1,48,896]{2,1,0:T(8,128)(2,1)S(1)}, bf16[1,48,896]{2,1,0:T(8,128)(2,1)S(1)}, u32[]{:S(2)}, u32[]{:S(2)}) collective-permute-start(bf16[1,48,896]{2,1,0:T(8,128)(2,1)S(1)} %get-tuple-element.378), channel_id=1, source_target_pairs={{0,8},{1,9},{2,10},{3,11},{4,12},{5,13},{6,14},{7,15},{8,0},{9,1},... | collective-permute-start | bytes 258056 | tf_op jit(solution)/shard_map/flip_second_zz/ppermute | solution.py:637
  (13 other events, 32.1 us)

commit v4 on v3

--- a/solution.py
+++ b/solution.py
@@ -311,6 +311,7 @@
         cut = slice(start, start + 2 * E)
         q_pair, k_pair, v_pair = pair_of(saved, pair, width)
         grad_pair = o_grad[:, cut]
+        k_flat = k_pair.T
         q_grads, k_grads, v_grads = [], [], []
         for second in (0, 1):
             h = 2 * pair + second
@@ -320,8 +321,8 @@
             score_grad = (weights * (prob_grad - delta[h : h + 1, :])).astype(B16)
             v_grads.append(nn(weights.astype(B16), grad_pair))
             k_grads.append(nn(score_grad, q_pair))
-            q_grads.append(tn(score_grad, k_pair))
-        q_pair_grad = jnp.where(first, q_grads[0], q_grads[1]) + side_q_grad[:, cut]
+            q_grads.append(nn(k_flat[second * E : (second + 1) * E], score_grad))
+        q_pair_grad = jnp.concatenate(q_grads, axis=0).T + side_q_grad[:, cut]
         k_pair_grad = jnp.where(first, k_grads[0], k_grads[1])
         v_pair_grad = jnp.where(first, v_grads[0], v_grads[1])
         grads_out[:, start : start + 2 * E] = (q_pair_grad * FACTOR).astype(B16)
@@ -364,11 +365,12 @@
     start = part_one.shape[0] - own - 16
     total = part_one[start:, :].astype(F32) + part_two[start:, :].astype(F32)
     grad_out[...] = mid_grad[...] + norm_back(total[:own], unit, rate, gain[...].reshape(1, -1))
-    share, model = gain_out.shape[1], gain.shape[0]
+    share, model = gain_out.shape[0], gain.shape[0]
     row = lax.broadcasted_iota(jnp.int32, (share, model), 0)
     column = lax.broadcasted_iota(jnp.int32, (share, model), 1)
     kept = jnp.where(column == row + me[0] * share, total[own : own + 1], 0.0)
-    gain_out[...] = jnp.broadcast_to(jnp.sum(kept, axis=1, keepdims=True), (share, 8)).T
+    sums = jnp.broadcast_to(jnp.sum(kept, axis=1, keepdims=True), (share, 8))
+    gain_out[...] = sums.T[:1].reshape(share)
 
 
 def split_pairs(values, bit, share, send_out, keep_out):
@@ -486,7 +488,13 @@
     total = keep[0] + got[0].astype(F32)
     for out, (start, end, flat) in zip(outs, cuts):
         part = total[:, start:end]
-        out[...] = part.T[: out.shape[0]] if flat else part
+        if flat:
+            rows = part.T
+            share = rows.shape[1]
+            for i in range(out.shape[0] // share):
+                out[i * share : (i + 1) * share] = rows[i : i + 1, :].reshape(share)
+        else:
+            out[...] = part
 
 
 def latent_back_kernel(
@@ -712,7 +720,7 @@
 
     def finish(self, cuts):
         share = self.keeps[0].shape[1]
-        shapes = [(8, share) if flat else (share, e - s) for s, e, flat in cuts]
+        shapes = [(flat * share,) if flat else (share, e - s) for s, e, flat in cuts]
         return self.order.call(
             partial(finish_kernel, cuts),
             "finish",
@@ -757,14 +765,14 @@
     "first_z",
     "up_zz",
     "down_done",
+    "up_done",
     "first_zz",
-    "up_done",
     "second_z",
+    "leave",
     "result_1",
     "latent_leave",
-    "leave",
+    "first_done",
     "second_zz",
-    "first_done",
     "second_done",
 )
 SUMS = (
@@ -790,9 +798,10 @@
 )
 PIECES = (4, 2)
 TIE_UP = True
-TIE_DOWN_0 = "turn"
+TIE_DOWN_0 = "feed"
 TIE_DOWN_1 = "gain"
 MID_DIRECT = False
+FEED_CHUNKS = 3
 
 
 def local(
@@ -945,7 +954,7 @@
     def feed(g):
         count = 1 if g == groups - 1 else 2
         results = call(
-            partial(feed_kernel, g, hidden_units // 3),
+            partial(feed_kernel, g, hidden_units // FEED_CHUNKS),
             "feed",
             [((S // count, model), B16)] * count
             + [
@@ -1155,7 +1164,7 @@
         at["latent_grad"], at["latent_gain_sum"] = call(
             latent_leave_kernel,
             "latent_leave",
-            [((own, model), F32, OUT), ((8, share), F32, OUT)],
+            [((own, model), F32, OUT), ((share,), F32, OUT)],
             [
                 ("smem", me_row),
                 at["latents"],
@@ -1191,15 +1200,18 @@
         "latent_back": latent_back,
         "latent_leave": latent_leave,
         "leave": leave,
-        "down_done": partial(done, "down", (0, hidden_units, False)),
-        "up_done": partial(done, "up", (0, hidden_units, False)),
-        "first_done": partial(done, "first", (0, width, False), (width, 2 * width, False)),
+        "down_done": partial(done, "down", (0, hidden_units, 0)),
+        "up_done": partial(done, "up", (0, hidden_units, 0)),
+        "first_done": partial(done, "first", (0, width, 0), (width, 2 * width, 0)),
         "second_done": partial(
             done,
             "second",
-            (0, width, False),
-            (width, 2 * width, False),
-            (2 * width, 2 * width + 128, True),
+            (0, width, 0),
+            (width, 2 * width, 0),
+            (2 * width, 2 * width + 128, 1),
+            (2 * width + 1, 2 * width + 128, 1),
+            (2 * width + 2, 2 * width + 128, 1),
+            (2 * width + 3, 2 * width + 128, hidden_units // model),
         ),
     }
     for name, which in (
@@ -1230,7 +1242,7 @@
         steps[f"gather_{i}"] = partial(gather, "latents_held", bits, i == 0)
     mid_steps = gathered[:-1] if MID_DIRECT else one_by_one(gathered[:-1])
     for i, bits in enumerate(mid_steps):
-        steps[f"gather_mid_{i}"] = partial(gather, "mid_held", bits, False)
+        steps[f"gather_mid_{i}"] = partial(gather, "mid_held", bits, 0)
     order = [name for name in ORDER if name in steps and (aligned or name not in SUMS)]
     for name in steps:
         if name not in order and (aligned or name not in SUMS):
@@ -1241,7 +1253,7 @@
     if aligned:
         (down_done,), (up_done,) = at["down", "done"], at["up", "done"]
         query_done, key_done = at["first", "done"]
-        value_done, output_done, vectors_done = at["second", "done"]
+        value_done, output_done, *vectors_done = at["second", "done"]
     else:
 
         def flat(name, start, end):
@@ -1273,7 +1285,7 @@
         down_done, up_done, query_done, key_done, value_done, output_done, vectors_done = jnp.split(
             total, ends, axis=1
         )
-        vectors_done = vectors_done.T
+        vectors_done = [*vectors_done.T[:3], vectors_done.T[3:].reshape(-1)]
     latent_query_done, latent_key_done, latent_value_done, latent_output_done = at["latent_grads"]
     return (
         at["result", groups - 1],
@@ -1289,10 +1301,10 @@
         value_done,
         output_done.T,
         up_done,
-        vectors_done[3 : 3 + hidden_units // model].reshape(-1),
+        vectors_done[3],
         down_done.T,
         vectors_done[0],
-        at["latent_gain_sum"][0],
+        at["latent_gain_sum"],
         vectors_done[2],
         vectors_done[1],
     )

time: 131 us -> 130 us (level)
  waiting for transfers between devices: 30.2 us -> 33.8 us
  starting transfers between devices: 44.5 us -> 42.7 us
  local copies, waits for them, and re-layouts: 1.63 us -> 0.01 us
    ppermute x32, waiting for transfers between devices: 24.8 us -> 28.1 us  [flip(): return lax.ppermute(values, 'dp', [(i, i ^ bits) for i in range(size)])]
    ppermute x32, starting transfers between devices: 26.7 us -> 24.9 us  [flip(): return lax.ppermute(values, 'dp', [(i, i ^ bits) for i in range(size)])]
  transfers between devices with their start and end apart: 44 -> 44, of which waited for: 18 -> 19; matrix products, arithmetic and copies ran while one was open for 0% -> 0% of each run, Pallas kernels for 40% -> 40%
where the time goes in v4:
time: 130 us
  Pallas kernels  52.6 us (40%)
  starting transfers between devices  42.7 us (33%)
  waiting for transfers between devices  33.8 us (26%)
    pallas_call x41, Pallas kernels, call(): pl.pallas_call(kernel, out_shape=[result(*out) for out in outs], in_specs...  46.5 us
    ppermute x32, waiting for transfers between devices, flip(): return lax.ppermute(values, 'dp', [(i, i ^ bits) for i in range(size)])  28.1 us
    ppermute x32, starting transfers between devices, flip(): return lax.ppermute(values, 'dp', [(i, i ^ bits) for i in range(size)])  24.9 us
    ppermute x12, starting transfers between devices, swap_tp(): return lax.ppermute(values, 'tp', [(0, 1), (1, 0)])  17.9 us
    pallas_call x3, Pallas kernels, load(): pl.pallas_call(load_kernel, out_shape=[pltpu.VMEM(a.shape, a.dtype) for a...  6.04 us
    ppermute x12, waiting for transfers between devices, swap_tp(): return lax.ppermute(values, 'tp', [(0, 1), (1, 0)])  5.66 us
  transfers between devices with their start and end apart: 44, of which 19 were waited for; matrix products, arithmetic and copies ran while one was open for 0% of the time, Pallas kernels for 40%

profile of v4, /device:TPU:0, one launch (start us, length us, event | category | flops | bytes accessed | tf_op | source)
XLA Modules:
  0.0 130.1 jit_solution(12878616511016978146)
XLA Ops:
  0.7 3.0 %collective-permute-start.7 = (bf16[384,768]{1,0:T(8,128)(2,1)}, bf16[384,768]{1,0:T(8,128)(2,1)S(1)}, u32[]{:S(2)}, u32[]{:S(2)}) collective-permute-start(bf16[384,768]{1,0:T(8,128)(2,1)} %refs_4_.3), channel_id=1, source_target_pairs={{0,16},{16,0},{1,17},{17,1},{2,18},{18,2},{3,19},{19,3},{4,20},{20... | collective-permute-start | bytes 1769480 | tf_op jit(solution)/shard_map/swap_output_weight/ppermute | solution.py:639
  5.2 2.6 %collective-permute-start.1 = (bf16[16,768]{1,0:T(8,128)(2,1)}, bf16[16,768]{1,0:T(8,128)(2,1)S(1)}, u32[]{:S(2)}, u32[]{:S(2)}) collective-permute-start(bf16[16,768]{1,0:T(8,128)(2,1)} %refs_0_), channel_id=1, source_target_pairs={{0,8},{1,9},{2,10},{3,11},{4,12},{5,13},{6,14},{7,15},{8,0},{9,1},... | collective-permute-start | bytes 73736 | tf_op jit(solution)/shard_map/flip_latents_held/ppermute | solution.py:645
  10.3 3.3 %collective-permute-done.2.refs_3_ = bf16[16,768]{1,0:T(8,128)(2,1)S(1)} collective-permute-done((bf16[16,768]{1,0:T(8,128)(2,1)}, bf16[16,768]{1,0:T(8,128)(2,1)S(1)}, u32[]{:S(2)}, u32[]{:S(2)}) %collective-permute-start.2) | collective-permute-done | bytes 24608 | tf_op jit(solution)/shard_map/flip_latents_held/ppermute | solution.py:645
  15.3 2.6 %load.4 = (bf16[512,768]{1,0:T(8,128)(2,1)S(1)}, bf16[768,384]{1,0:T(8,128)(2,1)S(1)}, bf16[768,384]{1,0:T(8,128)(2,1)S(1)}, bf16[768,384]{1,0:T(8,128)(2,1)S(1)...) custom-call(bf16[512,768]{1,0:T(8,128)(2,1)} %refs_0_.1, ...), custom_call_target="tpu_custom_call" | custom-call | tf_op jit(solution)/shard_map/load/pallas_call | solution.py:619
  20.5 2.1 %latent.1 = (bf16[256,768]{1,0:T(8,128)(2,1)S(1)}, bf16[256,384]{1,0:T(8,128)(2,1)S(1)}, bf16[256,384]{1,0:T(8,128)(2,1)S(1)}, bf16[256,384]{1,0:T(8,128)(2,1)S(1)}, bf16[16,768]{1,0:T(8,128)(2,1)S(1)}) custom-call(s32[1]{0:T(128)} %bitcast.1.me, s32[32]{0:T(128)S(1)} %copy-done, bf16[128,768]{1,0:T(8,128)(2,1)S(1)} %join.6.one, ...), custom_call_target="tpu_custom_call" | custom-call | tf_op jit(solution)/shard_map/latent/pallas_call | solution.py:595
  23.1 2.6 %load.5 = (bf16[768,1536]{1,0:T(8,128)(2,1)S(1)}, bf16[1536,768]{1,0:T(8,128)(2,1)S(1)}, bf16[512,768]{1,0:T(8,128)(2,1)S(1)}) custom-call(bf16[768,1536]{1,0:T(8,128)(2,1)} %refs_0_.2, bf16[1536,768]{1,0:T(8,128)(2,1)} %refs_1_.5, bf16[512,768]{1,0:T(8,128)(2,1)} %refs_2_.5), custom_call_target="tpu_custom_call" | custom-call | tf_op jit(solution)/shard_map/load/pallas_call | solution.py:619
  26.4 1.9 %attend.2 = (bf16[256,384]{1,0:T(8,128)(2,1)S(1)}, f32[56,256]{1,0:T(8,128)S(1)}, f32[8,1536]{1,0:T(8,128)S(1)}, f32[16,768]{1,0:T(8,128)S(1)}, bf16[16,768]{1,0:T(8,128)(2,1)}) custom-call(bf16[256,1920]{1,0:T(8,128)(2,1)S(1)} %enter.2.saved.refs_0_, bf16[16,768]{1,0:T(8,128)(2,1)S(1)} %get-tuple-element.209.refs_0_.latents, ...), custom_call_target="tpu_custom_call" | custom-call | tf_op jit(solution)/shard_map/attend/pallas_call | solution.py:595
  29.1 1.9 %attend.3 = (bf16[256,384]{1,0:T(8,128)(2,1)S(1)}, f32[56,256]{1,0:T(8,128)S(1)}, f32[8,1536]{1,0:T(8,128)S(1)}, f32[16,768]{1,0:T(8,128)}, bf16[16,768]{1,0:T(8,128)(2,1)}) custom-call(bf16[256,1920]{1,0:T(8,128)(2,1)S(1)} %enter.3.saved.refs_1_, bf16[16,768]{1,0:T(8,128)(2,1)S(1)} %get-tuple-element.209.refs_0_.latents, ...), custom_call_target="tpu_custom_call" | custom-call | tf_op jit(solution)/shard_map/attend/pallas_call | solution.py:595
  32.2 3.1 %collective-permute-done.6.o_two = bf16[256,384]{1,0:T(8,128)(2,1)S(1)} collective-permute-done((bf16[256,384]{1,0:T(8,128)(2,1)S(1)}, bf16[256,384]{1,0:T(8,128)(2,1)S(1)}, u32[]{:S(2)}, u32[]{:S(2)}) %collective-permute-start.6) | collective-permute-done | bytes 196640 | tf_op jit(solution)/shard_map/swap_o/ppermute | solution.py:639
  35.3 4.2 %feed.2 = (bf16[128,768]{1,0:T(8,128)(2,1)S(1)}, bf16[128,768]{1,0:T(8,128)(2,1)S(1)}, bf16[256,1536]{1,0:T(8,128)(2,1)S(1)}, bf16[256,1536]{1,0:T(8,128)(2,1)S(...) custom-call(s32[1]{0:T(128)} %bitcast.place, ...), custom_call_target="tpu_custom_call" | custom-call | tf_op jit(solution)/shard_map/feed/pallas_call | solution.py:595
  41.6 4.4 %feed.3 = (bf16[256,768]{1,0:T(8,128)(2,1)S(1)}, bf16[256,1536]{1,0:T(8,128)(2,1)S(1)}, bf16[256,1536]{1,0:T(8,128)(2,1)S(1)}, bf16[256,768]{1,0:T(8,128)(2,1)S(...) custom-call(s32[1]{0:T(128)} %bitcast.place, ...), custom_call_target="tpu_custom_call" | custom-call | tf_op jit(solution)/shard_map/feed/pallas_call | solution.py:595
  47.6 3.1 %weight_grad.1 = (bf16[8,48,384]{2,1,0:T(8,128)(2,1)S(1)}, bf16[8,48,384]{2,1,0:T(8,128)(2,1)S(1)}, bf16[8,48,384]{2,1,0:T(8,128)(2,1)S(1)}, bf16[8,48,384]{2,1,...) custom-call(s32[1]{0:T(128)} %bitcast.1.me, ...), custom_call_target="tpu_custom_call" | custom-call | tf_op jit(solution)/shard_map/weight_grad/pallas_call | solution.py:595
  50.7 1.8 %turn.2 = (bf16[256,384]{1,0:T(8,128)(2,1)S(1)}, f32[8,256]{1,0:T(8,128)S(1)}, bf16[48,256]{1,0:T(8,128)(2,1)S(1)}, f32[8,768]{1,0:T(8,128)S(1)}, f32[8,768]{1,0...) custom-call(bf16[512,768]{1,0:T(8,128)(2,1)S(1)} %get-tuple-element.226.cotangent, ...), custom_call_target="tpu_custom_call" | custom-call | tf_op jit(solution)/shard_map/turn/pallas_call | solution.py:595
  54.2 1.7 %collective-permute-start.17 = (bf16[256,768]{1,0:T(8,128)(2,1)S(1)}, bf16[256,768]{1,0:T(8,128)(2,1)S(1)}, u32[]{:S(2)}, u32[]{:S(2)}) collective-permute-start(bf16[256,768]{1,0:T(8,128)(2,1)S(1)} %get-tuple-element.288.part_one), channel_id=1, source_target_pairs={{0,16},{16,0},{1,17},{17,1},{2,18},{18,2},{3,19},{19,3},{4,20},{20... | collective-permute-start | bytes 1179656 | tf_op jit(solution)/shard_map/swap_down_part/ppermute | solution.py:639
  56.7 1.8 %turn.3 = (bf16[256,384]{1,0:T(8,128)(2,1)S(1)}, f32[8,256]{1,0:T(8,128)S(1)}, bf16[48,256]{1,0:T(8,128)(2,1)S(1)}, bf16[16,768]{1,0:T(8,128)(2,1)S(1)}, f32[8,7...) custom-call(bf16[512,768]{1,0:T(8,128)(2,1)S(1)} %get-tuple-element.226.cotangent, ...), custom_call_target="tpu_custom_call" | custom-call | tf_op jit(solution)/shard_map/turn/pallas_call | solution.py:595
  60.0 1.7 %collective-permute-start.16 = (bf16[16,768]{1,0:T(8,128)(2,1)S(1)}, bf16[16,768]{1,0:T(8,128)(2,1)S(1)}, u32[]{:S(2)}, u32[]{:S(2)}) collective-permute-start(bf16[16,768]{1,0:T(8,128)(2,1)S(1)} %get-tuple-element.285.part_one), channel_id=1, source_target_pairs={{0,16},{16,0},{1,17},{17,1},{2,18},{18,2},{3,19},{19,3},{4,20},{20... | collective-permute-start | bytes 73736 | tf_op jit(solution)/shard_map/swap_side_part/ppermute | solution.py:639
  61.8 2.6 %attend_back.2 = (bf16[256,768]{1,0:T(8,128)(2,1)S(1)}, bf16[256,1152]{1,0:T(8,128)(2,1)S(1)}, f32[1,768]{1,0:T(1,128)S(1)}) custom-call(bf16[512,768]{1,0:T(8,128)(2,1)S(1)} %get-tuple-element.211.tokens, bf16[256,1920]{1,0:T(8,128)(2,1)S(1)} %enter.2.saved.refs_0_, bf16[256,384]{1,0:T(8,128)(2,1)S(1)} %get-tuple-element.280.o_grad, ...), custom_call_target="tpu_custom_call" | custom-call | tf_op jit(solution)/shard_map/attend_back/pallas_call | solution.py:595
  66.3 2.8 %attend_back.3 = (bf16[512,768]{1,0:T(8,128)(2,1)S(1)}, bf16[256,1152]{1,0:T(8,128)(2,1)S(1)}, f32[1,768]{1,0:T(1,128)S(1)}) custom-call(bf16[512,768]{1,0:T(8,128)(2,1)S(1)} %get-tuple-element.211.tokens, bf16[256,1920]{1,0:T(8,128)(2,1)S(1)} %enter.3.saved.refs_1_, bf16[256,384]{1,0:T(8,128)(2,1)S(1)} %get-tuple-element.276.o_grad, ...), custom_call_target="tpu_custom_call" | custom-call | tf_op jit(solution)/shard_map/attend_back/pallas_call | solution.py:595
  70.1 1.8 %collective-permute-start.18 = (f32[1,768]{1,0:T(1,128)S(1)}, f32[1,768]{1,0:T(1,128)S(1)}, u32[]{:S(2)}, u32[]{:S(2)}) collective-permute-start(f32[1,768]{1,0:T(1,128)S(1)} %get-tuple-element.295.one), channel_id=1, source_target_pairs={{0,16},{16,0},{1,17},{17,1},{2,18},{18,2},{3,19},{19,3},{4,20},{20... | collective-permute-start | bytes 9224 | tf_op jit(solution)/shard_map/swap_gain/ppermute | solution.py:639
  71.9 2.1 %attention_grad.1 = (bf16[8,48,384]{2,1,0:T(8,128)(2,1)S(1)}, bf16[8,48,384]{2,1,0:T(8,128)(2,1)S(1)}, bf16[8,48,384]{2,1,0:T(8,128)(2,1)S(1)}, bf16[8,48,384]{2...) custom-call(s32[1]{0:T(128)} %bitcast.1.me, ...), custom_call_target="tpu_custom_call" | custom-call | tf_op jit(solution)/shard_map/attention_grad/pallas_call | solution.py:595
  76.7 3.0 %collective-permute-done.22.refs_1_ = bf16[64,768]{1,0:T(8,128)(2,1)S(1)} collective-permute-done((bf16[64,768]{1,0:T(8,128)(2,1)S(1)}, bf16[64,768]{1,0:T(8,128)(2,1)S(1)}, u32[]{:S(2)}, u32[]{:S(2)}) %collective-permute-start.22) | collective-permute-done | bytes 98336 | tf_op jit(solution)/shard_map/flip_mid_held/ppermute | solution.py:645
  83.9 5.9 %latent_back.1 = (bf16[544,768]{1,0:T(8,128)(2,1)S(1)}, f32[48,384]{1,0:T(8,128)}, f32[48,384]{1,0:T(8,128)}, f32[48,384]{1,0:T(8,128)}, f32[48,384]{1,0:T(8,128)}) custom-call(s32[1]{0:T(128)} %bitcast.1.me, s32[32]{0:T(128)S(1)} %copy-done, bf16[512,768]{1,0:T(8,128)(2,1)S(1)} %get-tuple-element.336.token_part, ...), custom_call_target="tpu_custom_call" | custom-call | tf_op jit(solution)/shard_map/latent_back/pallas_call | solution.py:595
  92.7 4.2 %collective-permute-done.33 = bf16[4,48,1536]{2,1,0:T(8,128)(2,1)S(1)} collective-permute-done((bf16[4,48,1536]{2,1,0:T(8,128)(2,1)S(1)}, bf16[4,48,1536]{2,1,0:T(8,128)(2,1)S(1)}, u32[]{:S(2)}, u32[]{:S(2)}) %collective-permute-start.33) | collective-permute-done | bytes 589856 | tf_op jit(solution)/shard_map/flip_up_y/ppermute | solution.py:645
  99.1 1.8 %collective-permute-start.36 = (bf16[1,48,1536]{2,1,0:T(8,128)(2,1)S(1)}, bf16[1,48,1536]{2,1,0:T(8,128)(2,1)S(1)}, u32[]{:S(2)}, u32[]{:S(2)}) collective-permute-start(bf16[1,48,1536]{2,1,0:T(8,128)(2,1)S(1)} %get-tuple-element.344), channel_id=1, source_target_pairs={{0,8},{1,9},{2,10},{3,11},{4,12},{5,13},{6,14},{7,15},{8,0},{9,1},... | collective-permute-start | bytes 442376 | tf_op jit(solution)/shard_map/flip_down_zz/ppermute | solution.py:645
  100.8 2.4 %collective-permute-done.34 = bf16[4,48,768]{2,1,0:T(8,128)(2,1)S(1)} collective-permute-done((bf16[4,48,768]{2,1,0:T(8,128)(2,1)S(1)}, bf16[4,48,768]{2,1,0:T(8,128)(2,1)S(1)}, u32[]{:S(2)}, u32[]{:S(2)}) %collective-permute-start.34) | collective-permute-done | bytes 294944 | tf_op jit(solution)/shard_map/flip_first_y/ppermute | solution.py:645
  103.2 1.7 %collective-permute-start.19 = (bf16[256,768]{1,0:T(8,128)(2,1)S(1)}, bf16[256,768]{1,0:T(8,128)(2,1)S(1)}, u32[]{:S(2)}, u32[]{:S(2)}) collective-permute-start(bf16[256,768]{1,0:T(8,128)(2,1)S(1)} %get-tuple-element.296.part_one), channel_id=1, source_target_pairs={{0,16},{16,0},{1,17},{17,1},{2,18},{18,2},{3,19},{19,3},{4,20},{20... | collective-permute-start | bytes 1179656 | tf_op jit(solution)/shard_map/swap_down_part/ppermute | solution.py:639
  105.0 2.7 %collective-permute-done.35 = bf16[2,48,1536]{2,1,0:T(8,128)(2,1)S(1)} collective-permute-done((bf16[2,48,1536]{2,1,0:T(8,128)(2,1)S(1)}, bf16[2,48,1536]{2,1,0:T(8,128)(2,1)S(1)}, u32[]{:S(2)}, u32[]{:S(2)}) %collective-permute-start.35) | collective-permute-done | bytes 294944 | tf_op jit(solution)/shard_map/flip_up_z/ppermute | solution.py:645
  108.6 2.7 %collective-permute-start.38 = (bf16[2,48,768]{2,1,0:T(8,128)(2,1)S(1)}, bf16[2,48,768]{2,1,0:T(8,128)(2,1)S(1)}, u32[]{:S(2)}, u32[]{:S(2)}) collective-permute-start(bf16[2,48,768]{2,1,0:T(8,128)(2,1)S(1)} %get-tuple-element.351), channel_id=1, source_target_pairs={{0,4},{1,5},{2,6},{3,7},{4,0},{5,1},{6,2},{7,3},{8,12},{9,13},{10,... | collective-permute-start | bytes 442376 | tf_op jit(solution)/shard_map/flip_first_z/ppermute | solution.py:645
  112.0 3.5 %collective-permute-done.37.got = bf16[1,48,1536]{2,1,0:T(8,128)(2,1)S(1)} collective-permute-done((bf16[1,48,1536]{2,1,0:T(8,128)(2,1)S(1)}, bf16[1,48,1536]{2,1,0:T(8,128)(2,1)S(1)}, u32[]{:S(2)}, u32[]{:S(2)}) %collective-permute-start.37) | collective-permute-done | bytes 147488 | tf_op jit(solution)/shard_map/flip_up_zz/ppermute | solution.py:645
  118.7 2.3 %leave.1 = f32[512,768]{1,0:T(8,128)} custom-call(bf16[512,768]{1,0:T(8,128)(2,1)S(1)} %get-tuple-element.211.tokens, f32[768]{0:T(1024)S(1)} %get-tuple-element.365.gain, bf16[544,768]{1,0:T(8,128)(2,1)S(1)} %get-tuple-element.366.part_one, bf16[544,768]{1,0:T(8,128)(2,1)S(1)} %collective-permute-done.40.part_two, ...), custom_call_target="tpu_custom_call" | custom-call | tf_op jit(solution)/shard_map/leave/pallas_call | solution.py:595
  123.8 1.9 %collective-permute-start.43 = (bf16[1,48,896]{2,1,0:T(8,128)(2,1)S(1)}, bf16[1,48,896]{2,1,0:T(8,128)(2,1)S(1)}, u32[]{:S(2)}, u32[]{:S(2)}) collective-permute-start(bf16[1,48,896]{2,1,0:T(8,128)(2,1)S(1)} %get-tuple-element.385), channel_id=1, source_target_pairs={{0,8},{1,9},{2,10},{3,11},{4,12},{5,13},{6,14},{7,15},{8,0},{9,1},... | collective-permute-start | bytes 258056 | tf_op jit(solution)/shard_map/flip_second_zz/ppermute | solution.py:645
  125.7 3.5 %collective-permute-done.43.got = bf16[1,48,896]{2,1,0:T(8,128)(2,1)S(1)} collective-permute-done((bf16[1,48,896]{2,1,0:T(8,128)(2,1)S(1)}, bf16[1,48,896]{2,1,0:T(8,128)(2,1)S(1)}, u32[]{:S(2)}, u32[]{:S(2)}) %collective-permute-start.43) | collective-permute-done | bytes 86048 | tf_op jit(solution)/shard_map/flip_second_zz/ppermute | solution.py:645
  (102 shorter events, 42.2 us)
Async XLA Ops:
  0.7 34.7 %collective-permute-start.7 = (bf16[384,768]{1,0:T(8,128)(2,1)}, bf16[384,768]{1,0:T(8,128)(2,1)S(1)}, u32[]{:S(2)}, u32[]{:S(2)}) collective-permute-start(bf16[384,768]{1,0:T(8,128)(2,1)} %refs_4_.3), channel_id=1, source_target_pairs={{0,16},{16,0},{1,17},{17,1},{2,18},{18,2},{3,19},{19,3},{4,20},{20... | collective-permute-start | bytes 1769480 | tf_op jit(solution)/shard_map/swap_output_weight/ppermute | solution.py:639
  3.7 5.2 %collective-permute-start = (bf16[16,768]{1,0:T(8,128)(2,1)}, bf16[16,768]{1,0:T(8,128)(2,1)S(1)}, u32[]{:S(2)}, u32[]{:S(2)}) collective-permute-start(bf16[16,768]{1,0:T(8,128)(2,1)} %refs_0_), channel_id=1, source_target_pairs={{0,4},{1,5},{2,6},{3,7},{4,0},{5,1},{6,2},{7,3},{8,12},{9,13},{10,... | collective-permute-start | bytes 73736 | tf_op jit(solution)/shard_map/flip_latents_held/ppermute | solution.py:645
  5.2 5.1 %collective-permute-start.1 = (bf16[16,768]{1,0:T(8,128)(2,1)}, bf16[16,768]{1,0:T(8,128)(2,1)S(1)}, u32[]{:S(2)}, u32[]{:S(2)}) collective-permute-start(bf16[16,768]{1,0:T(8,128)(2,1)} %refs_0_), channel_id=1, source_target_pairs={{0,8},{1,9},{2,10},{3,11},{4,12},{5,13},{6,14},{7,15},{8,0},{9,1},... | collective-permute-start | bytes 73736 | tf_op jit(solution)/shard_map/flip_latents_held/ppermute | solution.py:645
  7.8 5.8 %collective-permute-start.2 = (bf16[16,768]{1,0:T(8,128)(2,1)}, bf16[16,768]{1,0:T(8,128)(2,1)S(1)}, u32[]{:S(2)}, u32[]{:S(2)}) collective-permute-start(bf16[16,768]{1,0:T(8,128)(2,1)} %refs_0_), channel_id=1, source_target_pairs={{0,12},{1,13},{2,14},{3,15},{4,8},{5,9},{6,10},{7,11},{8,4},{9,5},... | collective-permute-start | bytes 73736 | tf_op jit(solution)/shard_map/flip_latents_held/ppermute | solution.py:645
  13.7 5.3 %collective-permute-start.3 = (bf16[64,768]{1,0:T(8,128)(2,1)S(1)}, bf16[64,768]{1,0:T(8,128)(2,1)S(1)}, u32[]{:S(2)}, u32[]{:S(2)}) collective-permute-start(bf16[64,768]{1,0:T(8,128)(2,1)S(1)} %join.5.refs_0_), channel_id=1, source_target_pairs={{0,2},{1,3},{2,0},{3,1},{4,6},{5,7},{6,4},{7,5},{8,10},{9,11},{10,... | collective-permute-start | bytes 294920 | tf_op jit(solution)/shard_map/flip_latents_held/ppermute | solution.py:645
  28.3 7.0 %collective-permute-start.6 = (bf16[256,384]{1,0:T(8,128)(2,1)S(1)}, bf16[256,384]{1,0:T(8,128)(2,1)S(1)}, u32[]{:S(2)}, u32[]{:S(2)}) collective-permute-start(bf16[256,384]{1,0:T(8,128)(2,1)S(1)} %get-tuple-element.232.o.refs_6_), channel_id=1, source_target_pairs={{0,16},{16,0},{1,17},{17,1},{2,18},{18,2},{3,19},{19,3},{4,20},{20... | collective-permute-start | bytes 589832 | tf_op jit(solution)/shard_map/swap_o/ppermute | solution.py:639
  31.0 10.6 %collective-permute-start.8 = (bf16[256,384]{1,0:T(8,128)(2,1)S(1)}, bf16[256,384]{1,0:T(8,128)(2,1)S(1)}, u32[]{:S(2)}, u32[]{:S(2)}) collective-permute-start(bf16[256,384]{1,0:T(8,128)(2,1)S(1)} %get-tuple-element.240.o.refs_7_), channel_id=1, source_target_pairs={{0,16},{16,0},{1,17},{17,1},{2,18},{18,2},{3,19},{19,3},{4,20},{20... | collective-permute-start | bytes 589832 | tf_op jit(solution)/shard_map/swap_o/ppermute | solution.py:639
  39.5 11.2 %collective-permute-start.10 = (bf16[128,768]{1,0:T(8,128)(2,1)S(1)}, bf16[128,768]{1,0:T(8,128)(2,1)S(1)}, u32[]{:S(2)}, u32[]{:S(2)}) collective-permute-start(bf16[128,768]{1,0:T(8,128)(2,1)S(1)} %get-tuple-element.257.rest_1_), channel_id=1, source_target_pairs={{0,16},{16,0},{1,17},{17,1},{2,18},{18,2},{3,19},{19,3},{4,20},{20... | collective-permute-start | bytes 589832 | tf_op jit(solution)/shard_map/swap_feed_part/ppermute | solution.py:639
  41.1 9.6 %collective-permute-start.9 = (bf16[128,768]{1,0:T(8,128)(2,1)S(1)}, bf16[128,768]{1,0:T(8,128)(2,1)S(1)}, u32[]{:S(2)}, u32[]{:S(2)}) collective-permute-start(bf16[128,768]{1,0:T(8,128)(2,1)S(1)} %get-tuple-element.256.rest_0_), channel_id=1, source_target_pairs={{0,16},{16,0},{1,17},{17,1},{2,18},{18,2},{3,19},{19,3},{4,20},{20... | collective-permute-start | bytes 589832 | tf_op jit(solution)/shard_map/swap_feed_part/ppermute | solution.py:639
  46.0 10.7 %collective-permute-start.15 = (bf16[256,768]{1,0:T(8,128)(2,1)S(1)}, bf16[256,768]{1,0:T(8,128)(2,1)S(1)}, u32[]{:S(2)}, u32[]{:S(2)}) collective-permute-start(bf16[256,768]{1,0:T(8,128)(2,1)S(1)} %get-tuple-element.274.rest_0_), channel_id=1, source_target_pairs={{0,16},{16,0},{1,17},{17,1},{2,18},{18,2},{3,19},{19,3},{4,20},{20... | collective-permute-start | bytes 1179656 | tf_op jit(solution)/shard_map/swap_feed_part/ppermute | solution.py:639
  54.2 11.4 %collective-permute-start.17 = (bf16[256,768]{1,0:T(8,128)(2,1)S(1)}, bf16[256,768]{1,0:T(8,128)(2,1)S(1)}, u32[]{:S(2)}, u32[]{:S(2)}) collective-permute-start(bf16[256,768]{1,0:T(8,128)(2,1)S(1)} %get-tuple-element.288.part_one), channel_id=1, source_target_pairs={{0,16},{16,0},{1,17},{17,1},{2,18},{18,2},{3,19},{19,3},{4,20},{20... | collective-permute-start | bytes 1179656 | tf_op jit(solution)/shard_map/swap_down_part/ppermute | solution.py:639
  58.6 21.2 %collective-permute-start.24 = (bf16[8,48,768]{2,1,0:T(8,128)(2,1)S(1)}, bf16[8,48,768]{2,1,0:T(8,128)(2,1)S(1)}, u32[]{:S(2)}, u32[]{:S(2)}) collective-permute-start(bf16[8,48,768]{2,1,0:T(8,128)(2,1)S(1)} %get-tuple-element.318), channel_id=1, source_target_pairs={{0,1},{1,0},{2,3},{3,2},{4,5},{5,4},{6,7},{7,6},{8,9},{9,8},{10,11... | collective-permute-start | bytes 1769480 | tf_op jit(solution)/shard_map/flip_up_core/ppermute | solution.py:645
  58.6 21.7 %collective-permute-start.23 = (bf16[8,48,768]{2,1,0:T(8,128)(2,1)S(1)}, bf16[8,48,768]{2,1,0:T(8,128)(2,1)S(1)}, u32[]{:S(2)}, u32[]{:S(2)}) collective-permute-start(bf16[8,48,768]{2,1,0:T(8,128)(2,1)S(1)} %get-tuple-element.316), channel_id=1, source_target_pairs={{0,1},{1,0},{2,3},{3,2},{4,5},{5,4},{6,7},{7,6},{8,9},{9,8},{10,11... | collective-permute-start | bytes 1769480 | tf_op jit(solution)/shard_map/flip_up_core/ppermute | solution.py:645
  59.1 21.5 %collective-permute-start.25 = (bf16[4,48,1536]{2,1,0:T(8,128)(2,1)S(1)}, bf16[4,48,1536]{2,1,0:T(8,128)(2,1)S(1)}, u32[]{:S(2)}, u32[]{:S(2)}) collective-permute-start(bf16[4,48,1536]{2,1,0:T(8,128)(2,1)S(1)} %get-tuple-element.271), channel_id=1, source_target_pairs={{0,2},{1,3},{2,0},{3,1},{4,6},{5,7},{6,4},{7,5},{8,10},{9,11},{10,... | collective-permute-start | bytes 1769480 | tf_op jit(solution)/shard_map/flip_down_y/ppermute | solution.py:645
  60.0 5.9 %collective-permute-start.16 = (bf16[16,768]{1,0:T(8,128)(2,1)S(1)}, bf16[16,768]{1,0:T(8,128)(2,1)S(1)}, u32[]{:S(2)}, u32[]{:S(2)}) collective-permute-start(bf16[16,768]{1,0:T(8,128)(2,1)S(1)} %get-tuple-element.285.part_one), channel_id=1, source_target_pairs={{0,16},{16,0},{1,17},{17,1},{2,18},{18,2},{3,19},{19,3},{4,20},{20... | collective-permute-start | bytes 73736 | tf_op jit(solution)/shard_map/swap_side_part/ppermute | solution.py:639
  70.1 5.0 %collective-permute-start.21 = (bf16[32,768]{1,0:T(8,128)(2,1)S(1)}, bf16[32,768]{1,0:T(8,128)(2,1)S(1)}, u32[]{:S(2)}, u32[]{:S(2)}) collective-permute-start(bf16[32,768]{1,0:T(8,128)(2,1)S(1)} %join.7.refs_0_), channel_id=1, source_target_pairs={{0,8},{1,9},{2,10},{3,11},{4,12},{5,13},{6,14},{7,15},{8,0},{9,1},... | collective-permute-start | bytes 147464 | tf_op jit(solution)/shard_map/flip_mid_held/ppermute | solution.py:645
  70.1 6.0 %collective-permute-start.18 = (f32[1,768]{1,0:T(1,128)S(1)}, f32[1,768]{1,0:T(1,128)S(1)}, u32[]{:S(2)}, u32[]{:S(2)}) collective-permute-start(f32[1,768]{1,0:T(1,128)S(1)} %get-tuple-element.295.one), channel_id=1, source_target_pairs={{0,16},{16,0},{1,17},{17,1},{2,18},{18,2},{3,19},{19,3},{4,20},{20... | collective-permute-start | bytes 9224 | tf_op jit(solution)/shard_map/swap_gain/ppermute | solution.py:639
  75.1 4.7 %collective-permute-start.22 = (bf16[64,768]{1,0:T(8,128)(2,1)S(1)}, bf16[64,768]{1,0:T(8,128)(2,1)S(1)}, u32[]{:S(2)}, u32[]{:S(2)}) collective-permute-start(bf16[64,768]{1,0:T(8,128)(2,1)S(1)} %join.8.refs_0_), channel_id=1, source_target_pairs={{0,2},{1,3},{2,0},{3,1},{4,6},{5,7},{6,4},{7,5},{8,10},{9,11},{10,... | collective-permute-start | bytes 294920 | tf_op jit(solution)/shard_map/flip_mid_held/ppermute | solution.py:645
  76.1 6.1 %collective-permute-start.26 = (bf16[8,48,384]{2,1,0:T(8,128)(2,1)S(1)}, bf16[8,48,384]{2,1,0:T(8,128)(2,1)S(1)}, u32[]{:S(2)}, u32[]{:S(2)}) collective-permute-start(bf16[8,48,384]{2,1,0:T(8,128)(2,1)S(1)} %get-tuple-element.305), channel_id=1, source_target_pairs={{0,1},{1,0},{2,3},{3,2},{4,5},{5,4},{6,7},{7,6},{8,9},{9,8},{10,11... | collective-permute-start | bytes 884744 | tf_op jit(solution)/shard_map/flip_first_core/ppermute | solution.py:645
  80.6 16.3 %collective-permute-start.33 = (bf16[4,48,1536]{2,1,0:T(8,128)(2,1)S(1)}, bf16[4,48,1536]{2,1,0:T(8,128)(2,1)S(1)}, u32[]{:S(2)}, u32[]{:S(2)}) collective-permute-start(bf16[4,48,1536]{2,1,0:T(8,128)(2,1)S(1)} %get-tuple-element.347), channel_id=1, source_target_pairs={{0,2},{1,3},{2,0},{3,1},{4,6},{5,7},{6,4},{7,5},{8,10},{9,11},{10,... | collective-permute-start | bytes 1769480 | tf_op jit(solution)/shard_map/flip_up_y/ppermute | solution.py:645
  82.3 10.3 %collective-permute-start.32 = (bf16[2,48,1536]{2,1,0:T(8,128)(2,1)S(1)}, bf16[2,48,1536]{2,1,0:T(8,128)(2,1)S(1)}, u32[]{:S(2)}, u32[]{:S(2)}) collective-permute-start(bf16[2,48,1536]{2,1,0:T(8,128)(2,1)S(1)} %get-tuple-element.322), channel_id=1, source_target_pairs={{0,4},{1,5},{2,6},{3,7},{4,0},{5,1},{6,2},{7,3},{8,12},{9,13},{10,... | collective-permute-start | bytes 884744 | tf_op jit(solution)/shard_map/flip_down_z/ppermute | solution.py:645
  89.8 28.9 %collective-permute-start.40 = (bf16[544,768]{1,0:T(8,128)(2,1)S(1)}, bf16[544,768]{1,0:T(8,128)(2,1)S(1)}, u32[]{:S(2)}, u32[]{:S(2)}) collective-permute-start(bf16[544,768]{1,0:T(8,128)(2,1)S(1)} %get-tuple-element.366.part_one), channel_id=1, source_target_pairs={{0,16},{16,0},{1,17},{17,1},{2,18},{18,2},{3,19},{19,3},{4,20},{20... | collective-permute-start | bytes 2506760 | tf_op jit(solution)/shard_map/swap_all_part/ppermute | solution.py:639
  91.5 11.7 %collective-permute-start.34 = (bf16[4,48,768]{2,1,0:T(8,128)(2,1)S(1)}, bf16[4,48,768]{2,1,0:T(8,128)(2,1)S(1)}, u32[]{:S(2)}, u32[]{:S(2)}) collective-permute-start(bf16[4,48,768]{2,1,0:T(8,128)(2,1)S(1)} %get-tuple-element.327), channel_id=1, source_target_pairs={{0,2},{1,3},{2,0},{3,1},{4,6},{5,7},{6,4},{7,5},{8,10},{9,11},{10,... | collective-permute-start | bytes 884744 | tf_op jit(solution)/shard_map/flip_first_y/ppermute | solution.py:645
  97.0 10.7 %collective-permute-start.35 = (bf16[2,48,1536]{2,1,0:T(8,128)(2,1)S(1)}, bf16[2,48,1536]{2,1,0:T(8,128)(2,1)S(1)}, u32[]{:S(2)}, u32[]{:S(2)}) collective-permute-start(bf16[2,48,1536]{2,1,0:T(8,128)(2,1)S(1)} %get-tuple-element.348), channel_id=1, source_target_pairs={{0,4},{1,5},{2,6},{3,7},{4,0},{5,1},{6,2},{7,3},{8,12},{9,13},{10,... | collective-permute-start | bytes 884744 | tf_op jit(solution)/shard_map/flip_up_z/ppermute | solution.py:645
  98.1 19.0 %collective-permute-start.39 = (bf16[4,48,896]{2,1,0:T(8,128)(2,1)S(1)}, bf16[4,48,896]{2,1,0:T(8,128)(2,1)S(1)}, u32[]{:S(2)}, u32[]{:S(2)}) collective-permute-start(bf16[4,48,896]{2,1,0:T(8,128)(2,1)S(1)} %get-tuple-element.334), channel_id=1, source_target_pairs={{0,2},{1,3},{2,0},{3,1},{4,6},{5,7},{6,4},{7,5},{8,10},{9,11},{10,... | collective-permute-start | bytes 1032200 | tf_op jit(solution)/shard_map/flip_second_y/ppermute | solution.py:645
  99.1 9.5 %collective-permute-start.36 = (bf16[1,48,1536]{2,1,0:T(8,128)(2,1)S(1)}, bf16[1,48,1536]{2,1,0:T(8,128)(2,1)S(1)}, u32[]{:S(2)}, u32[]{:S(2)}) collective-permute-start(bf16[1,48,1536]{2,1,0:T(8,128)(2,1)S(1)} %get-tuple-element.344), channel_id=1, source_target_pairs={{0,8},{1,9},{2,10},{3,11},{4,12},{5,13},{6,14},{7,15},{8,0},{9,1},... | collective-permute-start | bytes 442376 | tf_op jit(solution)/shard_map/flip_down_zz/ppermute | solution.py:645
  103.2 17.9 %collective-permute-start.19 = (bf16[256,768]{1,0:T(8,128)(2,1)S(1)}, bf16[256,768]{1,0:T(8,128)(2,1)S(1)}, u32[]{:S(2)}, u32[]{:S(2)}) collective-permute-start(bf16[256,768]{1,0:T(8,128)(2,1)S(1)} %get-tuple-element.296.part_one), channel_id=1, source_target_pairs={{0,16},{16,0},{1,17},{17,1},{2,18},{18,2},{3,19},{19,3},{4,20},{20... | collective-permute-start | bytes 1179656 | tf_op jit(solution)/shard_map/swap_down_part/ppermute | solution.py:639
  107.7 7.8 %collective-permute-start.37 = (bf16[1,48,1536]{2,1,0:T(8,128)(2,1)S(1)}, bf16[1,48,1536]{2,1,0:T(8,128)(2,1)S(1)}, u32[]{:S(2)}, u32[]{:S(2)}) collective-permute-start(bf16[1,48,1536]{2,1,0:T(8,128)(2,1)S(1)} %get-tuple-element.356), channel_id=1, source_target_pairs={{0,8},{1,9},{2,10},{3,11},{4,12},{5,13},{6,14},{7,15},{8,0},{9,1},... | collective-permute-start | bytes 442376 | tf_op jit(solution)/shard_map/flip_up_zz/ppermute | solution.py:645
  108.6 8.5 %collective-permute-start.38 = (bf16[2,48,768]{2,1,0:T(8,128)(2,1)S(1)}, bf16[2,48,768]{2,1,0:T(8,128)(2,1)S(1)}, u32[]{:S(2)}, u32[]{:S(2)}) collective-permute-start(bf16[2,48,768]{2,1,0:T(8,128)(2,1)S(1)} %get-tuple-element.351), channel_id=1, source_target_pairs={{0,4},{1,5},{2,6},{3,7},{4,0},{5,1},{6,2},{7,3},{8,12},{9,13},{10,... | collective-permute-start | bytes 442376 | tf_op jit(solution)/shard_map/flip_first_z/ppermute | solution.py:645
  117.2 6.5 %collective-permute-start.42 = (bf16[2,48,896]{2,1,0:T(8,128)(2,1)S(1)}, bf16[2,48,896]{2,1,0:T(8,128)(2,1)S(1)}, u32[]{:S(2)}, u32[]{:S(2)}) collective-permute-start(bf16[2,48,896]{2,1,0:T(8,128)(2,1)S(1)} %get-tuple-element.364), channel_id=1, source_target_pairs={{0,4},{1,5},{2,6},{3,7},{4,0},{5,1},{6,2},{7,3},{8,12},{9,13},{10,... | collective-permute-start | bytes 516104 | tf_op jit(solution)/shard_map/flip_second_z/ppermute | solution.py:645
  117.7 5.4 %collective-permute-start.41 = (bf16[1,48,768]{2,1,0:T(8,128)(2,1)S(1)}, bf16[1,48,768]{2,1,0:T(8,128)(2,1)S(1)}, u32[]{:S(2)}, u32[]{:S(2)}) collective-permute-start(bf16[1,48,768]{2,1,0:T(8,128)(2,1)S(1)} %get-tuple-element.361), channel_id=1, source_target_pairs={{0,8},{1,9},{2,10},{3,11},{4,12},{5,13},{6,14},{7,15},{8,0},{9,1},... | collective-permute-start | bytes 221192 | tf_op jit(solution)/shard_map/flip_first_zz/ppermute | solution.py:645
  123.8 5.4 %collective-permute-start.43 = (bf16[1,48,896]{2,1,0:T(8,128)(2,1)S(1)}, bf16[1,48,896]{2,1,0:T(8,128)(2,1)S(1)}, u32[]{:S(2)}, u32[]{:S(2)}) collective-permute-start(bf16[1,48,896]{2,1,0:T(8,128)(2,1)S(1)} %get-tuple-element.385), channel_id=1, source_target_pairs={{0,8},{1,9},{2,10},{3,11},{4,12},{5,13},{6,14},{7,15},{8,0},{9,1},... | collective-permute-start | bytes 258056 | tf_op jit(solution)/shard_map/flip_second_zz/ppermute | solution.py:645
  (13 other events, 31.3 us)
